TPU v7x, 512 devices: a whole 4x4x16 slice. The times are simulated.
512 devices in a mesh: seq: 64 (over x, z_hi, y, core), head: 8 (over z_lo).
Axes of the slice: x: 4, y: 4, z: 16 (z_hi: 2, z_lo: 8; z = z_hi * 8 + z_lo), core: 2. Of those that a mesh axis runs over, the one named last changes fastest.
Arguments:
- queries: bfloat16 [64, 256, 16384], P('head', 'seq'), may hold values from -6 to 6
- keys: bfloat16 [64, 256, 1024], P('head', 'seq'), may hold values from -6 to 6
- values: bfloat16 [64, 256, 1024], P('head', 'seq'), may hold values from -6 to 6
- links: int32 [64, 6], replicated, may hold values from 0 to 63, as said below
Outputs:
- attended: bfloat16 [64, 256, 16384], P('head', 'seq')
Inputs may be any that keep to these rules, and one draw needn't show every extreme that they name: For i >= 1, links[i, 0] = i - 1; every entry in slot k of row i is either i - 2 ** k or i; in the last row every slot k < 5 with 2 ** k < 64 holds 64 - 1 - 2 ** k, and slot 5 holds 63.
All inputs are finite; a program needn't handle non-finite values.
Results may differ from a plain program's by a relative error of at most 0.0095.
Values may be sent and summed in bfloat16 or wider, within the bound.
No kernel may reach another device: no remote copies, remote signals or barrier semaphores. Data moves between devices by JAX's collectives and lax.ppermute only.
A program may use at most 128 MiB of HBM per device.

v0:
```python
import jax
import jax.numpy as jnp
from jax import lax
from jax.sharding import PartitionSpec as P

HD = 128


def absorb_block(state, query_block, key_block, value_block, allowed):
    peak, total, summed = state
    scores = jnp.einsum(
        "qgrd,kgd->grqk", query_block, key_block, preferred_element_type=jnp.float32
    ) * HD ** (-0.5)
    scores = jnp.where(allowed[None, None], scores, -1e30)
    new_peak = jnp.maximum(peak, jnp.max(scores, axis=-1))
    factor = jnp.exp(peak - new_peak)
    weights = jnp.where(allowed[None, None], jnp.exp(scores - new_peak[..., None]), 0.0)
    total = total * factor + jnp.sum(weights, axis=-1)
    rounded = weights.astype(jnp.bfloat16)
    summed = summed * factor[..., None] + jnp.einsum(
        "grqk,kgd->grqd", rounded, value_block, preferred_element_type=jnp.float32
    )
    return (new_peak, total, summed)


def allowed_for(member_resp, member_start, member_rows, member_links, key_resp, key_pos):
    query_pos = member_start + jnp.arange(member_rows, dtype=jnp.int32)
    own = (key_resp == member_resp)[None, :] & (key_pos[None, :] <= query_pos[:, None])
    cross = jnp.any(member_links[:, None] == key_resp[None, :], axis=0) & (key_resp < member_resp)
    return own | cross[None, :]


def local(queries, keys, values, links):
    seq_index = lax.axis_index("seq")
    moved_q, moved_k, moved_v = (
        lax.all_to_all(queries, "head", split_axis=2, concat_axis=0, tiled=True),
        lax.all_to_all(keys, "head", split_axis=2, concat_axis=0, tiled=True),
        lax.all_to_all(values, "head", split_axis=2, concat_axis=0, tiled=True),
    )
    kv_width = moved_k.shape[2]
    pairs = jnp.concatenate([moved_k, moved_v], axis=2)
    query_rows, kv_rows = (
        lax.all_to_all(moved_q, "seq", split_axis=0, concat_axis=1, tiled=True),
        lax.all_to_all(pairs, "seq", split_axis=0, concat_axis=1, tiled=True),
    )
    resp_len = query_rows.shape[1]
    query_width = query_rows.shape[2]
    groups = kv_width // HD
    repeat = query_width // kv_width
    members = [(seq_index, 0, resp_len)]
    query_blocks = [
        query_rows[0, start : start + count].reshape(count, groups, repeat, HD)
        for owner, start, count in members
    ]
    member_links = [links[owner] for owner, start, count in members]
    start_state = tuple(
        (
            (
                jnp.full((groups, repeat, count), -1e30, jnp.float32),
                jnp.zeros((groups, repeat, count), jnp.float32),
                jnp.zeros((groups, repeat, count, HD), jnp.float32),
            )
            for owner, start, count in members
        )
    )
    own_pairs = kv_rows[0, :, : 2 * kv_width]

    def split_pair(block):
        width = block.shape[0]
        return (
            block[:, :kv_width].reshape(width, groups, HD),
            block[:, kv_width : 2 * kv_width].reshape(width, groups, HD),
        )

    def take_block(state, member, block, key_resp, key_pos):
        owner, start, count = members[member]
        key_block, value_block = split_pair(block)
        allowed = allowed_for(owner, start, count, member_links[member], key_resp, key_pos)
        query_block = query_blocks[member]
        return lax.cond(
            jnp.any(allowed),
            lambda held: absorb_block(held, query_block, key_block, value_block, allowed),
            lambda held: held,
            state,
        )

    piece = lax.all_gather(own_pairs, "seq", axis=0, tiled=True)
    total_rows = piece.shape[0]
    width = resp_len
    steps_count = total_rows // width

    def advance(index, state):
        offset = index * width
        block = lax.dynamic_slice_in_dim(piece, offset, width, 0)
        where_rows = offset + jnp.arange(width, dtype=jnp.int32)
        key_resp = where_rows // resp_len
        key_pos = where_rows % resp_len
        return tuple(
            (
                take_block(state[member], member, block, key_resp, key_pos)
                for member in range(len(members))
            )
        )

    final = lax.fori_loop(0, steps_count, advance, start_state)
    member = 0
    peak, total, summed = final[member]
    count = members[member][2]
    result = summed / total[..., None]
    outputs = jnp.transpose(result, (2, 0, 1, 3)).reshape(count, query_width)
    attended = outputs[None].astype(jnp.bfloat16)
    returned = lax.all_to_all(attended, "seq", split_axis=1, concat_axis=0, tiled=True)
    return lax.all_to_all(returned, "head", split_axis=0, concat_axis=2, tiled=True)


def solution(mesh):
    placed = (P("head", "seq", None), P("head", "seq", None), P("head", "seq", None), P())
    return jax.shard_map(
        local, mesh=mesh, in_specs=placed, out_specs=P("head", "seq", None), check_vma=False
    )
```

profile of v0, /device:TPU:1, one launch (start us, length us, event | category | flops | bytes accessed | tf_op | source)
XLA Modules:
  0.0 610.9 jit_solution(1927362102122485354)
XLA Ops:
  9.9 13.2 %all-to-all-start = ((bf16[8,2,2048]{2,1,0:T(2,128)(2,1)}), bf16[8,2,2048]{2,1,0:T(2,128)(2,1)S(1)}, u32[]{:S(2)}, u32[]{:S(2)}) async-start(bf16[8,2,2048]{2,1,0:T(2,128)(2,1)} %reshape.119), calls=%async_computation | async-start | bytes 131072 | tf_op jit(solution)/shard_map/all_to_all | solution.py:37
  26.5 6.4 %all-to-all-done = bf16[8,2,2048]{2,1,0:T(2,128)(2,1)S(1)} async-done(((bf16[8,2,2048]{2,1,0:T(2,128)(2,1)}), bf16[8,2,2048]{2,1,0:T(2,128)(2,1)S(1)}, u32[]{:S(2)}, u32[]{:S(2)}) %all-to-all-start) | async-done | bytes 65568 | tf_op jit(solution)/shard_map/all_to_all | solution.py:37
  32.9 3.5 all-to-all-start.1
  38.3 7.9 %all-to-all-done.1 = bf16[8,2,2048]{2,1,0:T(2,128)(2,1)S(1)} async-done(((bf16[8,2,2048]{2,1,0:T(2,128)(2,1)}), bf16[8,2,2048]{2,1,0:T(2,128)(2,1)S(1)}, u32[]{:S(2)}, u32[]{:S(2)}) %all-to-all-start.1) | async-done | bytes 65568 | tf_op jit(solution)/shard_map/all_to_all | solution.py:38
  48.1 33.3 %all_to_all.102 = bf16[64,4,256]{2,1,0:T(4,128)(2,1)S(1)} all-to-all(bf16[64,4,256]{2,1,0:T(4,128)(2,1)S(1)} %copy.99), channel_id=1, replica_groups=mesh['seq'=64,'head'=8] {'seq'}, dimensions={0} | all-to-all | bytes 262144 | tf_op jit(solution)/shard_map/all_to_all | solution.py:44
  82.1 15.8 %copy.100 = bf16[8,4,16384]{0,1,2:T(4,128)(2,1)} copy(bf16[8,4,16384]{2,1,0:T(4,128)(2,1)S(1)} %copy-done.3) | data formatting | bytes 2097152 | tf_op args[0]
  97.9 19.8 %reshape.121 = bf16[8,2,32768]{2,1,0:T(2,128)(2,1)S(1)} reshape(bf16[16384,4,8]{2,1,0:T(4,128)(2,1)} %bitcast.82) | data formatting | bytes 2097152
  117.7 71.6 %all_to_all.103 = bf16[8,2,32768]{2,1,0:T(2,128)(2,1)S(1)} all-to-all(bf16[8,2,32768]{2,1,0:T(2,128)(2,1)S(1)} %reshape.121), channel_id=1, replica_groups=mesh['seq'=64,'head'=8] {'head'}, dimensions={0} | all-to-all | bytes 2097152 | tf_op jit(solution)/shard_map/all_to_all | solution.py:36
  189.3 20.7 %reshape.122 = bf16[16384,4,8]{2,1,0:T(4,128)(2,1)} reshape(bf16[8,2,32768]{2,1,0:T(2,128)(2,1)S(1)} %all_to_all.103) | data formatting | bytes 2097152
  209.9 21.3 %copy.115 = bf16[8,4,8,2048]{3,0,2,1:T(8,128)(2,1)S(1)} copy(bf16[8,4,8,2048]{0,1,3,2:T(4,128)(2,1)} %bitcast.81) | data formatting | bytes 2097152 | tf_op jit(solution)/shard_map/all_to_all | solution.py:36
  233.0 4.8 all-to-all-start.4
  238.0 73.8 %all-to-all-done.4 = bf16[64,4,2048]{2,1,0:T(4,128)(2,1)S(1)} async-done(((bf16[64,4,2048]{2,1,0:T(4,128)(2,1)}), bf16[64,4,2048]{2,1,0:T(4,128)(2,1)S(1)}, u32[]{:S(2)}, u32[]{:S(2)}) %all-to-all-start.4) | async-done | bytes 1048608 | tf_op jit(solution)/shard_map/all_to_all | solution.py:43
  313.0 120.3 %while.19 = (s32[]{:T(128)}, f32[1,16,256]{2,1,0:T(8,128)S(1)}, f32[1,16,256]{2,1,0:T(8,128)S(1)}, f32[1,16,256,128]{3,2,1,0:T(8,128)S(1)}, s32[]{:T(128)}, /*in...) while((s32[]{:T(128)}, f32[1,16,256]{2,1,0:T(8,128)S(1)}, ...), condition=%wide.region_7.8_spmd, body=%wide.region_0.7_spmd.sunk | while | flops 551840256 | bytes 35264360 | solution.py:105
  314.6 8.2 %conditional.2 = ((f32[1,16,256]{2,1,0:T(8,128)S(1)}, f32[1,16,256]{2,1,0:T(8,128)S(1)}, f32[1,16,256,128]{3,2,1,0:T(8,128)S(1)})) conditional(s32[]{:T(128)} %convert_element_type.42, (f32[1,16,256]{2,1,0:T(8,128)S(1)}, f32[1,16,256]{2,1,0:T(8,128)S(1)}, f32[1,16,256,128]{3,2,1,0:T(8,128)S(1)}) %tuple.63, (pred[256,256]{0,1:T(8,128)(4,1)S(1)}, ...), branch_computations={%region_3.3_spmd, %region_4.6_spmd} | conditional | flops 551563264 | bytes 35192952 | solution.py:80
  314.7 3.6 fusion
  318.2 3.5 bitcast_add_fusion
  324.4 8.2 %conditional.2 = ((f32[1,16,256]{2,1,0:T(8,128)S(1)}, f32[1,16,256]{2,1,0:T(8,128)S(1)}, f32[1,16,256,128]{3,2,1,0:T(8,128)S(1)})) conditional(s32[]{:T(128)} %convert_element_type.42, (f32[1,16,256]{2,1,0:T(8,128)S(1)}, f32[1,16,256]{2,1,0:T(8,128)S(1)}, f32[1,16,256,128]{3,2,1,0:T(8,128)S(1)}) %tuple.63, (pred[256,256]{0,1:T(8,128)(4,1)S(1)}, ...), branch_computations={%region_3.3_spmd, %region_4.6_spmd} | conditional | flops 551563264 | bytes 35192952 | solution.py:80
  324.5 3.6 fusion
  328.1 3.5 bitcast_add_fusion
  437.0 2.0 copy.106
  439.5 6.8 %reduce.6 = bf16[256,2048]{1,0:T(8,128)(2,1)S(1)} reduce(bf16[256,1,2048]{2,1,0:T(2,128)(2,1)S(1)} %bitcast.83, bf16[]{:T(256)} %broadcast.305), dimensions={1}, to_apply=%bitcast.71.reduce_sub_computation | reduce | bytes 2097154
  447.2 77.8 %all_to_all.104 = bf16[64,2,4096]{2,1,0:T(2,128)(2,1)S(1)} all-to-all(bf16[64,2,4096]{2,1,0:T(2,128)(2,1)S(1)} %reshape.123), channel_id=1, replica_groups=mesh['seq'=64,'head'=8] {'seq'}, dimensions={0} | all-to-all | bytes 2097152 | tf_op jit(solution)/shard_map/all_to_all | solution.py:112
  526.1 6.1 bitcast_reduce_fusion
  532.6 69.1 %all_to_all.105 = bf16[64,4,2048]{2,1,0:T(4,128)(2,1)S(1)} all-to-all(bf16[64,4,2048]{2,1,0:T(4,128)(2,1)S(1)} %all_to_all.90), channel_id=1, replica_groups=mesh['seq'=64,'head'=8] {'head'}, dimensions={0} | all-to-all | bytes 2097152 | tf_op jit(solution)/shard_map/all_to_all | solution.py:113
  (430 shorter events, 87.8 us)
Async XLA Ops:
  6.5 231.3 %copy-start = (s32[64,6]{0,1:T(8,128)S(1)}, s32[64,6]{0,1:T(8,128)}, u32[]{:S(2)}) copy-start(s32[64,6]{0,1:T(8,128)} %param.11) | copy-start | bytes 4612
  9.9 72.2 %copy-start.3 = (bf16[8,4,16384]{2,1,0:T(4,128)(2,1)S(1)}, bf16[8,4,16384]{2,1,0:T(4,128)(2,1)}, u32[]{:S(2)}) copy-start(bf16[8,4,16384]{2,1,0:T(4,128)(2,1)} %param.8) | copy-start | bytes 3145732
  9.9 23.0 %all-to-all-start = ((bf16[8,2,2048]{2,1,0:T(2,128)(2,1)}), bf16[8,2,2048]{2,1,0:T(2,128)(2,1)S(1)}, u32[]{:S(2)}, u32[]{:S(2)}) async-start(bf16[8,2,2048]{2,1,0:T(2,128)(2,1)} %reshape.119), calls=%async_computation | async-start | bytes 131072 | tf_op jit(solution)/shard_map/all_to_all | solution.py:37
  32.9 13.3 %all-to-all-start.1 = ((bf16[8,2,2048]{2,1,0:T(2,128)(2,1)}), bf16[8,2,2048]{2,1,0:T(2,128)(2,1)S(1)}, u32[]{:S(2)}, u32[]{:S(2)}) async-start(bf16[8,2,2048]{2,1,0:T(2,128)(2,1)} %reshape.117), calls=%async_computation.1 | async-start | bytes 131072 | tf_op jit(solution)/shard_map/all_to_all | solution.py:38
  36.4 276.4 %all-gather.2.cloned.1.call-start = ((), (), s32[]{:S(2)}) async-start(), calls=%async_computation.7 | async-start | bytes 8519680 | tf_op jit(solution)/shard_map/all_gather | solution.py:87
  233.0 78.8 %all-to-all-start.4 = ((bf16[64,4,2048]{2,1,0:T(4,128)(2,1)}), bf16[64,4,2048]{2,1,0:T(4,128)(2,1)S(1)}, u32[]{:S(2)}, u32[]{:S(2)}) async-start(bf16[64,4,2048]{2,1,0:T(4,128)(2,1)} %copy.103), calls=%async_computation.4 | async-start | bytes 2097152 | tf_op jit(solution)/shard_map/all_to_all | solution.py:43
  318.2 3.5 copy-start.2
  328.0 3.5 copy-start.2
  526.1 78.0 %copy-start.1 = (s32[64,6]{0,1:T(8,128)S(1)}, s32[64,6]{0,1:T(8,128)}, u32[]{:S(2)}) copy-start(s32[64,6]{0,1:T(8,128)} %param.11) | copy-start | bytes 4612
Sparse Core Ops, SparseCore 0:
  82.2 198.5 all-gather.1
where the time goes:
time: 613 us; the launch traced here: 611 us
  blocking collectives  252 us (41%)
  local copies, waits for them, and re-layouts  107 us (17%)
  waiting for transfers between devices  88.1 us (14%)
  other arithmetic  72.3 us (12%)
  loops' own time  42.5 us (7%)
  starting transfers between devices  21.5 us (4%)
  matrix products  14.2 us (2%)
  between operations  13.6 us (2%)
    all_to_all x1, blocking collectives, local(): lax.all_to_all(attended, 'seq', split_axis=1, concat_axis=0, tiled=True)  77.8 us
    all_to_all x1, waiting for transfers between devices, local(): lax.all_to_all(moved_q, 'seq', split_axis=0, concat_axis=1, tiled=True)  73.8 us
    all_to_all x1, blocking collectives, local(): lax.all_to_all(queries, 'head', split_axis=2, concat_axis=0, tiled=True)  71.6 us
    all_to_all x1, blocking collectives, local(): lax.all_to_all(returned, 'head', split_axis=0, concat_axis=2, tiled=True)  69.1 us
    unnamed x19, local copies, waits for them, and re-layouts  67.9 us
    or x64, other arithmetic, allowed_for(): return own | cross[None, :]  53.5 us
    another operation x1, loops' own time, local(): final = lax.fori_loop(0, steps_count, advance, start_state)  41.5 us
    all_to_all x1, blocking collectives, local(): lax.all_to_all(pairs, 'seq', split_axis=0, concat_axis=1, tiled=True)  33.3 us
  transfers between devices with their start and end apart: 4, of which 3 were waited for; matrix products, arithmetic and copies ran while one was open for 14% of the time, Pallas kernels for 0%

commit v1 on v0

v1 whole, which is shorter than its diff:
```python
import functools
import math

import jax
import jax.numpy as jnp
from jax import lax
from jax.experimental import pallas as pl
from jax.experimental.pallas import tpu as pltpu
from jax.sharding import Mesh, PartitionSpec as P

HD = 128
SLOTS = 6
FACTOR = HD ** (-0.5) * math.log2(math.e)
CHUNK = 512
PLANE = ("x", "y", "c")
OWN, ONE, TWO, EIGHT, SIXTEEN, THIRTYTWO = 0, 2, 4, 6, 8, 10
SOURCES = (
    (ONE, TWO, EIGHT + 1, EIGHT, SIXTEEN, THIRTYTWO),
    (ONE + 1, TWO + 1, OWN, EIGHT + 1, SIXTEEN + 1, THIRTYTWO + 1),
)


def attend_kernel(live_ref, place_ref, q_ref, own_ref, one_ref, two_ref, *refs):
    halves = refs[:6]
    o_ref, k_all, v_all, s_all, peak, acc = refs[6:]
    half_keys = k_all.shape[1] // 2
    keys = 2 * half_keys
    zh, x = place_ref[0], place_ref[1]
    v_all[:, :, HD:] = jnp.ones((v_all.shape[0], keys, HD), jnp.bfloat16)

    def keep(index, half, key_block, value_block):
        at = half * half_keys
        k_all[index, at : at + half_keys, :] = key_block
        v_all[index, at : at + half_keys, :HD] = value_block

    for half in range(2):
        for m in range(2):
            keep(OWN + m, half, own_ref[half, 0, m], own_ref[half, 1, m])
            keep(ONE + jnp.where(x < 1, 1 - m, m), half, one_ref[m, half, 0], one_ref[m, half, 1])
            keep(TWO + jnp.where(x < 2, 1 - m, m), half, two_ref[m, half, 0], two_ref[m, half, 1])
            for place, pair in ((EIGHT, 0), (SIXTEEN, 2), (THIRTYTWO, 4)):
                keep(place + m, half, halves[pair + half][0, m], halves[pair + half][1, m])

    sources = q_ref.shape[0]
    per = q_ref.shape[2]
    step_sources = CHUNK // per

    def scores_of(query, index):
        return (
            lax.dot_general(
                query, k_all[index], (((1,), (1,)), ((), ())), preferred_element_type=jnp.float32
            )
            * FACTOR
        )

    def sums_of(slot, index):
        top = peak[...]
        shifted = s_all[slot] - jnp.concatenate([top] * (keys // HD), axis=1)
        return jnp.dot(
            jnp.exp2(shifted).astype(jnp.bfloat16), v_all[index], preferred_element_type=jnp.float32
        )

    def widest(scores):
        return functools.reduce(
            jnp.maximum, [scores[:, at : at + HD] for at in range(0, keys, HD)]
        )

    key = lax.broadcasted_iota(jnp.int32, (1, keys), 1)
    inner = key % half_keys
    key_half = jnp.where(key < half_keys, zh, 1 - zh)
    key_pos = (inner // 32) * 64 + key_half * 32 + inner % 32

    for m in range(2):

        def chunk(step, carry, m=m):
            start = step * step_sources
            query = q_ref[pl.ds(start, step_sources), m].reshape(CHUNK, HD)
            row = lax.broadcasted_iota(jnp.int32, (CHUNK, 1), 0)
            source = start + row // per
            query_pos = (source // 8) * 64 + zh * 32 + (source % 8) * 4 + row % 4
            scores = jnp.where(key_pos <= query_pos, scores_of(query, OWN + m), -1e30)
            s_all[0] = scores
            peak[...] = widest(scores)
            for slot, index in enumerate(SOURCES[m]):

                @pl.when(live_ref[m, slot] != 0)
                def _(slot=slot, index=index):
                    scores = scores_of(query, index)
                    s_all[slot + 1] = scores
                    peak[...] = jnp.maximum(peak[...], widest(scores))

            peak[...] = jnp.broadcast_to(jnp.max(peak[...], axis=1, keepdims=True), (CHUNK, HD))
            acc[...] = sums_of(0, OWN + m)
            for slot, index in enumerate(SOURCES[m]):

                @pl.when(live_ref[m, slot] != 0)
                def _(slot=slot, index=index):
                    acc[...] += sums_of(slot + 1, index)

            result = (acc[:, :HD] / acc[:, HD:]).astype(jnp.bfloat16)
            o_ref[pl.ds(start, step_sources), m] = result.reshape(step_sources, per, HD)
            return carry

        lax.fori_loop(0, sources // step_sources, chunk, 0)


def attend(live, place, query, own, one, two, halves):
    keys = 2 * own.shape[3]
    smem = pl.BlockSpec(memory_space=pltpu.SMEM)
    vmem = pl.BlockSpec(memory_space=pltpu.VMEM)
    return pl.pallas_call(
        attend_kernel,
        out_shape=jax.ShapeDtypeStruct(query.shape, jnp.bfloat16),
        in_specs=[smem, smem] + [vmem] * (4 + len(halves)),
        out_specs=vmem,
        scratch_shapes=[
            pltpu.VMEM((12, keys, HD), jnp.bfloat16),
            pltpu.VMEM((12, keys, 2 * HD), jnp.bfloat16),
            pltpu.VMEM((SLOTS + 1, CHUNK, keys), jnp.float32),
            pltpu.VMEM((CHUNK, HD), jnp.float32),
            pltpu.VMEM((CHUNK, 2 * HD), jnp.float32),
        ],
        compiler_params=pltpu.CompilerParams(vmem_limit_bytes=40 * 1024 * 1024),
    )(live, place, query, own, one, two, *halves)


def ring(value, by, keep=lambda h: True):
    pairs = [(z, (z + by) % 16) for z in range(16) if keep(z % 8)]
    return lax.ppermute(value, ("zh", "h"), pairs)


def along(value, by):
    return ring(value, by, lambda h: h + by < 8)


def across(value, by, rises):
    pairs = []
    for x in range(4):
        for h in range(8):
            to = h + 1 if rises and x + by >= 4 else h
            if to < 8:
                pairs.append((x * 8 + h, (x + by) % 4 * 8 + to))
    return lax.ppermute(value, ("x", "h"), pairs)


def local(queries, keys, values, links):
    resp, near, width = queries.shape
    groups = keys.shape[2] // HD
    repeat = width // keys.shape[2]
    x, zh, h = lax.axis_index("x"), lax.axis_index("zh"), lax.axis_index("h")

    with jax.named_scope("key_value_exchange"):
        pairs = jnp.stack([keys, values]).reshape(2, 2, 4, near, groups, HD)
        pairs = pairs.transpose(2, 4, 0, 1, 3, 5).reshape(4 * groups, 2, 2, near, HD)
        pairs = lax.all_to_all(pairs, PLANE, split_axis=0, concat_axis=0, tiled=True)
        pairs = pairs.transpose(1, 2, 0, 3, 4).reshape(2, 2, 4 * groups * near, HD)
    with jax.named_scope("query_exchange"):
        packed = queries.reshape(2, 4, near, groups, repeat, HD).transpose(1, 3, 0, 4, 2, 5)
        packed = packed.reshape(4 * groups, 2, repeat * near, HD)
        query = lax.all_to_all(packed, PLANE, split_axis=0, concat_axis=0, tiled=True)
    with jax.named_scope("key_value_spread"):
        above = ring(pairs, -4)
        below = along(pairs, 4)
        eight = along(pairs, 1)
        sixteen = along(pairs, 2)
        other = ring(above, -4)
        pairs, other, above, below, eight, sixteen = lax.optimization_barrier(
            (pairs, other, above, below, eight, sixteen)
        )
        own = jnp.stack([pairs, other])
        blocks = own.transpose(2, 0, 1, 3, 4)
        one = jnp.stack([across(blocks[0], 1, False), across(blocks[1], 1, True)])
        two = jnp.stack([across(blocks[0], 2, False), across(blocks[1], 2, True)])
        halves = (eight, along(other, 1), sixteen, along(other, 2), below, above)
    with jax.named_scope("attend"):
        place = jnp.stack([zh, x]).astype(jnp.int32)
        index = h * resp + x + 4 * jnp.arange(2)
        live = (links[index] != index[:, None]).astype(jnp.int32)
        result = attend(live, place, query, own, one, two, halves)
    with jax.named_scope("return_exchange"):
        result = lax.all_to_all(result, PLANE, split_axis=0, concat_axis=0, tiled=True)
        result = result.reshape(4, groups, 2, repeat, near, HD).transpose(2, 0, 4, 1, 3, 5)
        return result.reshape(resp, near, width)


def solution(mesh):
    fine = Mesh(mesh.devices.reshape(4, 2, 4, 2, 8), ("x", "zh", "y", "c", "h"))
    placed = P("h", ("x", "zh", "y", "c"), None)
    return jax.shard_map(
        local, mesh=fine, in_specs=(placed, placed, placed, P()), out_specs=placed, check_vma=False
    )
```

time: 613 us -> 140 us (0.23)
  the two profiles are of different devices: /device:TPU:1 before, /device:TPU:161 now
where the time goes in v1:
time: 140 us
  blocking collectives  52.9 us (38%)
  starting transfers between devices  36.7 us (26%)
  waiting for transfers between devices  26 us (19%)
  Pallas kernels  16.2 us (12%)
  local copies, waits for them, and re-layouts  7.45 us (5%)
    all_to_all x1, blocking collectives, local(): lax.all_to_all(result, PLANE, split_axis=0, concat_axis=0, tiled=True)  37.6 us
    ppermute x7, waiting for transfers between devices, ring(): return lax.ppermute(value, ('zh', 'h'), pairs)  21.5 us
    ppermute x7, starting transfers between devices, ring(): return lax.ppermute(value, ('zh', 'h'), pairs)  21.2 us
    pallas_call x1, Pallas kernels, attend(): pl.pallas_call(attend_kernel, out_shape=jax.ShapeDtypeStruct(query.shape,...  16.2 us
    all_to_all x1, blocking collectives, local(): lax.all_to_all(pairs, PLANE, split_axis=0, concat_axis=0, tiled=True)  15.3 us
    ppermute x4, starting transfers between devices, across(): return lax.ppermute(value, ('x', 'h'), pairs)  11.6 us
    ppermute x4, waiting for transfers between devices, across(): return lax.ppermute(value, ('x', 'h'), pairs)  4.5 us
    all_to_all x1, starting transfers between devices, local(): lax.all_to_all(packed, PLANE, split_axis=0, concat_axis=0, tiled=True)  3.98 us
  transfers between devices with their start and end apart: 12, of which 7 were waited for; matrix products, arithmetic and copies ran while one was open for 3% of the time, Pallas kernels for 0%

profile of v1, /device:TPU:161, one launch (start us, length us, event | category | flops | bytes accessed | tf_op | source)
XLA Modules:
  0.0 139.9 jit_solution(3880905998458755864)
XLA Ops:
  0.0 1.0 stack.49
  1.0 0.9 stack.48
  2.0 15.3 %all_to_all.15 = bf16[32,2,2,4,128]{4,3,2,1,0:T(4,128)(2,1)S(1)} all-to-all(bf16[32,2,2,4,128]{4,3,2,1,0:T(4,128)(2,1)S(1)} %bitcast.32), channel_id=1, replica_groups=mesh['x'=4,'zh'=2,'y'=4,'c'=2,'h'=8] {'x','y','c'}, dimensions={0} | all-to-all | bytes 262144 | tf_op jit(solution)/shard_map/key_value_exchange/all_to_all | solution.py:155
  17.3 1.9 %collective-permute-start = (bf16[2,2,128,128]{3,2,1,0:T(8,128)(2,1)S(1)}, bf16[2,2,128,128]{3,2,1,0:T(8,128)(2,1)S(1)}, u32[]{:S(2)}, u32[]{:S(2)}) collective-permute-start(bf16[2,2,128,128]{3,2,1,0:T(8,128)(2,1)S(1)} %bitcast.34), channel_id=1, source_target_pairs={{0,68},{1,69},{2,70},{3,71},{4,0},{5,1},{6,2},{7,3},{64,4},{65,5},... | collective-permute-start | bytes 393224 | tf_op jit(solution)/shard_map/key_value_spread/ppermute | solution.py:129
  19.3 1.1 reshape.44
  20.4 2.3 %copy.11 = bf16[2,4,4,8,16,128]{5,2,4,0,3,1:T(4,128)(2,1)} copy(bf16[2,4,4,8,16,128]{5,4,3,2,1,0:T(8,128)(2,1)S(1)} %reshape.44) | data formatting | bytes 2097152 | tf_op jit(solution)/shard_map/query_exchange/reshape | solution.py:158
  22.7 4.0 %all-to-all-start = ((bf16[32,2,64,128]{3,2,1,0:T(8,128)(2,1)}), bf16[32,2,64,128]{3,2,1,0:T(8,128)(2,1)S(1)}, u32[]{:S(2)}, u32[]{:S(2)}) async-start(bf16[32,2,64,128]{3,2,1,0:T(8,128)(2,1)} %bitcast.4), calls=%async_computation | async-start | bytes 2097152 | tf_op jit(solution)/shard_map/query_exchange/all_to_all | solution.py:160
  26.7 1.3 collective-permute-start.2
  28.0 3.5 %collective-permute-start.3 = (bf16[2,2,128,128]{3,2,1,0:T(8,128)(2,1)S(1)}, bf16[2,2,128,128]{3,2,1,0:T(8,128)(2,1)S(1)}, u32[]{:S(2)}, u32[]{:S(2)}) collective-permute-start(bf16[2,2,128,128]{3,2,1,0:T(8,128)(2,1)S(1)} %bitcast.36), channel_id=1, source_target_pairs={{0,1},{1,2},{2,3},{3,4},{4,5},{5,6},{6,7},{64,65},{65,66},{66,67},... | collective-permute-start | bytes 393224 | tf_op jit(solution)/shard_map/key_value_spread/ppermute | solution.py:129
  31.6 2.6 %collective-permute-start.4 = (bf16[2,2,128,128]{3,2,1,0:T(8,128)(2,1)S(1)}, bf16[2,2,128,128]{3,2,1,0:T(8,128)(2,1)S(1)}, u32[]{:S(2)}, u32[]{:S(2)}) collective-permute-start(bf16[2,2,128,128]{3,2,1,0:T(8,128)(2,1)S(1)} %bitcast.37), channel_id=1, source_target_pairs={{0,2},{1,3},{2,4},{3,5},{4,6},{5,7},{64,66},{65,67},{66,68},{67,69... | collective-permute-start | bytes 393224 | tf_op jit(solution)/shard_map/key_value_spread/ppermute | solution.py:129
  34.2 1.2 collective-permute-done.refs_5_
  35.4 7.9 %collective-permute-start.1 = (bf16[2,2,128,128]{3,2,1,0:T(8,128)(2,1)S(1)}, bf16[2,2,128,128]{3,2,1,0:T(8,128)(2,1)S(1)}, u32[]{:S(2)}, u32[]{:S(2)}) collective-permute-start(bf16[2,2,128,128]{3,2,1,0:T(8,128)(2,1)S(1)} %collective-permute-done.refs_5_), channel_id=1, source_target_pairs={{0,68},{1,69},{2,70},{3,71},{4,0},{5,1},{6,2},{7,3},{64,4},{65,5},... | collective-permute-start | bytes 393224 | tf_op jit(solution)/shard_map/key_value_spread/ppermute | solution.py:129
  44.1 11.9 %collective-permute-done.4.refs_2_ = bf16[2,2,128,128]{3,2,1,0:T(8,128)(2,1)S(1)} collective-permute-done((bf16[2,2,128,128]{3,2,1,0:T(8,128)(2,1)S(1)}, bf16[2,2,128,128]{3,2,1,0:T(8,128)(2,1)S(1)}, u32[]{:S(2)}, u32[]{:S(2)}) %collective-permute-start.4) | collective-permute-done | bytes 131104 | tf_op jit(solution)/shard_map/key_value_spread/ppermute | solution.py:129
  56.7 3.3 %collective-permute-start.6 = (bf16[2,2,128,128]{3,2,1,0:T(8,128)(2,1)S(1)}, bf16[2,2,128,128]{3,2,1,0:T(8,128)(2,1)S(1)}, u32[]{:S(2)}, u32[]{:S(2)}) collective-permute-start(bf16[2,2,128,128]{3,2,1,0:T(8,128)(2,1)S(1)} %get-tuple-element.18), channel_id=1, source_target_pairs={{0,128},{1,129},{2,130},{3,131},{4,132},{5,133},{6,134},{7,135},{1... | collective-permute-start | bytes 393224 | tf_op jit(solution)/shard_map/key_value_spread/ppermute | solution.py:143
  60.1 3.1 %collective-permute-start.5 = (bf16[2,2,128,128]{3,2,1,0:T(8,128)(2,1)S(1)}, bf16[2,2,128,128]{3,2,1,0:T(8,128)(2,1)S(1)}, u32[]{:S(2)}, u32[]{:S(2)}) collective-permute-start(bf16[2,2,128,128]{3,2,1,0:T(8,128)(2,1)S(1)} %get-tuple-element.17), channel_id=1, source_target_pairs={{0,128},{1,129},{2,130},{3,131},{4,132},{5,133},{6,134},{7,135},{1... | collective-permute-start | bytes 393224 | tf_op jit(solution)/shard_map/key_value_spread/ppermute | solution.py:143
  63.3 3.2 %collective-permute-start.8 = (bf16[2,2,128,128]{3,2,1,0:T(8,128)(2,1)S(1)}, bf16[2,2,128,128]{3,2,1,0:T(8,128)(2,1)S(1)}, u32[]{:S(2)}, u32[]{:S(2)}) collective-permute-start(bf16[2,2,128,128]{3,2,1,0:T(8,128)(2,1)S(1)} %get-tuple-element.18), channel_id=1, source_target_pairs={{0,256},{1,257},{2,258},{3,259},{4,260},{5,261},{6,262},{7,263},{1... | collective-permute-start | bytes 393224 | tf_op jit(solution)/shard_map/key_value_spread/ppermute | solution.py:143
  66.5 1.9 %collective-permute-start.7 = (bf16[2,2,128,128]{3,2,1,0:T(8,128)(2,1)S(1)}, bf16[2,2,128,128]{3,2,1,0:T(8,128)(2,1)S(1)}, u32[]{:S(2)}, u32[]{:S(2)}) collective-permute-start(bf16[2,2,128,128]{3,2,1,0:T(8,128)(2,1)S(1)} %get-tuple-element.17), channel_id=1, source_target_pairs={{0,256},{1,257},{2,258},{3,259},{4,260},{5,261},{6,262},{7,263},{1... | collective-permute-start | bytes 393224 | tf_op jit(solution)/shard_map/key_value_spread/ppermute | solution.py:143
  68.5 1.9 %collective-permute-start.9 = (bf16[2,2,128,128]{3,2,1,0:T(8,128)(2,1)S(1)}, bf16[2,2,128,128]{3,2,1,0:T(8,128)(2,1)S(1)}, u32[]{:S(2)}, u32[]{:S(2)}) collective-permute-start(bf16[2,2,128,128]{3,2,1,0:T(8,128)(2,1)S(1)} %collective-permute-done.1), channel_id=1, source_target_pairs={{0,1},{1,2},{2,3},{3,4},{4,5},{5,6},{6,7},{64,65},{65,66},{66,67},... | collective-permute-start | bytes 393224 | tf_op jit(solution)/shard_map/key_value_spread/ppermute | solution.py:129
  70.4 1.9 %collective-permute-start.10 = (bf16[2,2,128,128]{3,2,1,0:T(8,128)(2,1)S(1)}, bf16[2,2,128,128]{3,2,1,0:T(8,128)(2,1)S(1)}, u32[]{:S(2)}, u32[]{:S(2)}) collective-permute-start(bf16[2,2,128,128]{3,2,1,0:T(8,128)(2,1)S(1)} %collective-permute-done.1), channel_id=1, source_target_pairs={{0,2},{1,3},{2,4},{3,5},{4,6},{5,7},{64,66},{65,67},{66,68},{67,69... | collective-permute-start | bytes 393224 | tf_op jit(solution)/shard_map/key_value_spread/ppermute | solution.py:129
  73.2 3.7 %collective-permute-done.7 = bf16[2,2,128,128]{3,2,1,0:T(8,128)(2,1)S(1)} collective-permute-done((bf16[2,2,128,128]{3,2,1,0:T(8,128)(2,1)S(1)}, bf16[2,2,128,128]{3,2,1,0:T(8,128)(2,1)S(1)}, u32[]{:S(2)}, u32[]{:S(2)}) %collective-permute-start.7) | collective-permute-done | bytes 131104 | tf_op jit(solution)/shard_map/key_value_spread/ppermute | solution.py:143
  77.1 7.6 %collective-permute-done.10.refs_3_ = bf16[2,2,128,128]{3,2,1,0:T(8,128)(2,1)S(1)} collective-permute-done((bf16[2,2,128,128]{3,2,1,0:T(8,128)(2,1)S(1)}, bf16[2,2,128,128]{3,2,1,0:T(8,128)(2,1)S(1)}, u32[]{:S(2)}, u32[]{:S(2)}) %collective-permute-start.10) | collective-permute-done | bytes 131104 | tf_op jit(solution)/shard_map/key_value_spread/ppermute | solution.py:129
  84.6 16.2 %attend.1 = bf16[32,2,64,128]{3,2,1,0:T(8,128)(2,1)S(1)} custom-call(s32[2,6]{1,0:T(2,128)S(1)} %compare_convert_fusion.live_ref, s32[2]{0:T(128)S(1)} %pad_add_fusion.place_ref, bf16[32,2,64,128]{3,2,1,0:T(8,128)(2,1)S(1)} %all-to-all-done.q_ref, bf16[2,2,2,128,128]{4,3,2,1,0:T(8,128)(2,1)S(1)} %get-tuple-element.20.own_ref, ...), custom_call_target="tpu_custom_call" | custom-call | tf_op jit(solution)/shard_map/attend/pallas_call | solution.py:111
  100.9 37.6 %all_to_all.16 = bf16[32,2,64,128]{3,2,1,0:T(8,128)(2,1)S(1)} all-to-all(bf16[32,2,64,128]{3,2,1,0:T(8,128)(2,1)S(1)} %attend.1), channel_id=1, replica_groups=mesh['x'=4,'zh'=2,'y'=4,'c'=2,'h'=8] {'x','y','c'}, dimensions={0} | all-to-all | bytes 2097152 | tf_op jit(solution)/shard_map/return_exchange/all_to_all | solution.py:181
  138.7 1.1 reshape.49
  (28 shorter events, 3.0 us)
Async XLA Ops:
  0.0 19.2 %copy-start = (bf16[8,4,16384]{2,1,0:T(4,128)(2,1)S(1)}, bf16[8,4,16384]{2,1,0:T(4,128)(2,1)}, u32[]{:S(2)}) copy-start(bf16[8,4,16384]{2,1,0:T(4,128)(2,1)} %param.4) | copy-start | bytes 3145732
  17.3 18.1 %collective-permute-start = (bf16[2,2,128,128]{3,2,1,0:T(8,128)(2,1)S(1)}, bf16[2,2,128,128]{3,2,1,0:T(8,128)(2,1)S(1)}, u32[]{:S(2)}, u32[]{:S(2)}) collective-permute-start(bf16[2,2,128,128]{3,2,1,0:T(8,128)(2,1)S(1)} %bitcast.34), channel_id=1, source_target_pairs={{0,68},{1,69},{2,70},{3,71},{4,0},{5,1},{6,2},{7,3},{64,4},{65,5},... | collective-permute-start | bytes 393224 | tf_op jit(solution)/shard_map/key_value_spread/ppermute | solution.py:129
  22.7 61.9 %all-to-all-start = ((bf16[32,2,64,128]{3,2,1,0:T(8,128)(2,1)}), bf16[32,2,64,128]{3,2,1,0:T(8,128)(2,1)S(1)}, u32[]{:S(2)}, u32[]{:S(2)}) async-start(bf16[32,2,64,128]{3,2,1,0:T(8,128)(2,1)} %bitcast.4), calls=%async_computation | async-start | bytes 2097152 | tf_op jit(solution)/shard_map/query_exchange/all_to_all | solution.py:160
  26.7 16.7 %copy-start.1 = (s32[64,6]{0,1:T(8,128)S(1)}, s32[64,6]{0,1:T(8,128)}, u32[]{:S(2)}) copy-start(s32[64,6]{0,1:T(8,128)} %param.7) | copy-start | bytes 4612
  26.7 17.3 %collective-permute-start.2 = (bf16[2,2,128,128]{3,2,1,0:T(8,128)(2,1)S(1)}, bf16[2,2,128,128]{3,2,1,0:T(8,128)(2,1)S(1)}, u32[]{:S(2)}, u32[]{:S(2)}) collective-permute-start(bf16[2,2,128,128]{3,2,1,0:T(8,128)(2,1)S(1)} %bitcast.35), channel_id=1, source_target_pairs={{0,4},{1,5},{2,6},{3,7},{64,68},{65,69},{66,70},{67,71},{8,12},{9,... | collective-permute-start | bytes 393224 | tf_op jit(solution)/shard_map/key_value_spread/ppermute | solution.py:129
  28.0 16.1 %collective-permute-start.3 = (bf16[2,2,128,128]{3,2,1,0:T(8,128)(2,1)S(1)}, bf16[2,2,128,128]{3,2,1,0:T(8,128)(2,1)S(1)}, u32[]{:S(2)}, u32[]{:S(2)}) collective-permute-start(bf16[2,2,128,128]{3,2,1,0:T(8,128)(2,1)S(1)} %bitcast.36), channel_id=1, source_target_pairs={{0,1},{1,2},{2,3},{3,4},{4,5},{5,6},{6,7},{64,65},{65,66},{66,67},... | collective-permute-start | bytes 393224 | tf_op jit(solution)/shard_map/key_value_spread/ppermute | solution.py:129
  31.6 24.4 %collective-permute-start.4 = (bf16[2,2,128,128]{3,2,1,0:T(8,128)(2,1)S(1)}, bf16[2,2,128,128]{3,2,1,0:T(8,128)(2,1)S(1)}, u32[]{:S(2)}, u32[]{:S(2)}) collective-permute-start(bf16[2,2,128,128]{3,2,1,0:T(8,128)(2,1)S(1)} %bitcast.37), channel_id=1, source_target_pairs={{0,2},{1,3},{2,4},{3,5},{4,6},{5,7},{64,66},{65,67},{66,68},{67,69... | collective-permute-start | bytes 393224 | tf_op jit(solution)/shard_map/key_value_spread/ppermute | solution.py:129
  35.4 21.2 %collective-permute-start.1 = (bf16[2,2,128,128]{3,2,1,0:T(8,128)(2,1)S(1)}, bf16[2,2,128,128]{3,2,1,0:T(8,128)(2,1)S(1)}, u32[]{:S(2)}, u32[]{:S(2)}) collective-permute-start(bf16[2,2,128,128]{3,2,1,0:T(8,128)(2,1)S(1)} %collective-permute-done.refs_5_), channel_id=1, source_target_pairs={{0,68},{1,69},{2,70},{3,71},{4,0},{5,1},{6,2},{7,3},{64,4},{65,5},... | collective-permute-start | bytes 393224 | tf_op jit(solution)/shard_map/key_value_spread/ppermute | solution.py:129
  56.7 13.7 %collective-permute-start.6 = (bf16[2,2,128,128]{3,2,1,0:T(8,128)(2,1)S(1)}, bf16[2,2,128,128]{3,2,1,0:T(8,128)(2,1)S(1)}, u32[]{:S(2)}, u32[]{:S(2)}) collective-permute-start(bf16[2,2,128,128]{3,2,1,0:T(8,128)(2,1)S(1)} %get-tuple-element.18), channel_id=1, source_target_pairs={{0,128},{1,129},{2,130},{3,131},{4,132},{5,133},{6,134},{7,135},{1... | collective-permute-start | bytes 393224 | tf_op jit(solution)/shard_map/key_value_spread/ppermute | solution.py:143
  60.1 12.3 %collective-permute-start.5 = (bf16[2,2,128,128]{3,2,1,0:T(8,128)(2,1)S(1)}, bf16[2,2,128,128]{3,2,1,0:T(8,128)(2,1)S(1)}, u32[]{:S(2)}, u32[]{:S(2)}) collective-permute-start(bf16[2,2,128,128]{3,2,1,0:T(8,128)(2,1)S(1)} %get-tuple-element.17), channel_id=1, source_target_pairs={{0,128},{1,129},{2,130},{3,131},{4,132},{5,133},{6,134},{7,135},{1... | collective-permute-start | bytes 393224 | tf_op jit(solution)/shard_map/key_value_spread/ppermute | solution.py:143
  63.3 9.9 %collective-permute-start.8 = (bf16[2,2,128,128]{3,2,1,0:T(8,128)(2,1)S(1)}, bf16[2,2,128,128]{3,2,1,0:T(8,128)(2,1)S(1)}, u32[]{:S(2)}, u32[]{:S(2)}) collective-permute-start(bf16[2,2,128,128]{3,2,1,0:T(8,128)(2,1)S(1)} %get-tuple-element.18), channel_id=1, source_target_pairs={{0,256},{1,257},{2,258},{3,259},{4,260},{5,261},{6,262},{7,263},{1... | collective-permute-start | bytes 393224 | tf_op jit(solution)/shard_map/key_value_spread/ppermute | solution.py:143
  66.5 10.4 %collective-permute-start.7 = (bf16[2,2,128,128]{3,2,1,0:T(8,128)(2,1)S(1)}, bf16[2,2,128,128]{3,2,1,0:T(8,128)(2,1)S(1)}, u32[]{:S(2)}, u32[]{:S(2)}) collective-permute-start(bf16[2,2,128,128]{3,2,1,0:T(8,128)(2,1)S(1)} %get-tuple-element.17), channel_id=1, source_target_pairs={{0,256},{1,257},{2,258},{3,259},{4,260},{5,261},{6,262},{7,263},{1... | collective-permute-start | bytes 393224 | tf_op jit(solution)/shard_map/key_value_spread/ppermute | solution.py:143
  68.5 8.6 %collective-permute-start.9 = (bf16[2,2,128,128]{3,2,1,0:T(8,128)(2,1)S(1)}, bf16[2,2,128,128]{3,2,1,0:T(8,128)(2,1)S(1)}, u32[]{:S(2)}, u32[]{:S(2)}) collective-permute-start(bf16[2,2,128,128]{3,2,1,0:T(8,128)(2,1)S(1)} %collective-permute-done.1), channel_id=1, source_target_pairs={{0,1},{1,2},{2,3},{3,4},{4,5},{5,6},{6,7},{64,65},{65,66},{66,67},... | collective-permute-start | bytes 393224 | tf_op jit(solution)/shard_map/key_value_spread/ppermute | solution.py:129
  70.4 14.2 %collective-permute-start.10 = (bf16[2,2,128,128]{3,2,1,0:T(8,128)(2,1)S(1)}, bf16[2,2,128,128]{3,2,1,0:T(8,128)(2,1)S(1)}, u32[]{:S(2)}, u32[]{:S(2)}) collective-permute-start(bf16[2,2,128,128]{3,2,1,0:T(8,128)(2,1)S(1)} %collective-permute-done.1), channel_id=1, source_target_pairs={{0,2},{1,3},{2,4},{3,5},{4,6},{5,7},{64,66},{65,67},{66,68},{67,69... | collective-permute-start | bytes 393224 | tf_op jit(solution)/shard_map/key_value_spread/ppermute | solution.py:129

commit v2 on v1

v2 whole, which is shorter than its diff:
```python
import functools
import math

import jax
import jax.numpy as jnp
from jax import lax
from jax.experimental import pallas as pl
from jax.experimental.pallas import tpu as pltpu
from jax.sharding import Mesh, PartitionSpec as P

HD = 128
SLOTS = 6
FACTOR = HD ** (-0.5) * math.log2(math.e)
CHUNK = 1024
SAFE_CHUNK = 512
LEAST, MOST = 2.0**-60, 2.0**60
PLANE = ("x", "y", "c")
OWN, ONE, TWO, EIGHT, SIXTEEN, THIRTYTWO = 0, 2, 4, 6, 8, 10
SOURCES = (
    (ONE + 1, ONE, TWO, EIGHT, SIXTEEN, THIRTYTWO),
    (OWN, ONE + 1, TWO + 1, EIGHT + 1, SIXTEEN + 1, THIRTYTWO + 1),
)


def scores_of(query, key_block):
    dims = (((1,), (1,)), ((), ()))
    return lax.dot_general(query, key_block, dims, preferred_element_type=jnp.float32) * FACTOR


def causal(start, count, per, zh, half_keys):
    key = lax.broadcasted_iota(jnp.int32, (1, 2 * half_keys), 1)
    inner = key % half_keys
    key_half = jnp.where(key < half_keys, zh, 1 - zh)
    key_pos = (inner // 32) * 64 + key_half * 32 + inner % 32
    row = lax.broadcasted_iota(jnp.int32, (count, 1), 0)
    source = start + row // per
    query_pos = (source // 8) * 64 + zh * 32 + (source % 8) * 4 + row % 4
    return key_pos <= query_pos


def place_block(k_some, v_some, at, block, m, live):
    half_keys = block.shape[3]
    keys = 2 * half_keys
    for half in range(2):
        columns = slice(half * half_keys, (half + 1) * half_keys)
        k_some[at, :, columns] = block[half, 0, m].T
        rows = slice(at * keys + half * half_keys, at * keys + (half + 1) * half_keys)
        ones = jnp.ones((half_keys, HD), jnp.bfloat16)
        value_block = block[half, 1, m]
        if live is not None:
            alive = jnp.where(live != 0, 1.0, 0.0) > 0
            value_block = jnp.where(alive, value_block, jnp.zeros_like(value_block))
            ones = jnp.where(alive, ones, jnp.zeros_like(ones))
        v_some[rows, :HD] = value_block
        v_some[rows, HD:] = ones


def weighted(query, k_some, v_some, first, count, allowed):
    keys = k_some.shape[2]
    parts = []
    for at in range(first, first + count):
        scores = jnp.dot(query, k_some[at], preferred_element_type=jnp.float32)
        weights = jnp.exp2(scores * FACTOR)
        if allowed is not None and at == first:
            weights = jnp.where(allowed, weights, 0.0)
        parts.append(weights.astype(jnp.bfloat16))
    values = v_some[first * keys : (first + count) * keys, :]
    return jnp.dot(jnp.concatenate(parts, axis=1), values, preferred_element_type=jnp.float32)


def early_kernel(live_ref, place_ref, q_ref, own, o_ref, k_some, v_some):
    zh = place_ref[0]
    place_block(k_some, v_some, 0, own, 0, None)
    place_block(k_some, v_some, 1, own, 1, None)
    place_block(k_some, v_some, 2, own, 0, live_ref[1, 0])
    per = q_ref.shape[2]
    step_sources = CHUNK // per
    for m in range(2):

        def chunk(step, carry, m=m):
            start = step * step_sources
            query = q_ref[pl.ds(start, step_sources), m].reshape(CHUNK, HD)
            allowed = causal(start, CHUNK, per, zh, own.shape[3])
            total = weighted(query, k_some, v_some, m, 1 + m, allowed)
            o_ref[pl.ds(start, step_sources), m] = total.reshape(step_sources, per, 2 * HD)
            return carry

        lax.fori_loop(0, q_ref.shape[0] // step_sources, chunk, 0)


def late_kernel(live_ref, place_ref, q_ref, early_ref, *refs):
    blocks = refs[:6]
    o_ref, k_some, v_some, k_all, v_all, s_all, peak, acc, bad_ref = refs[6:]
    own, one, two, eight, sixteen, thirtytwo = blocks
    zh = place_ref[0]
    half_keys = own.shape[3]
    keys = 2 * half_keys
    per = q_ref.shape[2]
    firsts, counts = (0, 6), (6, 5)
    for m in range(2):
        sets = [(one, 1, m), (two, m, 2), (eight, m, 3), (sixteen, m, 4), (thirtytwo, m, 5)]
        if m == 0:
            sets.append((one, 0, 1))
        for at, (block, which, slot) in enumerate(sets):
            place_block(k_some, v_some, firsts[m] + at, block, which, live_ref[m, slot])
    bad_ref[...] = jnp.zeros_like(bad_ref)

    for m in range(2):
        step_sources = CHUNK // per

        def quick(step, carry, m=m):
            start = step * step_sources
            query = q_ref[pl.ds(start, step_sources), m].reshape(CHUNK, HD)
            total = early_ref[pl.ds(start, step_sources), m].reshape(CHUNK, 2 * HD)
            total += weighted(query, k_some, v_some, firsts[m], counts[m], None)
            summed = total[:, HD:]
            fine = (summed >= LEAST) & (summed <= MOST)
            result = (total[:, :HD] / summed).astype(jnp.bfloat16)
            o_ref[pl.ds(start, step_sources), m] = result.reshape(step_sources, per, HD)
            bad = jnp.where(fine, 0.0, 1.0)
            bad_ref[...] = jnp.maximum(bad_ref[...], jnp.max(bad.reshape(-1, 8, HD), axis=0))
            return carry

        lax.fori_loop(0, q_ref.shape[0] // step_sources, quick, 0)

    @pl.when(jnp.max(bad_ref[...]) > 0.0)
    def _():
        v_all[:, :, HD:] = jnp.ones((v_all.shape[0], keys, HD), jnp.bfloat16)
        for place, block in zip((OWN, ONE, TWO, EIGHT, SIXTEEN, THIRTYTWO), blocks):
            for m in range(2):
                for half in range(2):
                    rows = slice(half * half_keys, (half + 1) * half_keys)
                    k_all[place + m, rows, :] = block[half, 0, m]
                    v_all[place + m, rows, :HD] = block[half, 1, m]
        step_sources = SAFE_CHUNK // per

        def sums_of(slot, index):
            top = peak[...]
            shifted = s_all[slot] - jnp.concatenate([top] * (keys // HD), axis=1)
            return jnp.dot(
                jnp.exp2(shifted).astype(jnp.bfloat16),
                v_all[index],
                preferred_element_type=jnp.float32,
            )

        def widest(scores):
            return functools.reduce(
                jnp.maximum, [scores[:, at : at + HD] for at in range(0, keys, HD)]
            )

        for m in range(2):

            def chunk(step, carry, m=m):
                start = step * step_sources
                query = q_ref[pl.ds(start, step_sources), m].reshape(SAFE_CHUNK, HD)
                allowed = causal(start, SAFE_CHUNK, per, zh, half_keys)
                scores = jnp.where(allowed, scores_of(query, k_all[OWN + m]), -1e30)
                s_all[0] = scores
                peak[...] = widest(scores)
                for slot, index in enumerate(SOURCES[m]):

                    @pl.when(live_ref[m, slot] != 0)
                    def _(slot=slot, index=index):
                        scores = scores_of(query, k_all[index])
                        s_all[slot + 1] = scores
                        peak[...] = jnp.maximum(peak[...], widest(scores))

                top = jnp.max(peak[...], axis=1, keepdims=True)
                peak[...] = jnp.broadcast_to(top, (SAFE_CHUNK, HD))
                acc[...] = sums_of(0, OWN + m)
                for slot, index in enumerate(SOURCES[m]):

                    @pl.when(live_ref[m, slot] != 0)
                    def _(slot=slot, index=index):
                        acc[...] += sums_of(slot + 1, index)

                result = (acc[:, :HD] / acc[:, HD:]).astype(jnp.bfloat16)
                o_ref[pl.ds(start, step_sources), m] = result.reshape(step_sources, per, HD)
                return carry

            lax.fori_loop(0, q_ref.shape[0] // step_sources, chunk, 0)


def call(kernel, outputs, scratch, blocks, scalars, arrays):
    smem = pl.BlockSpec(memory_space=pltpu.SMEM)
    vmem = pl.BlockSpec(memory_space=pltpu.VMEM)
    rows = 4096
    return pl.pallas_call(
        kernel,
        out_shape=outputs,
        in_specs=[smem] * len(scalars) + [vmem] * len(arrays),
        out_specs=vmem,
        scratch_shapes=scratch,
        compiler_params=pltpu.CompilerParams(vmem_limit_bytes=44 * 1024 * 1024),
        cost_estimate=pl.CostEstimate(
            flops=int(rows * blocks * 256 * HD * 6),
            bytes_accessed=8 * 1024 * 1024,
            transcendentals=int(rows * blocks * 256),
        ),
    )(*scalars, *arrays)


def block_scratch(count, keys):
    return [
        pltpu.VMEM((count, HD, keys), jnp.bfloat16),
        pltpu.VMEM((count * keys, 2 * HD), jnp.bfloat16),
    ]


def attend_early(live, place, query, own):
    keys = 2 * own.shape[3]
    output = jax.ShapeDtypeStruct(query.shape[:3] + (2 * HD,), jnp.float32)
    return call(early_kernel, output, block_scratch(3, keys), 1.5, (live, place), (query, own))


def attend_late(live, place, query, early, *blocks):
    keys = 2 * blocks[0].shape[3]
    output = jax.ShapeDtypeStruct(query.shape, jnp.bfloat16)
    scratch = block_scratch(11, keys) + [
        pltpu.VMEM((12, keys, HD), jnp.bfloat16),
        pltpu.VMEM((12, keys, 2 * HD), jnp.bfloat16),
        pltpu.VMEM((SLOTS + 1, SAFE_CHUNK, keys), jnp.float32),
        pltpu.VMEM((SAFE_CHUNK, HD), jnp.float32),
        pltpu.VMEM((SAFE_CHUNK, 2 * HD), jnp.float32),
        pltpu.VMEM((8, HD), jnp.float32),
    ]
    return call(late_kernel, output, scratch, 5.5, (live, place), (query, early) + blocks)


def ring(value, by, keep=lambda h: True):
    pairs = [(z, (z + by) % 16) for z in range(16) if keep(z % 8)]
    return lax.ppermute(value, ("zh", "h"), pairs)


def along(value, by):
    return ring(value, by, lambda h: h + by < 8)


def across(value, by):
    pairs = []
    for x in range(4):
        for h in range(8):
            to = h + (x + by) // 4
            if to < 8:
                pairs.append((x * 8 + h, (x + by) % 4 * 8 + to))
    return lax.ppermute(value, ("x", "h"), pairs)


def local(queries, keys, values, links):
    resp, near, width = queries.shape
    groups = keys.shape[2] // HD
    repeat = width // keys.shape[2]
    x, zh, h = lax.axis_index("x"), lax.axis_index("zh"), lax.axis_index("h")

    with jax.named_scope("key_value_exchange"):
        pairs = jnp.stack([keys, values]).reshape(2, 4, 2, near, groups, HD)
        pairs = pairs.transpose(1, 4, 0, 2, 3, 5).reshape(4 * groups, 2, 2, near, HD)
        pairs = lax.all_to_all(pairs, PLANE, split_axis=0, concat_axis=0, tiled=True)
        pairs = pairs.transpose(1, 2, 0, 3, 4).reshape(2, 2, 4 * groups * near, HD)
    with jax.named_scope("other_half"):
        own = jnp.stack([pairs, ring(pairs, 8)])
    with jax.named_scope("query_exchange"):
        packed = queries.reshape(4, 2, near, groups, repeat, HD).transpose(0, 3, 1, 4, 2, 5)
        packed = packed.reshape(4 * groups, 2, repeat * near, HD)
        query = lax.all_to_all(packed, PLANE, split_axis=0, concat_axis=0, tiled=True)
    with jax.named_scope("key_value_spread"):
        thirtytwo = ring(own, -4, lambda h: h < 4)
        sixteen = along(own, 2)
        two = across(own, 2)
        one = across(own, 1)
        eight = along(own, 1)
    with jax.named_scope("attend"):
        place = jnp.stack([zh, x]).astype(jnp.int32)
        index = h * resp + 2 * x + jnp.arange(2)
        live = (links[index] != index[:, None]).astype(jnp.int32)
        early = attend_early(live, place, query, own)
        result = attend_late(live, place, query, early, own, one, two, eight, sixteen, thirtytwo)
    with jax.named_scope("return_exchange"):
        result = lax.all_to_all(result, PLANE, split_axis=0, concat_axis=0, tiled=True)
        result = result.reshape(4, groups, 2, repeat, near, HD).transpose(0, 2, 4, 1, 3, 5)
        return result.reshape(resp, near, width)


def solution(mesh):
    fine = Mesh(mesh.devices.reshape(4, 2, 4, 2, 8), ("x", "zh", "y", "c", "h"))
    placed = P("h", ("x", "zh", "y", "c"), None)
    return jax.shard_map(
        local, mesh=fine, in_specs=(placed, placed, placed, P()), out_specs=placed, check_vma=False
    )
```

time: 140 us -> 135 us (0.964)
  the two profiles are of different devices: /device:TPU:161 before, /device:TPU:449 now
where the time goes in v2:
time: 135 us; the launch traced here: 134 us
  Pallas kernels  37.8 us (28%)
  waiting for transfers between devices  37.3 us (28%)
  starting transfers between devices  28.5 us (21%)
  blocking collectives  21.2 us (16%)
  local copies, waits for them, and re-layouts  8.38 us (6%)
    pallas_call x2, Pallas kernels, call(): pl.pallas_call(kernel, out_shape=outputs, in_specs=[smem] * len(scalars)...  37.8 us
    all_to_all x1, blocking collectives, local(): lax.all_to_all(result, PLANE, split_axis=0, concat_axis=0, tiled=True)  21.2 us
    ppermute x4, waiting for transfers between devices, ring(): return lax.ppermute(value, ('zh', 'h'), pairs)  20.3 us
    ppermute x2, waiting for transfers between devices, across(): return lax.ppermute(value, ('x', 'h'), pairs)  13.8 us
    ppermute x4, starting transfers between devices, ring(): return lax.ppermute(value, ('zh', 'h'), pairs)  9.66 us
    all_to_all x1, starting transfers between devices, local(): lax.all_to_all(pairs, PLANE, split_axis=0, concat_axis=0, tiled=True)  7.76 us
    ppermute x2, starting transfers between devices, across(): return lax.ppermute(value, ('x', 'h'), pairs)  6.89 us
    reshape x2, local copies, waits for them, and re-layouts, local(): queries.reshape(4, 2, near, groups, repeat, HD).transpose(0, 3, 1, 4, 2, 5)  4.47 us
  transfers between devices with their start and end apart: 8, of which 6 were waited for; matrix products, arithmetic and copies ran while one was open for 4% of the time, Pallas kernels for 3%

profile of v2, /device:TPU:449, one launch (start us, length us, event | category | flops | bytes accessed | tf_op | source)
XLA Modules:
  0.0 134.3 jit_solution(7693725611009043358)
XLA Ops:
  0.0 0.9 stack.27
  0.9 0.9 stack.28
  1.8 0.7 pad_maximum_fusion.1
  2.6 7.8 %all-to-all-start.1 = ((bf16[32,2,2,4,128]{4,3,2,1,0:T(4,128)(2,1)}), bf16[32,2,2,4,128]{4,3,2,1,0:T(4,128)(2,1)S(1)}, u32[]{:S(2)}, u32[]{:S(2)}) async-start(bf16[32,2,2,4,128]{4,3,2,1,0:T(4,128)(2,1)} %bitcast.6), calls=%async_computation.1 | async-start | bytes 262144 | tf_op jit(solution)/shard_map/key_value_exchange/all_to_all | solution.py:258
  10.3 2.2 %reshape.44 = bf16[4,2,4,8,16,128]{5,4,3,2,1,0:T(8,128)(2,1)S(1)} reshape(bf16[8,4,16384]{2,1,0:T(4,128)(2,1)} %param.4) | data formatting | bytes 2097152 | tf_op jit(solution)/shard_map/query_exchange/reshape | solution.py:263
  12.5 2.3 %copy.10 = bf16[4,2,4,8,16,128]{5,2,4,1,3,0:T(4,128)(2,1)} copy(bf16[4,2,4,8,16,128]{5,4,3,2,1,0:T(8,128)(2,1)S(1)} %reshape.44) | data formatting | bytes 2097152 | tf_op jit(solution)/shard_map/query_exchange/reshape | solution.py:263
  14.8 3.2 %all-to-all-done.1 = bf16[32,2,2,4,128]{4,3,2,1,0:T(4,128)(2,1)S(1)} async-done(((bf16[32,2,2,4,128]{4,3,2,1,0:T(4,128)(2,1)}), bf16[32,2,2,4,128]{4,3,2,1,0:T(4,128)(2,1)S(1)}, u32[]{:S(2)}, u32[]{:S(2)}) %all-to-all-start.1) | async-done | bytes 131104 | tf_op jit(solution)/shard_map/key_value_exchange/all_to_all | solution.py:258
  18.0 4.2 %all-to-all-start = ((bf16[32,2,64,128]{3,2,1,0:T(8,128)(2,1)}), bf16[32,2,64,128]{3,2,1,0:T(8,128)(2,1)S(1)}, u32[]{:S(2)}, u32[]{:S(2)}) async-start(bf16[32,2,64,128]{3,2,1,0:T(8,128)(2,1)} %bitcast.4), calls=%async_computation | async-start | bytes 2097152 | tf_op jit(solution)/shard_map/query_exchange/all_to_all | solution.py:265
  22.3 5.2 %collective-permute-start = (bf16[2,2,128,128]{3,2,1,0:T(8,128)(2,1)S(1)}, bf16[2,2,128,128]{3,2,1,0:T(8,128)(2,1)S(1)}, u32[]{:S(2)}, u32[]{:S(2)}) collective-permute-start(bf16[2,2,128,128]{3,2,1,0:T(8,128)(2,1)S(1)} %bitcast.21), channel_id=1, source_target_pairs={{0,64},{1,65},{2,66},{3,67},{4,68},{5,69},{6,70},{7,71},{64,0},{65... | collective-permute-start | bytes 393224 | tf_op jit(solution)/shard_map/other_half/ppermute | solution.py:232
  27.6 0.6 gather_fusion
  28.1 18.0 %collective-permute-done = bf16[2,2,128,128]{3,2,1,0:T(8,128)(2,1)S(1)} collective-permute-done((bf16[2,2,128,128]{3,2,1,0:T(8,128)(2,1)S(1)}, bf16[2,2,128,128]{3,2,1,0:T(8,128)(2,1)S(1)}, u32[]{:S(2)}, u32[]{:S(2)}) %collective-permute-start) | collective-permute-done | bytes 131104 | tf_op jit(solution)/shard_map/other_half/ppermute | solution.py:232
  46.2 1.3 collective-permute-start.5
  47.5 1.3 collective-permute-start.4
  48.8 1.9 %collective-permute-start.3 = (bf16[2,2,2,128,128]{4,3,2,1,0:T(8,128)(2,1)S(1)}, bf16[2,2,2,128,128]{4,3,2,1,0:T(8,128)(2,1)S(1)}, u32[]{:S(2)}, u32[]{:S(2)}) collective-permute-start(bf16[2,2,2,128,128]{4,3,2,1,0:T(8,128)(2,1)S(1)} %pad_maximum_fusion.own.refs_0_), channel_id=1, source_target_pairs={{0,1},{1,2},{2,3},{3,4},{4,5},{5,6},{6,7},{64,65},{65,66},{66,67},... | collective-permute-start | bytes 786440 | tf_op jit(solution)/shard_map/key_value_spread/ppermute | solution.py:232
  50.7 4.7 %collective-permute-start.2 = (bf16[2,2,2,128,128]{4,3,2,1,0:T(8,128)(2,1)S(1)}, bf16[2,2,2,128,128]{4,3,2,1,0:T(8,128)(2,1)S(1)}, u32[]{:S(2)}, u32[]{:S(2)}) collective-permute-start(bf16[2,2,2,128,128]{4,3,2,1,0:T(8,128)(2,1)S(1)} %pad_maximum_fusion.own.refs_0_), channel_id=1, source_target_pairs={{0,256},{1,257},{2,258},{3,259},{4,260},{5,261},{6,262},{7,263},{1... | collective-permute-start | bytes 786440 | tf_op jit(solution)/shard_map/key_value_spread/ppermute | solution.py:246
  55.4 2.2 %collective-permute-start.1 = (bf16[2,2,2,128,128]{4,3,2,1,0:T(8,128)(2,1)S(1)}, bf16[2,2,2,128,128]{4,3,2,1,0:T(8,128)(2,1)S(1)}, u32[]{:S(2)}, u32[]{:S(2)}) collective-permute-start(bf16[2,2,2,128,128]{4,3,2,1,0:T(8,128)(2,1)S(1)} %pad_maximum_fusion.own.refs_0_), channel_id=1, source_target_pairs={{0,128},{1,129},{2,130},{3,131},{4,132},{5,133},{6,134},{7,135},{1... | collective-permute-start | bytes 786440 | tf_op jit(solution)/shard_map/key_value_spread/ppermute | solution.py:246
  57.8 4.4 %attend.2.early_ref = f32[32,2,64,256]{3,2,1,0:T(8,128)S(1)} custom-call(s32[2,6]{1,0:T(2,128)S(1)} %compare_convert_fusion.live_ref, s32[2]{0:T(128)S(1)} %pad_add_fusion.place_ref, bf16[32,2,64,128]{3,2,1,0:T(8,128)(2,1)S(1)} %all-to-all-done.q_ref, bf16[2,2,2,128,128]{4,3,2,1,0:T(8,128)(2,1)S(1)} %pad_maximum_fusion.own.refs_0_), custom_call_target="tpu_custom_call" | custom-call | flops 1207959552 | bytes 8388608 | tf_op jit(solution)/shard_map/attend/pallas_call | solution.py:188
  62.2 0.3 collective-permute-done.5.refs_5_
  62.5 1.9 %collective-permute-done.3.refs_3_ = bf16[2,2,2,128,128]{4,3,2,1,0:T(8,128)(2,1)S(1)} collective-permute-done((bf16[2,2,2,128,128]{4,3,2,1,0:T(8,128)(2,1)S(1)}, bf16[2,2,2,128,128]{4,3,2,1,0:T(8,128)(2,1)S(1)}, u32[]{:S(2)}, u32[]{:S(2)}) %collective-permute-start.3) | collective-permute-done | bytes 262176 | tf_op jit(solution)/shard_map/key_value_spread/ppermute | solution.py:232
  64.5 8.2 %collective-permute-done.2.refs_2_ = bf16[2,2,2,128,128]{4,3,2,1,0:T(8,128)(2,1)S(1)} collective-permute-done((bf16[2,2,2,128,128]{4,3,2,1,0:T(8,128)(2,1)S(1)}, bf16[2,2,2,128,128]{4,3,2,1,0:T(8,128)(2,1)S(1)}, u32[]{:S(2)}, u32[]{:S(2)}) %collective-permute-start.2) | collective-permute-done | bytes 262176 | tf_op jit(solution)/shard_map/key_value_spread/ppermute | solution.py:246
  72.7 5.6 %collective-permute-done.1.refs_1_ = bf16[2,2,2,128,128]{4,3,2,1,0:T(8,128)(2,1)S(1)} collective-permute-done((bf16[2,2,2,128,128]{4,3,2,1,0:T(8,128)(2,1)S(1)}, bf16[2,2,2,128,128]{4,3,2,1,0:T(8,128)(2,1)S(1)}, u32[]{:S(2)}, u32[]{:S(2)}) %collective-permute-start.1) | collective-permute-done | bytes 262176 | tf_op jit(solution)/shard_map/key_value_spread/ppermute | solution.py:246
  78.2 33.4 %attend.3 = bf16[32,2,64,128]{3,2,1,0:T(8,128)(2,1)S(1)} custom-call(s32[2,6]{1,0:T(2,128)S(1)} %compare_convert_fusion.live_ref, s32[2]{0:T(128)S(1)} %pad_add_fusion.place_ref, bf16[32,2,64,128]{3,2,1,0:T(8,128)(2,1)S(1)} %all-to-all-done.q_ref, f32[32,2,64,256]{3,2,1,0:T(8,128)S(1)} %attend.2.early_ref, ...), custom_call_target="tpu_custom_call" | custom-call | flops 4429185024 | bytes 8388608 | tf_op jit(solution)/shard_map/attend/pallas_call | solution.py:188
  111.7 21.2 %all_to_all.15 = bf16[32,2,64,128]{3,2,1,0:T(8,128)(2,1)S(1)} all-to-all(bf16[32,2,64,128]{3,2,1,0:T(8,128)(2,1)S(1)} %attend.3), channel_id=1, replica_groups=mesh['x'=4,'zh'=2,'y'=4,'c'=2,'h'=8] {'x','y','c'}, dimensions={0} | all-to-all | bytes 2097152 | tf_op jit(solution)/shard_map/return_exchange/all_to_all | solution.py:279
  133.1 1.1 reshape.50
  (15 shorter events, 0.6 us)
Async XLA Ops:
  0.0 27.5 %copy-start = (s32[64,6]{0,1:T(8,128)S(1)}, s32[64,6]{0,1:T(8,128)}, u32[]{:S(2)}) copy-start(s32[64,6]{0,1:T(8,128)} %param.7) | copy-start | bytes 4612
  2.6 15.5 %all-to-all-start.1 = ((bf16[32,2,2,4,128]{4,3,2,1,0:T(4,128)(2,1)}), bf16[32,2,2,4,128]{4,3,2,1,0:T(4,128)(2,1)S(1)}, u32[]{:S(2)}, u32[]{:S(2)}) async-start(bf16[32,2,2,4,128]{4,3,2,1,0:T(4,128)(2,1)} %bitcast.6), calls=%async_computation.1 | async-start | bytes 262144 | tf_op jit(solution)/shard_map/key_value_exchange/all_to_all | solution.py:258
  18.0 39.8 %all-to-all-start = ((bf16[32,2,64,128]{3,2,1,0:T(8,128)(2,1)}), bf16[32,2,64,128]{3,2,1,0:T(8,128)(2,1)S(1)}, u32[]{:S(2)}, u32[]{:S(2)}) async-start(bf16[32,2,64,128]{3,2,1,0:T(8,128)(2,1)} %bitcast.4), calls=%async_computation | async-start | bytes 2097152 | tf_op jit(solution)/shard_map/query_exchange/all_to_all | solution.py:265
  22.3 23.9 %collective-permute-start = (bf16[2,2,128,128]{3,2,1,0:T(8,128)(2,1)S(1)}, bf16[2,2,128,128]{3,2,1,0:T(8,128)(2,1)S(1)}, u32[]{:S(2)}, u32[]{:S(2)}) collective-permute-start(bf16[2,2,128,128]{3,2,1,0:T(8,128)(2,1)S(1)} %bitcast.21), channel_id=1, source_target_pairs={{0,64},{1,65},{2,66},{3,67},{4,68},{5,69},{6,70},{7,71},{64,0},{65... | collective-permute-start | bytes 393224 | tf_op jit(solution)/shard_map/other_half/ppermute | solution.py:232
  46.2 16.3 %collective-permute-start.5 = (bf16[2,2,2,128,128]{4,3,2,1,0:T(8,128)(2,1)S(1)}, bf16[2,2,2,128,128]{4,3,2,1,0:T(8,128)(2,1)S(1)}, u32[]{:S(2)}, u32[]{:S(2)}) collective-permute-start(bf16[2,2,2,128,128]{4,3,2,1,0:T(8,128)(2,1)S(1)} %pad_maximum_fusion.own.refs_0_), channel_id=1, source_target_pairs={{0,68},{1,69},{2,70},{3,71},{64,4},{65,5},{66,6},{67,7},{8,76},{9,... | collective-permute-start | bytes 786440 | tf_op jit(solution)/shard_map/key_value_spread/ppermute | solution.py:232
  47.5 15.0 %collective-permute-start.4 = (bf16[2,2,2,128,128]{4,3,2,1,0:T(8,128)(2,1)S(1)}, bf16[2,2,2,128,128]{4,3,2,1,0:T(8,128)(2,1)S(1)}, u32[]{:S(2)}, u32[]{:S(2)}) collective-permute-start(bf16[2,2,2,128,128]{4,3,2,1,0:T(8,128)(2,1)S(1)} %pad_maximum_fusion.own.refs_0_), channel_id=1, source_target_pairs={{0,2},{1,3},{2,4},{3,5},{4,6},{5,7},{64,66},{65,67},{66,68},{67,69... | collective-permute-start | bytes 786440 | tf_op jit(solution)/shard_map/key_value_spread/ppermute | solution.py:232
  48.8 15.7 %collective-permute-start.3 = (bf16[2,2,2,128,128]{4,3,2,1,0:T(8,128)(2,1)S(1)}, bf16[2,2,2,128,128]{4,3,2,1,0:T(8,128)(2,1)S(1)}, u32[]{:S(2)}, u32[]{:S(2)}) collective-permute-start(bf16[2,2,2,128,128]{4,3,2,1,0:T(8,128)(2,1)S(1)} %pad_maximum_fusion.own.refs_0_), channel_id=1, source_target_pairs={{0,1},{1,2},{2,3},{3,4},{4,5},{5,6},{6,7},{64,65},{65,66},{66,67},... | collective-permute-start | bytes 786440 | tf_op jit(solution)/shard_map/key_value_spread/ppermute | solution.py:232
  50.7 21.9 %collective-permute-start.2 = (bf16[2,2,2,128,128]{4,3,2,1,0:T(8,128)(2,1)S(1)}, bf16[2,2,2,128,128]{4,3,2,1,0:T(8,128)(2,1)S(1)}, u32[]{:S(2)}, u32[]{:S(2)}) collective-permute-start(bf16[2,2,2,128,128]{4,3,2,1,0:T(8,128)(2,1)S(1)} %pad_maximum_fusion.own.refs_0_), channel_id=1, source_target_pairs={{0,256},{1,257},{2,258},{3,259},{4,260},{5,261},{6,262},{7,263},{1... | collective-permute-start | bytes 786440 | tf_op jit(solution)/shard_map/key_value_spread/ppermute | solution.py:246
  55.4 22.8 %collective-permute-start.1 = (bf16[2,2,2,128,128]{4,3,2,1,0:T(8,128)(2,1)S(1)}, bf16[2,2,2,128,128]{4,3,2,1,0:T(8,128)(2,1)S(1)}, u32[]{:S(2)}, u32[]{:S(2)}) collective-permute-start(bf16[2,2,2,128,128]{4,3,2,1,0:T(8,128)(2,1)S(1)} %pad_maximum_fusion.own.refs_0_), channel_id=1, source_target_pairs={{0,128},{1,129},{2,130},{3,131},{4,132},{5,133},{6,134},{7,135},{1... | collective-permute-start | bytes 786440 | tf_op jit(solution)/shard_map/key_value_spread/ppermute | solution.py:246

commit v3 on v2

--- a/solution.py
+++ b/solution.py
@@ -27,11 +27,8 @@
     return lax.dot_general(query, key_block, dims, preferred_element_type=jnp.float32) * FACTOR
 
 
-def causal(start, count, per, zh, half_keys):
-    key = lax.broadcasted_iota(jnp.int32, (1, 2 * half_keys), 1)
-    inner = key % half_keys
-    key_half = jnp.where(key < half_keys, zh, 1 - zh)
-    key_pos = (inner // 32) * 64 + key_half * 32 + inner % 32
+def causal(start, count, per, zh, keys):
+    key_pos = lax.broadcasted_iota(jnp.int32, (1, keys), 1)
     row = lax.broadcasted_iota(jnp.int32, (count, 1), 0)
     source = start + row // per
     query_pos = (source // 8) * 64 + zh * 32 + (source % 8) * 4 + row % 4
@@ -39,20 +36,17 @@
 
 
 def place_block(k_some, v_some, at, block, m, live):
-    half_keys = block.shape[3]
-    keys = 2 * half_keys
-    for half in range(2):
-        columns = slice(half * half_keys, (half + 1) * half_keys)
-        k_some[at, :, columns] = block[half, 0, m].T
-        rows = slice(at * keys + half * half_keys, at * keys + (half + 1) * half_keys)
-        ones = jnp.ones((half_keys, HD), jnp.bfloat16)
-        value_block = block[half, 1, m]
-        if live is not None:
-            alive = jnp.where(live != 0, 1.0, 0.0) > 0
-            value_block = jnp.where(alive, value_block, jnp.zeros_like(value_block))
-            ones = jnp.where(alive, ones, jnp.zeros_like(ones))
-        v_some[rows, :HD] = value_block
-        v_some[rows, HD:] = ones
+    keys = block.shape[2]
+    k_some[at] = block[0, m].T
+    rows = slice(at * keys, (at + 1) * keys)
+    ones = jnp.ones((keys, HD), jnp.bfloat16)
+    value_block = block[1, m]
+    if live is not None:
+        alive = jnp.where(live != 0, 1.0, 0.0) > 0
+        value_block = jnp.where(alive, value_block, jnp.zeros_like(value_block))
+        ones = jnp.where(alive, ones, jnp.zeros_like(ones))
+    v_some[rows, :HD] = value_block
+    v_some[rows, HD:] = ones
 
 
 def weighted(query, k_some, v_some, first, count, allowed):
@@ -68,11 +62,13 @@
     return jnp.dot(jnp.concatenate(parts, axis=1), values, preferred_element_type=jnp.float32)
 
 
-def early_kernel(live_ref, place_ref, q_ref, own, o_ref, k_some, v_some):
-    zh = place_ref[0]
+def prepare_kernel(live_ref, own, k_some, v_some):
     place_block(k_some, v_some, 0, own, 0, None)
     place_block(k_some, v_some, 1, own, 1, None)
     place_block(k_some, v_some, 2, own, 0, live_ref[1, 0])
+
+
+def early_kernel(place_ref, q_ref, k_some, v_some, o_ref):
     per = q_ref.shape[2]
     step_sources = CHUNK // per
     for m in range(2):
@@ -80,8 +76,27 @@
         def chunk(step, carry, m=m):
             start = step * step_sources
             query = q_ref[pl.ds(start, step_sources), m].reshape(CHUNK, HD)
-            allowed = causal(start, CHUNK, per, zh, own.shape[3])
+            allowed = causal(start, CHUNK, per, place_ref[0], k_some.shape[2])
             total = weighted(query, k_some, v_some, m, 1 + m, allowed)
+            o_ref[pl.ds(start, step_sources), m] = total.reshape(step_sources, per, 2 * HD)
+            return carry
+
+        lax.fori_loop(0, q_ref.shape[0] // step_sources, chunk, 0)
+
+
+def middle_kernel(live_ref, q_ref, early_ref, eight, sixteen, o_ref, k_some, v_some):
+    per = q_ref.shape[2]
+    step_sources = CHUNK // per
+    for m in range(2):
+        place_block(k_some, v_some, 2 * m, eight, m, live_ref[m, 3])
+        place_block(k_some, v_some, 2 * m + 1, sixteen, m, live_ref[m, 4])
+    for m in range(2):
+
+        def chunk(step, carry, m=m):
+            start = step * step_sources
+            query = q_ref[pl.ds(start, step_sources), m].reshape(CHUNK, HD)
+            total = early_ref[pl.ds(start, step_sources), m].reshape(CHUNK, 2 * HD)
+            total += weighted(query, k_some, v_some, 2 * m, 2, None)
             o_ref[pl.ds(start, step_sources), m] = total.reshape(step_sources, per, 2 * HD)
             return carry
 
@@ -93,12 +108,11 @@
     o_ref, k_some, v_some, k_all, v_all, s_all, peak, acc, bad_ref = refs[6:]
     own, one, two, eight, sixteen, thirtytwo = blocks
     zh = place_ref[0]
-    half_keys = own.shape[3]
-    keys = 2 * half_keys
+    keys = own.shape[2]
     per = q_ref.shape[2]
-    firsts, counts = (0, 6), (6, 5)
-    for m in range(2):
-        sets = [(one, 1, m), (two, m, 2), (eight, m, 3), (sixteen, m, 4), (thirtytwo, m, 5)]
+    firsts, counts = (0, 4), (4, 3)
+    for m in range(2):
+        sets = [(one, 1, m), (two, m, 2), (thirtytwo, m, 5)]
         if m == 0:
             sets.append((one, 0, 1))
         for at, (block, which, slot) in enumerate(sets):
@@ -128,10 +142,8 @@
         v_all[:, :, HD:] = jnp.ones((v_all.shape[0], keys, HD), jnp.bfloat16)
         for place, block in zip((OWN, ONE, TWO, EIGHT, SIXTEEN, THIRTYTWO), blocks):
             for m in range(2):
-                for half in range(2):
-                    rows = slice(half * half_keys, (half + 1) * half_keys)
-                    k_all[place + m, rows, :] = block[half, 0, m]
-                    v_all[place + m, rows, :HD] = block[half, 1, m]
+                k_all[place + m] = block[0, m]
+                v_all[place + m, :, :HD] = block[1, m]
         step_sources = SAFE_CHUNK // per
 
         def sums_of(slot, index):
@@ -153,7 +165,7 @@
             def chunk(step, carry, m=m):
                 start = step * step_sources
                 query = q_ref[pl.ds(start, step_sources), m].reshape(SAFE_CHUNK, HD)
-                allowed = causal(start, SAFE_CHUNK, per, zh, half_keys)
+                allowed = causal(start, SAFE_CHUNK, per, zh, keys)
                 scores = jnp.where(allowed, scores_of(query, k_all[OWN + m]), -1e30)
                 s_all[0] = scores
                 peak[...] = widest(scores)
@@ -181,42 +193,49 @@
             lax.fori_loop(0, q_ref.shape[0] // step_sources, chunk, 0)
 
 
-def call(kernel, outputs, scratch, blocks, scalars, arrays):
+def call(kernel, outputs, scratch, flops, scalars, arrays):
     smem = pl.BlockSpec(memory_space=pltpu.SMEM)
     vmem = pl.BlockSpec(memory_space=pltpu.VMEM)
-    rows = 4096
     return pl.pallas_call(
         kernel,
         out_shape=outputs,
         in_specs=[smem] * len(scalars) + [vmem] * len(arrays),
-        out_specs=vmem,
+        out_specs=jax.tree.map(lambda _: vmem, outputs),
         scratch_shapes=scratch,
         compiler_params=pltpu.CompilerParams(vmem_limit_bytes=44 * 1024 * 1024),
-        cost_estimate=pl.CostEstimate(
-            flops=int(rows * blocks * 256 * HD * 6),
-            bytes_accessed=8 * 1024 * 1024,
-            transcendentals=int(rows * blocks * 256),
-        ),
+        cost_estimate=pl.CostEstimate(flops=flops, bytes_accessed=2**20, transcendentals=0),
     )(*scalars, *arrays)
 
 
+def block_shapes(count, keys):
+    return [(count, HD, keys), (count * keys, 2 * HD)]
+
+
 def block_scratch(count, keys):
-    return [
-        pltpu.VMEM((count, HD, keys), jnp.bfloat16),
-        pltpu.VMEM((count * keys, 2 * HD), jnp.bfloat16),
-    ]
-
-
-def attend_early(live, place, query, own):
-    keys = 2 * own.shape[3]
+    return [pltpu.VMEM(shape, jnp.bfloat16) for shape in block_shapes(count, keys)]
+
+
+def attend_prepare(live, own):
+    keys = own.shape[2]
+    outputs = [jax.ShapeDtypeStruct(shape, jnp.bfloat16) for shape in block_shapes(3, keys)]
+    return call(prepare_kernel, outputs, [], 30 * 10**9, (live,), (own,))
+
+
+def attend_early(place, query, keys_own, values_own):
     output = jax.ShapeDtypeStruct(query.shape[:3] + (2 * HD,), jnp.float32)
-    return call(early_kernel, output, block_scratch(3, keys), 1.5, (live, place), (query, own))
+    return call(early_kernel, output, [], 4 * 10**9, (place,), (query, keys_own, values_own))
+
+
+def attend_middle(live, query, early, eight, sixteen):
+    output = jax.ShapeDtypeStruct(early.shape, jnp.float32)
+    scratch = block_scratch(4, eight.shape[2])
+    return call(middle_kernel, output, scratch, 4 * 10**9, (live,), (query, early, eight, sixteen))
 
 
 def attend_late(live, place, query, early, *blocks):
-    keys = 2 * blocks[0].shape[3]
+    keys = blocks[0].shape[2]
     output = jax.ShapeDtypeStruct(query.shape, jnp.bfloat16)
-    scratch = block_scratch(11, keys) + [
+    scratch = block_scratch(7, keys) + [
         pltpu.VMEM((12, keys, HD), jnp.bfloat16),
         pltpu.VMEM((12, keys, 2 * HD), jnp.bfloat16),
         pltpu.VMEM((SLOTS + 1, SAFE_CHUNK, keys), jnp.float32),
@@ -224,7 +243,7 @@
         pltpu.VMEM((SAFE_CHUNK, 2 * HD), jnp.float32),
         pltpu.VMEM((8, HD), jnp.float32),
     ]
-    return call(late_kernel, output, scratch, 5.5, (live, place), (query, early) + blocks)
+    return call(late_kernel, output, scratch, 6 * 10**9, (live, place), (query, early) + blocks)
 
 
 def ring(value, by, keep=lambda h: True):
@@ -237,13 +256,7 @@
 
 
 def across(value, by):
-    pairs = []
-    for x in range(4):
-        for h in range(8):
-            to = h + (x + by) // 4
-            if to < 8:
-                pairs.append((x * 8 + h, (x + by) % 4 * 8 + to))
-    return lax.ppermute(value, ("x", "h"), pairs)
+    return lax.ppermute(value, "x", [(x, (x + by) % 4) for x in range(4)])
 
 
 def local(queries, keys, values, links):
@@ -253,27 +266,28 @@
     x, zh, h = lax.axis_index("x"), lax.axis_index("zh"), lax.axis_index("h")
 
     with jax.named_scope("key_value_exchange"):
-        pairs = jnp.stack([keys, values]).reshape(2, 4, 2, near, groups, HD)
-        pairs = pairs.transpose(1, 4, 0, 2, 3, 5).reshape(4 * groups, 2, 2, near, HD)
-        pairs = lax.all_to_all(pairs, PLANE, split_axis=0, concat_axis=0, tiled=True)
-        pairs = pairs.transpose(1, 2, 0, 3, 4).reshape(2, 2, 4 * groups * near, HD)
-    with jax.named_scope("other_half"):
-        own = jnp.stack([pairs, ring(pairs, 8)])
+        own = jnp.stack([keys, values]).reshape(2, 4, 2, near, groups, HD).transpose(1, 4, 0, 2, 3, 5)
+        own = jnp.broadcast_to(own[:, None], (4, 2, groups, 2, 2, near, HD))
+        own = own.reshape(8 * groups, 2, 2, near, HD)
+        own = lax.all_to_all(own, ("x", "zh", "y", "c"), split_axis=0, concat_axis=0, tiled=True)
+        own = own.transpose(1, 2, 0, 3, 4).reshape(2, 2, 8 * groups * near, HD)
     with jax.named_scope("query_exchange"):
         packed = queries.reshape(4, 2, near, groups, repeat, HD).transpose(0, 3, 1, 4, 2, 5)
         packed = packed.reshape(4 * groups, 2, repeat * near, HD)
         query = lax.all_to_all(packed, PLANE, split_axis=0, concat_axis=0, tiled=True)
+    place = zh.astype(jnp.int32).reshape(1)
+    index = h * resp + 2 * x + jnp.arange(2)
+    live = (links[index] != index[:, None]).astype(jnp.int32)
     with jax.named_scope("key_value_spread"):
+        eight = along(own, 1)
         thirtytwo = ring(own, -4, lambda h: h < 4)
         sixteen = along(own, 2)
-        two = across(own, 2)
-        one = across(own, 1)
-        eight = along(own, 1)
+        two = across(jnp.where(x >= 2, eight, own), 2)
+        one = across(jnp.where(x >= 3, eight, own), 1)
     with jax.named_scope("attend"):
-        place = jnp.stack([zh, x]).astype(jnp.int32)
-        index = h * resp + 2 * x + jnp.arange(2)
-        live = (links[index] != index[:, None]).astype(jnp.int32)
-        early = attend_early(live, place, query, own)
+        query, eight = lax.optimization_barrier((query, eight))
+        early = attend_early(place, query, *attend_prepare(live, own))
+        early = attend_middle(live, query, early, eight, sixteen)
         result = attend_late(live, place, query, early, own, one, two, eight, sixteen, thirtytwo)
     with jax.named_scope("return_exchange"):
         result = lax.all_to_all(result, PLANE, split_axis=0, concat_axis=0, tiled=True)

time: 135 us -> 133 us (0.985)
  the two profiles are of different devices: /device:TPU:449 before, /device:TPU:385 now
where the time goes in v3:
time: 133 us; the launch traced here: 132 us
  starting transfers between devices  37 us (28%)
  Pallas kernels  33.3 us (25%)
  blocking collectives  27.4 us (21%)
  waiting for transfers between devices  24.6 us (18%)
  local copies, waits for them, and re-layouts  9.86 us (7%)
    pallas_call x4, Pallas kernels, call(): pl.pallas_call(kernel, out_shape=outputs, in_specs=[smem] * len(scalars)...  33.3 us
    all_to_all x1, blocking collectives, local(): lax.all_to_all(result, PLANE, split_axis=0, concat_axis=0, tiled=True)  27.4 us
    all_to_all x1, starting transfers between devices, local(): lax.all_to_all(own, ('x', 'zh', 'y', 'c'), split_axis=0, concat_axis=0, t...  18 us
    ppermute x3, waiting for transfers between devices, ring(): return lax.ppermute(value, ('zh', 'h'), pairs)  9.28 us
    ppermute x3, starting transfers between devices, ring(): return lax.ppermute(value, ('zh', 'h'), pairs)  9.04 us
    all_to_all x1, waiting for transfers between devices, local(): lax.all_to_all(own, ('x', 'zh', 'y', 'c'), split_axis=0, concat_axis=0, t...  8.17 us
    all_to_all x1, waiting for transfers between devices, local(): lax.all_to_all(packed, PLANE, split_axis=0, concat_axis=0, tiled=True)  7.11 us
    ppermute x2, starting transfers between devices, across(): return lax.ppermute(value, 'x', [(x, (x + by) % 4) for x in range(4)])  5.74 us
  transfers between devices with their start and end apart: 7, of which 3 were waited for; matrix products, arithmetic and copies ran while one was open for 5% of the time, Pallas kernels for 6%

profile of v3, /device:TPU:385, one launch (start us, length us, event | category | flops | bytes accessed | tf_op | source)
XLA Modules:
  0.0 132.3 jit_solution(1957617152525391456)
XLA Ops:
  0.0 0.9 stack.10
  0.9 0.9 stack.9
  1.8 0.8 broadcast_in_dim.2
  2.6 18.0 %all-to-all-start.1 = ((bf16[64,2,2,4,128]{4,3,2,1,0:T(4,128)(2,1)}), bf16[64,2,2,4,128]{4,3,2,1,0:T(4,128)(2,1)S(1)}, u32[]{:S(2)}, u32[]{:S(2)}) async-start(bf16[64,2,2,4,128]{4,3,2,1,0:T(4,128)(2,1)} %bitcast.5), calls=%async_computation.1 | async-start | bytes 524288 | tf_op jit(solution)/shard_map/key_value_exchange/all_to_all | solution.py:272
  20.6 0.8 copy.9
  21.4 2.1 %reshape.46 = bf16[4,2,4,8,16,128]{5,4,3,2,1,0:T(8,128)(2,1)S(1)} reshape(bf16[8,4,16384]{2,1,0:T(4,128)(2,1)} %param.4) | data formatting | bytes 2097152 | tf_op jit(solution)/shard_map/query_exchange/reshape | solution.py:275
  23.5 2.3 %copy.10 = bf16[4,2,4,8,16,128]{5,2,4,1,3,0:T(4,128)(2,1)} copy(bf16[4,2,4,8,16,128]{5,4,3,2,1,0:T(8,128)(2,1)S(1)} %reshape.46) | data formatting | bytes 2097152 | tf_op jit(solution)/shard_map/query_exchange/reshape | solution.py:275
  25.9 0.6 gather_fusion
  26.5 8.2 %all-to-all-done.1 = bf16[64,2,2,4,128]{4,3,2,1,0:T(4,128)(2,1)S(1)} async-done(((bf16[64,2,2,4,128]{4,3,2,1,0:T(4,128)(2,1)}), bf16[64,2,2,4,128]{4,3,2,1,0:T(4,128)(2,1)S(1)}, u32[]{:S(2)}, u32[]{:S(2)}) %all-to-all-start.1) | async-done | bytes 262176 | tf_op jit(solution)/shard_map/key_value_exchange/all_to_all | solution.py:272
  34.7 4.2 %all-to-all-start = ((bf16[32,2,64,128]{3,2,1,0:T(8,128)(2,1)}), bf16[32,2,64,128]{3,2,1,0:T(8,128)(2,1)S(1)}, u32[]{:S(2)}, u32[]{:S(2)}) async-start(bf16[32,2,64,128]{3,2,1,0:T(8,128)(2,1)} %bitcast.3), calls=%async_computation | async-start | bytes 2097152 | tf_op jit(solution)/shard_map/query_exchange/all_to_all | solution.py:277
  39.0 1.9 %collective-permute-start = (bf16[2,2,256,128]{3,2,1,0:T(8,128)(2,1)S(1)}, bf16[2,2,256,128]{3,2,1,0:T(8,128)(2,1)S(1)}, u32[]{:S(2)}, u32[]{:S(2)}) collective-permute-start(bf16[2,2,256,128]{3,2,1,0:T(8,128)(2,1)S(1)} %bitcast.16), channel_id=1, source_target_pairs={{0,1},{1,2},{2,3},{3,4},{4,5},{5,6},{6,7},{64,65},{65,66},{66,67},... | collective-permute-start | bytes 786440 | tf_op jit(solution)/shard_map/key_value_spread/ppermute | solution.py:251
  40.9 5.8 %collective-permute-start.1 = (bf16[2,2,256,128]{3,2,1,0:T(8,128)(2,1)S(1)}, bf16[2,2,256,128]{3,2,1,0:T(8,128)(2,1)S(1)}, u32[]{:S(2)}, u32[]{:S(2)}) collective-permute-start(bf16[2,2,256,128]{3,2,1,0:T(8,128)(2,1)S(1)} %bitcast.17), channel_id=1, source_target_pairs={{0,2},{1,3},{2,4},{3,5},{4,6},{5,7},{64,66},{65,67},{66,68},{67,69... | collective-permute-start | bytes 786440 | tf_op jit(solution)/shard_map/key_value_spread/ppermute | solution.py:251
  46.8 1.3 collective-permute-start.4
  48.1 0.7 attend.4
  48.7 7.1 %all-to-all-done.q_ref = bf16[32,2,64,128]{3,2,1,0:T(8,128)(2,1)S(1)} async-done(((bf16[32,2,64,128]{3,2,1,0:T(8,128)(2,1)}), bf16[32,2,64,128]{3,2,1,0:T(8,128)(2,1)S(1)}, u32[]{:S(2)}, u32[]{:S(2)}) %all-to-all-start) | async-done | bytes 1048608 | tf_op jit(solution)/shard_map/query_exchange/all_to_all | solution.py:277
  55.9 1.9 %collective-permute-start.2 = (bf16[2,2,256,128]{3,2,1,0:T(8,128)(2,1)S(1)}, bf16[2,2,256,128]{3,2,1,0:T(8,128)(2,1)S(1)}, u32[]{:S(2)}, u32[]{:S(2)}) collective-permute-start(bf16[2,2,256,128]{3,2,1,0:T(8,128)(2,1)S(1)} %get-tuple-element.14), channel_id=1, source_target_pairs={{0,128},{128,256},{256,384},{384,0},{1,129},{129,257},{257,385},{3... | collective-permute-start | bytes 786440 | tf_op jit(solution)/shard_map/key_value_spread/ppermute | solution.py:259
  57.8 3.8 %collective-permute-start.3 = (bf16[2,2,256,128]{3,2,1,0:T(8,128)(2,1)S(1)}, bf16[2,2,256,128]{3,2,1,0:T(8,128)(2,1)S(1)}, u32[]{:S(2)}, u32[]{:S(2)}) collective-permute-start(bf16[2,2,256,128]{3,2,1,0:T(8,128)(2,1)S(1)} %get-tuple-element.13), channel_id=1, source_target_pairs={{0,256},{128,384},{256,0},{384,128},{1,257},{129,385},{257,1},{385... | collective-permute-start | bytes 786440 | tf_op jit(solution)/shard_map/key_value_spread/ppermute | solution.py:259
  61.6 3.8 %attend.5.early_ref = f32[32,2,64,256]{3,2,1,0:T(8,128)S(1)} custom-call(s32[1]{0:T(128)} %bitcast.1.place_ref, bf16[32,2,64,128]{3,2,1,0:T(8,128)(2,1)S(1)} %all-to-all-done.q_ref, bf16[3,128,256]{2,1,0:T(8,128)(2,1)S(1)} %get-tuple-element.10.k_some, bf16[768,256]{1,0:T(8,128)(2,1)S(1)} %get-tuple-element.11.v_some), custom_call_target="tpu_custom_call" | custom-call | flops 4000000000 | bytes 1048576 | tf_op jit(solution)/shard_map/attend/pallas_call | solution.py:199
  65.5 3.5 %attend.6.early_ref = f32[32,2,64,256]{3,2,1,0:T(8,128)S(1)} custom-call(s32[2,6]{1,0:T(2,128)S(1)} %compare_convert_fusion.live_ref, bf16[32,2,64,128]{3,2,1,0:T(8,128)(2,1)S(1)} %all-to-all-done.q_ref, f32[32,2,64,256]{3,2,1,0:T(8,128)S(1)} %attend.5.early_ref, bf16[2,2,256,128]{3,2,1,0:T(8,128)(2,1)S(1)} %collective-permute-done.eight.refs_3_, ...), custom_call_target="tpu_custom_call" | custom-call | flops 4000000000 | bytes 1048576 | tf_op jit(solution)/shard_map/attend/pallas_call | solution.py:199
  69.0 9.3 %collective-permute-done.4.refs_5_ = bf16[2,2,256,128]{3,2,1,0:T(8,128)(2,1)S(1)} collective-permute-done((bf16[2,2,256,128]{3,2,1,0:T(8,128)(2,1)S(1)}, bf16[2,2,256,128]{3,2,1,0:T(8,128)(2,1)S(1)}, u32[]{:S(2)}, u32[]{:S(2)}) %collective-permute-start.4) | collective-permute-done | bytes 262176 | tf_op jit(solution)/shard_map/key_value_spread/ppermute | solution.py:251
  78.3 25.3 %attend.7 = bf16[32,2,64,128]{3,2,1,0:T(8,128)(2,1)S(1)} custom-call(s32[2,6]{1,0:T(2,128)S(1)} %compare_convert_fusion.live_ref, s32[1]{0:T(128)} %bitcast.1.place_ref, bf16[32,2,64,128]{3,2,1,0:T(8,128)(2,1)S(1)} %all-to-all-done.q_ref, f32[32,2,64,256]{3,2,1,0:T(8,128)S(1)} %attend.6.early_ref, bf16[2,2,256,128]{3,2,1,0:T(8,128)(2,1)S(1)} %bitcast.21, ...), custom_call_target="tpu_custom_call" | custom-call | flops 6000000000 | bytes 1048576 | tf_op jit(solution)/shard_map/attend/pallas_call | solution.py:199
  103.5 27.4 %all_to_all.15 = bf16[32,2,64,128]{3,2,1,0:T(8,128)(2,1)S(1)} all-to-all(bf16[32,2,64,128]{3,2,1,0:T(8,128)(2,1)S(1)} %attend.7), channel_id=1, replica_groups=mesh['x'=4,'zh'=2,'y'=4,'c'=2,'h'=8] {'x','y','c'}, dimensions={0} | all-to-all | bytes 2097152 | tf_op jit(solution)/shard_map/return_exchange/all_to_all | solution.py:293
  130.9 0.2 copy.13
  131.2 1.1 reshape.51
  (12 shorter events, 0.3 us)
Async XLA Ops:
  2.6 32.1 %all-to-all-start.1 = ((bf16[64,2,2,4,128]{4,3,2,1,0:T(4,128)(2,1)}), bf16[64,2,2,4,128]{4,3,2,1,0:T(4,128)(2,1)S(1)}, u32[]{:S(2)}, u32[]{:S(2)}) async-start(bf16[64,2,2,4,128]{4,3,2,1,0:T(4,128)(2,1)} %bitcast.5), calls=%async_computation.1 | async-start | bytes 524288 | tf_op jit(solution)/shard_map/key_value_exchange/all_to_all | solution.py:272
  34.7 21.2 %all-to-all-start = ((bf16[32,2,64,128]{3,2,1,0:T(8,128)(2,1)}), bf16[32,2,64,128]{3,2,1,0:T(8,128)(2,1)S(1)}, u32[]{:S(2)}, u32[]{:S(2)}) async-start(bf16[32,2,64,128]{3,2,1,0:T(8,128)(2,1)} %bitcast.3), calls=%async_computation | async-start | bytes 2097152 | tf_op jit(solution)/shard_map/query_exchange/all_to_all | solution.py:277
  39.0 16.8 %collective-permute-start = (bf16[2,2,256,128]{3,2,1,0:T(8,128)(2,1)S(1)}, bf16[2,2,256,128]{3,2,1,0:T(8,128)(2,1)S(1)}, u32[]{:S(2)}, u32[]{:S(2)}) collective-permute-start(bf16[2,2,256,128]{3,2,1,0:T(8,128)(2,1)S(1)} %bitcast.16), channel_id=1, source_target_pairs={{0,1},{1,2},{2,3},{3,4},{4,5},{5,6},{6,7},{64,65},{65,66},{66,67},... | collective-permute-start | bytes 786440 | tf_op jit(solution)/shard_map/key_value_spread/ppermute | solution.py:251
  40.9 24.5 %collective-permute-start.1 = (bf16[2,2,256,128]{3,2,1,0:T(8,128)(2,1)S(1)}, bf16[2,2,256,128]{3,2,1,0:T(8,128)(2,1)S(1)}, u32[]{:S(2)}, u32[]{:S(2)}) collective-permute-start(bf16[2,2,256,128]{3,2,1,0:T(8,128)(2,1)S(1)} %bitcast.17), channel_id=1, source_target_pairs={{0,2},{1,3},{2,4},{3,5},{4,6},{5,7},{64,66},{65,67},{66,68},{67,69... | collective-permute-start | bytes 786440 | tf_op jit(solution)/shard_map/key_value_spread/ppermute | solution.py:251
  46.8 31.5 %collective-permute-start.4 = (bf16[2,2,256,128]{3,2,1,0:T(8,128)(2,1)S(1)}, bf16[2,2,256,128]{3,2,1,0:T(8,128)(2,1)S(1)}, u32[]{:S(2)}, u32[]{:S(2)}) collective-permute-start(bf16[2,2,256,128]{3,2,1,0:T(8,128)(2,1)S(1)} %bitcast.18), channel_id=1, source_target_pairs={{0,68},{1,69},{2,70},{3,71},{64,4},{65,5},{66,6},{67,7},{8,76},{9,... | collective-permute-start | bytes 786440 | tf_op jit(solution)/shard_map/key_value_spread/ppermute | solution.py:251
  55.9 22.4 %collective-permute-start.2 = (bf16[2,2,256,128]{3,2,1,0:T(8,128)(2,1)S(1)}, bf16[2,2,256,128]{3,2,1,0:T(8,128)(2,1)S(1)}, u32[]{:S(2)}, u32[]{:S(2)}) collective-permute-start(bf16[2,2,256,128]{3,2,1,0:T(8,128)(2,1)S(1)} %get-tuple-element.14), channel_id=1, source_target_pairs={{0,128},{128,256},{256,384},{384,0},{1,129},{129,257},{257,385},{3... | collective-permute-start | bytes 786440 | tf_op jit(solution)/shard_map/key_value_spread/ppermute | solution.py:259
  57.8 20.4 %collective-permute-start.3 = (bf16[2,2,256,128]{3,2,1,0:T(8,128)(2,1)S(1)}, bf16[2,2,256,128]{3,2,1,0:T(8,128)(2,1)S(1)}, u32[]{:S(2)}, u32[]{:S(2)}) collective-permute-start(bf16[2,2,256,128]{3,2,1,0:T(8,128)(2,1)S(1)} %get-tuple-element.13), channel_id=1, source_target_pairs={{0,256},{128,384},{256,0},{384,128},{1,257},{129,385},{257,1},{385... | collective-permute-start | bytes 786440 | tf_op jit(solution)/shard_map/key_value_spread/ppermute | solution.py:259

commit v4 on v3

v4 whole, which is shorter than its diff:
```python
import functools
import math

import jax
import jax.numpy as jnp
from jax import lax
from jax.experimental import pallas as pl
from jax.experimental.pallas import tpu as pltpu
from jax.sharding import Mesh, PartitionSpec as P

HD = 128
SLOTS = 6
FACTOR = HD ** (-0.5) * math.log2(math.e)
CHUNK = 2048
SAFE_CHUNK = 512
LEAST, MOST = 2.0**-60, 2.0**60
PLANE = ("x", "y", "c")
OWN, ONE, TWO, EIGHT, SIXTEEN, THIRTYTWO = 0, 2, 4, 6, 8, 10
SOURCES = (
    (ONE + 1, ONE, TWO, EIGHT, SIXTEEN, THIRTYTWO),
    (OWN, ONE + 1, TWO + 1, EIGHT + 1, SIXTEEN + 1, THIRTYTWO + 1),
)


def scores_of(query, key_block):
    dims = (((1,), (1,)), ((), ()))
    return lax.dot_general(query, key_block, dims, preferred_element_type=jnp.float32) * FACTOR


def causal(start, count, per, zh, keys):
    key = lax.broadcasted_iota(jnp.int32, (1, keys), 1)
    inner = key % (keys // 2)
    key_half = jnp.where(key < keys // 2, zh, 1 - zh)
    key_pos = (inner // 32) * 64 + key_half * 32 + inner % 32
    row = lax.broadcasted_iota(jnp.int32, (count, 1), 0)
    source = start + row // per
    query_pos = (source // 8) * 64 + zh * 32 + (source % 8) * 4 + row % 4
    return key_pos <= query_pos


def weighted(query, total, parts, allowed):
    weights, values = [], []
    for at, (block, which, offset) in enumerate(parts):
        scores = scores_of(query, block[0, which])
        weight = jnp.exp2(scores if offset is None else scores + offset)
        if allowed is not None and at == 0:
            weight = jnp.where(allowed, weight, 0.0)
        weights.append(weight.astype(jnp.bfloat16))
        value_block = block[1, which]
        values.append(jnp.concatenate([value_block, jnp.ones_like(value_block)], axis=1))
    term = jnp.dot(
        jnp.concatenate(weights, axis=1),
        jnp.concatenate(values, axis=0),
        preferred_element_type=jnp.float32,
    )
    return term if total is None else total + term


def live_of(links_ref, place_ref, m, slot):
    index = place_ref[1] + m
    return links_ref[slot, index] != index


def offset_of(links_ref, place_ref, m, slot):
    return jnp.where(live_of(links_ref, place_ref, m, slot), 0.0, -1e30)


def pack_pairs_kernel(keys_ref, values_ref, o_ref, keys, values, sems):
    copies = [
        pltpu.make_async_copy(keys_ref, keys, sems.at[0]),
        pltpu.make_async_copy(values_ref, values, sems.at[1]),
    ]
    for copy in copies:
        copy.start()
    for copy in copies:
        copy.wait()
    groups = keys.shape[2] // HD
    for x in range(4):
        for group in range(groups):
            columns = slice(group * HD, (group + 1) * HD)
            for kind, array in enumerate((keys, values)):
                for m in range(2):
                    piece = array[2 * x + m, :, columns]
                    o_ref[x * groups + group, kind, m] = piece


def join_kernel(mine, other, o_ref):
    half_keys = mine.shape[2]
    o_ref[:, :, :half_keys] = mine[...]
    o_ref[:, :, half_keys:] = other[...]


def pack_queries_kernel(queries, o_ref):
    width = o_ref.shape[3]
    groups = queries.shape[2] // width
    for x in range(4):
        for group in range(groups):
            for m in range(2):
                piece = queries[2 * x + m, :, group * width : (group + 1) * width]
                o_ref[x * groups + group, m] = piece


def early_kernel(links_ref, place_ref, packed, own, eight, sixteen, q_ref, o_ref):
    sources, _, near, width = packed.shape
    per = q_ref.shape[2]
    step_sources = CHUNK // per
    for m in range(2):

        def unpack(source, carry, m=m):
            wide = packed[source, m].astype(jnp.float32)
            rows = [wide[:, at : at + HD] for at in range(0, width, HD)]
            q_ref[source, m] = jnp.concatenate(rows, axis=0).astype(jnp.bfloat16)
            return carry

        lax.fori_loop(0, sources, unpack, 0)
        parts = [(own, m, None)]
        if m == 1:
            parts.append((own, 0, offset_of(links_ref, place_ref, 1, 0)))
        parts.append((eight, m, offset_of(links_ref, place_ref, m, 3)))
        parts.append((sixteen, m, offset_of(links_ref, place_ref, m, 4)))

        def chunk(step, carry, m=m, parts=parts):
            start = step * step_sources
            query = q_ref[pl.ds(start, step_sources), m].reshape(CHUNK, HD)
            allowed = causal(start, CHUNK, per, place_ref[0], own.shape[2])
            total = weighted(query, None, parts, allowed)
            o_ref[pl.ds(start, step_sources), m] = total.reshape(step_sources, per, 2 * HD)
            return carry

        lax.fori_loop(0, sources // step_sources, chunk, 0)


def late_kernel(links_ref, place_ref, q_ref, early_ref, *refs):
    blocks = refs[:6]
    o_ref, k_all, v_all, s_all, peak, acc, bad_ref = refs[6:]
    own, one, two, eight, sixteen, thirtytwo = blocks
    zh = place_ref[0]
    keys = own.shape[2]
    per = q_ref.shape[2]
    bad_ref[...] = jnp.zeros_like(bad_ref)

    for m in range(2):
        step_sources = CHUNK // per
        sets = [(thirtytwo, m, 5), (two, m, 2), (one, 1, m)]
        if m == 0:
            sets.append((one, 0, 1))
        parts = [
            (block, which, offset_of(links_ref, place_ref, m, slot)) for block, which, slot in sets
        ]

        def quick(step, carry, m=m, parts=parts):
            start = step * step_sources
            query = q_ref[pl.ds(start, step_sources), m].reshape(CHUNK, HD)
            total = early_ref[pl.ds(start, step_sources), m].reshape(CHUNK, 2 * HD)
            total = weighted(query, total, parts, None)
            summed = total[:, HD:]
            fine = (summed >= LEAST) & (summed <= MOST)
            result = (total[:, :HD] / summed).astype(jnp.bfloat16)
            o_ref[pl.ds(start, step_sources), m] = result.reshape(step_sources, per, HD)
            bad = jnp.where(fine, 0.0, 1.0)
            bad_ref[...] = jnp.maximum(bad_ref[...], jnp.max(bad.reshape(-1, 8, HD), axis=0))
            return carry

        lax.fori_loop(0, q_ref.shape[0] // step_sources, quick, 0)

    @pl.when(jnp.max(bad_ref[...]) > 0.0)
    def _():
        v_all[:, :, HD:] = jnp.ones((v_all.shape[0], keys, HD), jnp.bfloat16)
        for place, block in zip((OWN, ONE, TWO, EIGHT, SIXTEEN, THIRTYTWO), blocks):
            for m in range(2):
                k_all[place + m] = block[0, m]
                v_all[place + m, :, :HD] = block[1, m]
        step_sources = SAFE_CHUNK // per

        def sums_of(slot, index):
            top = peak[...]
            shifted = s_all[slot] - jnp.concatenate([top] * (keys // HD), axis=1)
            return jnp.dot(
                jnp.exp2(shifted).astype(jnp.bfloat16),
                v_all[index],
                preferred_element_type=jnp.float32,
            )

        def widest(scores):
            return functools.reduce(
                jnp.maximum, [scores[:, at : at + HD] for at in range(0, keys, HD)]
            )

        for m in range(2):

            def chunk(step, carry, m=m):
                start = step * step_sources
                query = q_ref[pl.ds(start, step_sources), m].reshape(SAFE_CHUNK, HD)
                allowed = causal(start, SAFE_CHUNK, per, zh, keys)
                scores = jnp.where(allowed, scores_of(query, k_all[OWN + m]), -1e30)
                s_all[0] = scores
                peak[...] = widest(scores)
                for slot, index in enumerate(SOURCES[m]):

                    @pl.when(live_of(links_ref, place_ref, m, slot))
                    def _(slot=slot, index=index):
                        scores = scores_of(query, k_all[index])
                        s_all[slot + 1] = scores
                        peak[...] = jnp.maximum(peak[...], widest(scores))

                top = jnp.max(peak[...], axis=1, keepdims=True)
                peak[...] = jnp.broadcast_to(top, (SAFE_CHUNK, HD))
                acc[...] = sums_of(0, OWN + m)
                for slot, index in enumerate(SOURCES[m]):

                    @pl.when(live_of(links_ref, place_ref, m, slot))
                    def _(slot=slot, index=index):
                        acc[...] += sums_of(slot + 1, index)

                result = (acc[:, :HD] / acc[:, HD:]).astype(jnp.bfloat16)
                o_ref[pl.ds(start, step_sources), m] = result.reshape(step_sources, per, HD)
                return carry

            lax.fori_loop(0, q_ref.shape[0] // step_sources, chunk, 0)


def call(kernel, outputs, scratch, flops, scalars, arrays):
    smem = pl.BlockSpec(memory_space=pltpu.SMEM)
    vmem = pl.BlockSpec(memory_space=pltpu.VMEM)
    return pl.pallas_call(
        kernel,
        out_shape=outputs,
        in_specs=[smem] * len(scalars) + [vmem] * len(arrays),
        out_specs=jax.tree.map(lambda _: vmem, outputs),
        scratch_shapes=scratch,
        compiler_params=pltpu.CompilerParams(vmem_limit_bytes=44 * 1024 * 1024),
        cost_estimate=pl.CostEstimate(flops=flops, bytes_accessed=2**20, transcendentals=0),
    )(*scalars, *arrays)


def pack_pairs(keys, values):
    resp, near, width = keys.shape
    output = jax.ShapeDtypeStruct((resp // 2 * width // HD, 2, 2, near, HD), jnp.bfloat16)
    block = pltpu.VMEM(keys.shape, keys.dtype)
    return pl.pallas_call(
        pack_pairs_kernel,
        out_shape=output,
        in_specs=[pl.BlockSpec(memory_space=pl.ANY)] * 2,
        out_specs=pl.BlockSpec(memory_space=pltpu.VMEM),
        scratch_shapes=[block, block, pltpu.SemaphoreType.DMA((2,))],
        compiler_params=pltpu.CompilerParams(vmem_limit_bytes=60 * 1024 * 1024),
    )(keys, values)


def join(mine, other):
    shape = mine.shape[:2] + (2 * mine.shape[2], HD)
    output = jax.ShapeDtypeStruct(shape, jnp.bfloat16)
    return call(join_kernel, output, [], 60 * 10**9, (), (mine, other))


def pack_queries(queries, groups):
    resp, near, width = queries.shape
    output = jax.ShapeDtypeStruct((resp // 2 * groups, 2, near, width // groups), jnp.bfloat16)
    return call(pack_queries_kernel, output, [], 10**6, (), (queries,))


def attend_early(links, place, packed, *blocks):
    sources, _, near, width = packed.shape
    shape = (sources, 2, near * width // HD)
    outputs = [
        jax.ShapeDtypeStruct(shape + (HD,), jnp.bfloat16),
        jax.ShapeDtypeStruct(shape + (2 * HD,), jnp.float32),
    ]
    return call(early_kernel, outputs, [], 4 * 10**9, (links, place), (packed,) + blocks)


def attend_late(links, place, query, early, *blocks):
    keys = blocks[0].shape[2]
    output = jax.ShapeDtypeStruct(query.shape, jnp.bfloat16)
    scratch = [
        pltpu.VMEM((12, keys, HD), jnp.bfloat16),
        pltpu.VMEM((12, keys, 2 * HD), jnp.bfloat16),
        pltpu.VMEM((SLOTS + 1, SAFE_CHUNK, keys), jnp.float32),
        pltpu.VMEM((SAFE_CHUNK, HD), jnp.float32),
        pltpu.VMEM((SAFE_CHUNK, 2 * HD), jnp.float32),
        pltpu.VMEM((8, HD), jnp.float32),
    ]
    return call(late_kernel, output, scratch, 6 * 10**9, (links, place), (query, early) + blocks)


def ring(value, by, keep=lambda h: True):
    pairs = [(z, (z + by) % 16) for z in range(16) if keep(z % 8)]
    return lax.ppermute(value, ("zh", "h"), pairs)


def along(value, by):
    return ring(value, by, lambda h: h + by < 8)


def across(value, by):
    return lax.ppermute(value, "x", [(x, (x + by) % 4) for x in range(4)])


def local(queries, keys, values, links):
    resp, near, width = queries.shape
    groups = keys.shape[2] // HD
    repeat = width // keys.shape[2]
    x, zh, h = lax.axis_index("x"), lax.axis_index("zh"), lax.axis_index("h")

    with jax.named_scope("key_value_exchange"):
        own = pack_pairs(keys, values)
        own = lax.all_to_all(own, PLANE, split_axis=0, concat_axis=0, tiled=True)
        own = own.transpose(1, 2, 0, 3, 4).reshape(2, 2, 4 * groups * near, HD)
        own = join(own, ring(own, 8))
    with jax.named_scope("query_exchange"):
        packed = pack_queries(queries, groups)
        packed = lax.all_to_all(packed, PLANE, split_axis=0, concat_axis=0, tiled=True)
    place = jnp.stack([zh, h * resp + 2 * x]).astype(jnp.int32)
    with jax.named_scope("key_value_spread"):
        eight = along(own, 1)
        thirtytwo = ring(own, -4, lambda h: h < 4)
        sixteen = along(own, 2)
        two = across(jnp.where(x >= 2, eight, own), 2)
        one = across(jnp.where(x >= 3, eight, own), 1)
    with jax.named_scope("attend"):
        links = links.T
        query, early = attend_early(links, place, packed, own, eight, sixteen)
        result = attend_late(links, place, query, early, own, one, two, eight, sixteen, thirtytwo)
    with jax.named_scope("return_exchange"):
        result = lax.all_to_all(result, PLANE, split_axis=0, concat_axis=0, tiled=True)
        result = result.reshape(4, groups, 2, repeat, near, HD).transpose(0, 2, 4, 1, 3, 5)
        return result.reshape(resp, near, width)


def solution(mesh):
    fine = Mesh(mesh.devices.reshape(4, 2, 4, 2, 8), ("x", "zh", "y", "c", "h"))
    placed = P("h", ("x", "zh", "y", "c"), None)
    return jax.shard_map(
        local, mesh=fine, in_specs=(placed, placed, placed, P()), out_specs=placed, check_vma=False
    )
```

time: 133 us -> 128 us (0.962)
  the two profiles are of different devices: /device:TPU:385 before, /device:TPU:449 now
where the time goes in v4:
time: 128 us; the launch traced here: 127 us
  blocking collectives  44.3 us (35%)
  Pallas kernels  41.6 us (32%)
  starting transfers between devices  19.7 us (15%)
  waiting for transfers between devices  18.8 us (15%)
  local copies, waits for them, and re-layouts  2.66 us (2%)
    pallas_call x4, Pallas kernels, call(): pl.pallas_call(kernel, out_shape=outputs, in_specs=[smem] * len(scalars)...  40.1 us
    all_to_all x1, blocking collectives, local(): lax.all_to_all(result, PLANE, split_axis=0, concat_axis=0, tiled=True)  28.8 us
    ppermute x4, waiting for transfers between devices, ring(): return lax.ppermute(value, ('zh', 'h'), pairs)  18.8 us
    all_to_all x1, blocking collectives, local(): own = lax.all_to_all(own, PLANE, split_axis=0, concat_axis=0, tiled=True)  15.5 us
    ppermute x4, starting transfers between devices, ring(): return lax.ppermute(value, ('zh', 'h'), pairs)  9.65 us
    ppermute x2, starting transfers between devices, across(): return lax.ppermute(value, 'x', [(x, (x + by) % 4) for x in range(4)])  5.83 us
    all_to_all x1, starting transfers between devices, local(): lax.all_to_all(packed, PLANE, split_axis=0, concat_axis=0, tiled=True)  4.26 us
  transfers between devices with their start and end apart: 7, of which 2 were waited for; matrix products, arithmetic and copies ran while one was open for 0% of the time, Pallas kernels for 7%

profile of v4, /device:TPU:449, one launch (start us, length us, event | category | flops | bytes accessed | tf_op | source)
XLA Modules:
  0.0 127.4 jit_solution(11004424182031690602)
XLA Ops:
  0.0 1.6 %key_value_exchange.2 = bf16[32,2,2,4,128]{4,3,2,1,0:T(4,128)(2,1)} custom-call(bf16[8,4,1024]{2,1,0:T(4,128)(2,1)} %keys_ref.1, bf16[8,4,1024]{2,1,0:T(4,128)(2,1)} %values_ref.1), custom_call_target="tpu_custom_call" | custom-call | tf_op jit(solution)/shard_map/key_value_exchange/pallas_call | solution.py:240
  1.6 15.5 %all_to_all.15 = bf16[32,2,2,4,128]{4,3,2,1,0:T(4,128)(2,1)S(1)} all-to-all(bf16[32,2,2,4,128]{4,3,2,1,0:T(4,128)(2,1)} %key_value_exchange.2), channel_id=1, replica_groups=mesh['x'=4,'zh'=2,'y'=4,'c'=2,'h'=8] {'x','y','c'}, dimensions={0} | all-to-all | bytes 262144 | tf_op jit(solution)/shard_map/key_value_exchange/all_to_all | solution.py:307
  17.1 5.2 %collective-permute-start = (bf16[2,2,128,128]{3,2,1,0:T(8,128)(2,1)S(1)}, bf16[2,2,128,128]{3,2,1,0:T(8,128)(2,1)S(1)}, u32[]{:S(2)}, u32[]{:S(2)}) collective-permute-start(bf16[2,2,128,128]{3,2,1,0:T(8,128)(2,1)S(1)} %bitcast.10), channel_id=1, source_target_pairs={{0,64},{1,65},{2,66},{3,67},{4,68},{5,69},{6,70},{7,71},{64,0},{65... | collective-permute-start | bytes 393224 | tf_op jit(solution)/shard_map/key_value_exchange/ppermute | solution.py:288
  22.3 0.0 copy-start
  22.3 1.2 copy-done
  23.5 1.0 query_exchange.1
  24.6 4.3 %all-to-all-start = ((bf16[32,2,4,2048]{3,2,1,0:T(4,128)(2,1)}), bf16[32,2,4,2048]{3,2,1,0:T(4,128)(2,1)S(1)}, u32[]{:S(2)}, u32[]{:S(2)}) async-start(bf16[32,2,4,2048]{3,2,1,0:T(4,128)(2,1)} %query_exchange.1), calls=%async_computation | async-start | bytes 2097152 | tf_op jit(solution)/shard_map/query_exchange/all_to_all | solution.py:312
  28.8 0.0 copy-start.1
  28.8 12.0 %collective-permute-done.other = bf16[2,2,128,128]{3,2,1,0:T(8,128)(2,1)S(1)} collective-permute-done((bf16[2,2,128,128]{3,2,1,0:T(8,128)(2,1)S(1)}, bf16[2,2,128,128]{3,2,1,0:T(8,128)(2,1)S(1)}, u32[]{:S(2)}, u32[]{:S(2)}) %collective-permute-start) | collective-permute-done | bytes 131104 | tf_op jit(solution)/shard_map/key_value_exchange/ppermute | solution.py:288
  40.8 1.9 %collective-permute-start.1 = (bf16[2,2,256,128]{3,2,1,0:T(8,128)(2,1)S(1)}, bf16[2,2,256,128]{3,2,1,0:T(8,128)(2,1)S(1)}, u32[]{:S(2)}, u32[]{:S(2)}) collective-permute-start(bf16[2,2,256,128]{3,2,1,0:T(8,128)(2,1)S(1)} %key_value_exchange.3.own.refs_0_), channel_id=1, source_target_pairs={{0,1},{1,2},{2,3},{3,4},{4,5},{5,6},{6,7},{64,65},{65,66},{66,67},... | collective-permute-start | bytes 786440 | tf_op jit(solution)/shard_map/key_value_spread/ppermute | solution.py:288
  42.8 1.3 %collective-permute-start.2 = (bf16[2,2,256,128]{3,2,1,0:T(8,128)(2,1)S(1)}, bf16[2,2,256,128]{3,2,1,0:T(8,128)(2,1)S(1)}, u32[]{:S(2)}, u32[]{:S(2)}) collective-permute-start(bf16[2,2,256,128]{3,2,1,0:T(8,128)(2,1)S(1)} %key_value_exchange.3.own.refs_0_), channel_id=1, source_target_pairs={{0,2},{1,3},{2,4},{3,5},{4,6},{5,7},{64,66},{65,67},{66,68},{67,69... | collective-permute-start | bytes 786440 | tf_op jit(solution)/shard_map/key_value_spread/ppermute | solution.py:288
  44.1 0.1 pad_add_fusion.place_ref
  44.2 1.3 %collective-permute-start.5 = (bf16[2,2,256,128]{3,2,1,0:T(8,128)(2,1)S(1)}, bf16[2,2,256,128]{3,2,1,0:T(8,128)(2,1)S(1)}, u32[]{:S(2)}, u32[]{:S(2)}) collective-permute-start(bf16[2,2,256,128]{3,2,1,0:T(8,128)(2,1)S(1)} %key_value_exchange.3.own.refs_0_), channel_id=1, source_target_pairs={{0,68},{1,69},{2,70},{3,71},{64,4},{65,5},{66,6},{67,7},{8,76},{9,... | collective-permute-start | bytes 786440 | tf_op jit(solution)/shard_map/key_value_spread/ppermute | solution.py:288
  45.4 6.8 %collective-permute-done.1.eight.refs_3_ = bf16[2,2,256,128]{3,2,1,0:T(8,128)(2,1)S(1)} collective-permute-done((bf16[2,2,256,128]{3,2,1,0:T(8,128)(2,1)S(1)}, bf16[2,2,256,128]{3,2,1,0:T(8,128)(2,1)S(1)}, u32[]{:S(2)}, u32[]{:S(2)}) %collective-permute-start.1) | collective-permute-done | bytes 262176 | tf_op jit(solution)/shard_map/key_value_spread/ppermute | solution.py:288
  52.3 2.2 %collective-permute-start.3 = (bf16[2,2,256,128]{3,2,1,0:T(8,128)(2,1)S(1)}, bf16[2,2,256,128]{3,2,1,0:T(8,128)(2,1)S(1)}, u32[]{:S(2)}, u32[]{:S(2)}) collective-permute-start(bf16[2,2,256,128]{3,2,1,0:T(8,128)(2,1)S(1)} %get-tuple-element.10), channel_id=1, source_target_pairs={{0,128},{128,256},{256,384},{384,0},{1,129},{129,257},{257,385},{3... | collective-permute-start | bytes 786440 | tf_op jit(solution)/shard_map/key_value_spread/ppermute | solution.py:296
  54.5 3.6 %collective-permute-start.4 = (bf16[2,2,256,128]{3,2,1,0:T(8,128)(2,1)S(1)}, bf16[2,2,256,128]{3,2,1,0:T(8,128)(2,1)S(1)}, u32[]{:S(2)}, u32[]{:S(2)}) collective-permute-start(bf16[2,2,256,128]{3,2,1,0:T(8,128)(2,1)S(1)} %get-tuple-element.9), channel_id=1, source_target_pairs={{0,256},{128,384},{256,0},{384,128},{1,257},{129,385},{257,1},{385... | collective-permute-start | bytes 786440 | tf_op jit(solution)/shard_map/key_value_spread/ppermute | solution.py:296
  58.1 0.0 collective-permute-done.2.sixteen.refs_4_
  58.2 8.4 %attend.2 = (bf16[32,2,64,128]{3,2,1,0:T(8,128)(2,1)S(1)}, f32[32,2,64,256]{3,2,1,0:T(8,128)S(1)}) custom-call(s32[6,64]{1,0:T(8,128)S(1)} %bitcast.12, s32[2]{0:T(128)S(1)} %pad_add_fusion.place_ref, bf16[32,2,4,2048]{3,2,1,0:T(4,128)(2,1)S(1)} %all-to-all-done.packed, bf16[2,2,256,128]{3,2,1,0:T(8,128)(2,1)S(1)} %key_value_exchange.3.own.refs_0_, ...), custom_call_target="tpu_custom_call" | custom-call | flops 4000000000 | bytes 1048576 | tf_op jit(solution)/shard_map/attend/pallas_call | solution.py:225
  66.6 0.0 collective-permute-done.3.refs_1_
  66.6 0.0 collective-permute-done.4.refs_2_
  66.6 30.6 %attend.3 = bf16[32,2,64,128]{3,2,1,0:T(8,128)(2,1)S(1)} custom-call(s32[6,64]{1,0:T(8,128)S(1)} %bitcast.13, s32[2]{0:T(128)S(1)} %pad_add_fusion.place_ref, bf16[32,2,64,128]{3,2,1,0:T(8,128)(2,1)S(1)} %get-tuple-element.7.q_ref, f32[32,2,64,256]{3,2,1,0:T(8,128)S(1)} %get-tuple-element.8.early_ref, ...), custom_call_target="tpu_custom_call" | custom-call | flops 6000000000 | bytes 1048576 | tf_op jit(solution)/shard_map/attend/pallas_call | solution.py:225
  97.2 28.8 %all_to_all.16 = bf16[32,2,64,128]{3,2,1,0:T(8,128)(2,1)S(1)} all-to-all(bf16[32,2,64,128]{3,2,1,0:T(8,128)(2,1)S(1)} %attend.3), channel_id=1, replica_groups=mesh['x'=4,'zh'=2,'y'=4,'c'=2,'h'=8] {'x','y','c'}, dimensions={0} | all-to-all | bytes 2097152 | tf_op jit(solution)/shard_map/return_exchange/all_to_all | solution.py:325
  126.0 0.2 copy.6
  126.3 1.1 reshape.11
  (6 shorter events, 0.1 us)
Async XLA Ops:
  17.1 23.7 %collective-permute-start = (bf16[2,2,128,128]{3,2,1,0:T(8,128)(2,1)S(1)}, bf16[2,2,128,128]{3,2,1,0:T(8,128)(2,1)S(1)}, u32[]{:S(2)}, u32[]{:S(2)}) collective-permute-start(bf16[2,2,128,128]{3,2,1,0:T(8,128)(2,1)S(1)} %bitcast.10), channel_id=1, source_target_pairs={{0,64},{1,65},{2,66},{3,67},{4,68},{5,69},{6,70},{7,71},{64,0},{65... | collective-permute-start | bytes 393224 | tf_op jit(solution)/shard_map/key_value_exchange/ppermute | solution.py:288
  22.3 1.2 copy-start
  24.6 33.6 %all-to-all-start = ((bf16[32,2,4,2048]{3,2,1,0:T(4,128)(2,1)}), bf16[32,2,4,2048]{3,2,1,0:T(4,128)(2,1)S(1)}, u32[]{:S(2)}, u32[]{:S(2)}) async-start(bf16[32,2,4,2048]{3,2,1,0:T(4,128)(2,1)} %query_exchange.1), calls=%async_computation | async-start | bytes 2097152 | tf_op jit(solution)/shard_map/query_exchange/all_to_all | solution.py:312
  28.8 29.4 %copy-start.1 = (s32[64,6]{0,1:T(8,128)S(1)}, s32[64,6]{0,1:T(8,128)}, u32[]{:S(2)}) copy-start(s32[64,6]{0,1:T(8,128)} %param.7) | copy-start | bytes 4612
  40.8 11.4 %collective-permute-start.1 = (bf16[2,2,256,128]{3,2,1,0:T(8,128)(2,1)S(1)}, bf16[2,2,256,128]{3,2,1,0:T(8,128)(2,1)S(1)}, u32[]{:S(2)}, u32[]{:S(2)}) collective-permute-start(bf16[2,2,256,128]{3,2,1,0:T(8,128)(2,1)S(1)} %key_value_exchange.3.own.refs_0_), channel_id=1, source_target_pairs={{0,1},{1,2},{2,3},{3,4},{4,5},{5,6},{6,7},{64,65},{65,66},{66,67},... | collective-permute-start | bytes 786440 | tf_op jit(solution)/shard_map/key_value_spread/ppermute | solution.py:288
  42.8 15.4 %collective-permute-start.2 = (bf16[2,2,256,128]{3,2,1,0:T(8,128)(2,1)S(1)}, bf16[2,2,256,128]{3,2,1,0:T(8,128)(2,1)S(1)}, u32[]{:S(2)}, u32[]{:S(2)}) collective-permute-start(bf16[2,2,256,128]{3,2,1,0:T(8,128)(2,1)S(1)} %key_value_exchange.3.own.refs_0_), channel_id=1, source_target_pairs={{0,2},{1,3},{2,4},{3,5},{4,6},{5,7},{64,66},{65,67},{66,68},{67,69... | collective-permute-start | bytes 786440 | tf_op jit(solution)/shard_map/key_value_spread/ppermute | solution.py:288
  44.2 22.4 %collective-permute-start.5 = (bf16[2,2,256,128]{3,2,1,0:T(8,128)(2,1)S(1)}, bf16[2,2,256,128]{3,2,1,0:T(8,128)(2,1)S(1)}, u32[]{:S(2)}, u32[]{:S(2)}) collective-permute-start(bf16[2,2,256,128]{3,2,1,0:T(8,128)(2,1)S(1)} %key_value_exchange.3.own.refs_0_), channel_id=1, source_target_pairs={{0,68},{1,69},{2,70},{3,71},{64,4},{65,5},{66,6},{67,7},{8,76},{9,... | collective-permute-start | bytes 786440 | tf_op jit(solution)/shard_map/key_value_spread/ppermute | solution.py:288
  52.3 14.3 %collective-permute-start.3 = (bf16[2,2,256,128]{3,2,1,0:T(8,128)(2,1)S(1)}, bf16[2,2,256,128]{3,2,1,0:T(8,128)(2,1)S(1)}, u32[]{:S(2)}, u32[]{:S(2)}) collective-permute-start(bf16[2,2,256,128]{3,2,1,0:T(8,128)(2,1)S(1)} %get-tuple-element.10), channel_id=1, source_target_pairs={{0,128},{128,256},{256,384},{384,0},{1,129},{129,257},{257,385},{3... | collective-permute-start | bytes 786440 | tf_op jit(solution)/shard_map/key_value_spread/ppermute | solution.py:296
  54.5 12.1 %collective-permute-start.4 = (bf16[2,2,256,128]{3,2,1,0:T(8,128)(2,1)S(1)}, bf16[2,2,256,128]{3,2,1,0:T(8,128)(2,1)S(1)}, u32[]{:S(2)}, u32[]{:S(2)}) collective-permute-start(bf16[2,2,256,128]{3,2,1,0:T(8,128)(2,1)S(1)} %get-tuple-element.9), channel_id=1, source_target_pairs={{0,256},{128,384},{256,0},{384,128},{1,257},{129,385},{257,1},{385... | collective-permute-start | bytes 786440 | tf_op jit(solution)/shard_map/key_value_spread/ppermute | solution.py:296

commit v5 on v4

--- a/solution.py
+++ b/solution.py
@@ -91,33 +91,29 @@
 
 
 def pack_queries_kernel(queries, o_ref):
-    width = o_ref.shape[3]
-    groups = queries.shape[2] // width
-    for x in range(4):
-        for group in range(groups):
-            for m in range(2):
-                piece = queries[2 * x + m, :, group * width : (group + 1) * width]
-                o_ref[x * groups + group, m] = piece
-
-
-def early_kernel(links_ref, place_ref, packed, own, eight, sixteen, q_ref, o_ref):
-    sources, _, near, width = packed.shape
+    groups = o_ref.shape[0] // 4
+    width = queries.shape[2] // groups
+
+    def one(x, carry):
+        for m in range(2):
+            for group in range(groups):
+                wide = queries[2 * x + m, :, group * width : (group + 1) * width]
+                wide = wide.astype(jnp.float32)
+                rows = [wide[:, at : at + HD] for at in range(0, width, HD)]
+                o_ref[x * groups + group, m] = jnp.concatenate(rows, axis=0).astype(jnp.bfloat16)
+        return carry
+
+    lax.fori_loop(0, 4, one, 0)
+
+
+def early_kernel(links_ref, place_ref, q_ref, own, eight, o_ref):
     per = q_ref.shape[2]
     step_sources = CHUNK // per
     for m in range(2):
-
-        def unpack(source, carry, m=m):
-            wide = packed[source, m].astype(jnp.float32)
-            rows = [wide[:, at : at + HD] for at in range(0, width, HD)]
-            q_ref[source, m] = jnp.concatenate(rows, axis=0).astype(jnp.bfloat16)
-            return carry
-
-        lax.fori_loop(0, sources, unpack, 0)
         parts = [(own, m, None)]
         if m == 1:
             parts.append((own, 0, offset_of(links_ref, place_ref, 1, 0)))
         parts.append((eight, m, offset_of(links_ref, place_ref, m, 3)))
-        parts.append((sixteen, m, offset_of(links_ref, place_ref, m, 4)))
 
         def chunk(step, carry, m=m, parts=parts):
             start = step * step_sources
@@ -127,7 +123,7 @@
             o_ref[pl.ds(start, step_sources), m] = total.reshape(step_sources, per, 2 * HD)
             return carry
 
-        lax.fori_loop(0, sources // step_sources, chunk, 0)
+        lax.fori_loop(0, q_ref.shape[0] // step_sources, chunk, 0)
 
 
 def late_kernel(links_ref, place_ref, q_ref, early_ref, *refs):
@@ -141,7 +137,7 @@
 
     for m in range(2):
         step_sources = CHUNK // per
-        sets = [(thirtytwo, m, 5), (two, m, 2), (one, 1, m)]
+        sets = [(sixteen, m, 4), (thirtytwo, m, 5), (two, m, 2), (one, 1, m)]
         if m == 0:
             sets.append((one, 0, 1))
         parts = [
@@ -255,18 +251,14 @@
 
 def pack_queries(queries, groups):
     resp, near, width = queries.shape
-    output = jax.ShapeDtypeStruct((resp // 2 * groups, 2, near, width // groups), jnp.bfloat16)
+    shape = (resp // 2 * groups, 2, near * width // groups // HD, HD)
+    output = jax.ShapeDtypeStruct(shape, jnp.bfloat16)
     return call(pack_queries_kernel, output, [], 10**6, (), (queries,))
 
 
-def attend_early(links, place, packed, *blocks):
-    sources, _, near, width = packed.shape
-    shape = (sources, 2, near * width // HD)
-    outputs = [
-        jax.ShapeDtypeStruct(shape + (HD,), jnp.bfloat16),
-        jax.ShapeDtypeStruct(shape + (2 * HD,), jnp.float32),
-    ]
-    return call(early_kernel, outputs, [], 4 * 10**9, (links, place), (packed,) + blocks)
+def attend_early(links, place, query, *blocks):
+    output = jax.ShapeDtypeStruct(query.shape[:3] + (2 * HD,), jnp.float32)
+    return call(early_kernel, output, [], 4 * 10**9, (links, place), (query,) + blocks)
 
 
 def attend_late(links, place, query, early, *blocks):
@@ -308,8 +300,8 @@
         own = own.transpose(1, 2, 0, 3, 4).reshape(2, 2, 4 * groups * near, HD)
         own = join(own, ring(own, 8))
     with jax.named_scope("query_exchange"):
-        packed = pack_queries(queries, groups)
-        packed = lax.all_to_all(packed, PLANE, split_axis=0, concat_axis=0, tiled=True)
+        query = pack_queries(queries, groups)
+        query = lax.all_to_all(query, PLANE, split_axis=0, concat_axis=0, tiled=True)
     place = jnp.stack([zh, h * resp + 2 * x]).astype(jnp.int32)
     with jax.named_scope("key_value_spread"):
         eight = along(own, 1)
@@ -319,7 +311,7 @@
         one = across(jnp.where(x >= 3, eight, own), 1)
     with jax.named_scope("attend"):
         links = links.T
-        query, early = attend_early(links, place, packed, own, eight, sixteen)
+        early = attend_early(links, place, query, own, eight)
         result = attend_late(links, place, query, early, own, one, two, eight, sixteen, thirtytwo)
     with jax.named_scope("return_exchange"):
         result = lax.all_to_all(result, PLANE, split_axis=0, concat_axis=0, tiled=True)

time: 128 us -> 125 us (0.977)
  Pallas kernels: 41.6 us -> 36.4 us
  blocking collectives: 44.3 us -> 48.2 us
    pallas_call x4, Pallas kernels: 40.1 us -> 34.8 us  [call(): pl.pallas_call(kernel, out_shape=outputs, in_specs=[smem] * len(scalars)...]
    all_to_all x1, blocking collectives: 28.8 us -> 32.7 us  [local(): lax.all_to_all(result, PLANE, split_axis=0, concat_axis=0, tiled=True)]
    ppermute x4, waiting for transfers between devices: 18.8 us -> 16.1 us  [ring(): return lax.ppermute(value, ('zh', 'h'), pairs)]
    ppermute x2, waiting for transfers between devices: 0.01 us -> 1.86 us  [across(): return lax.ppermute(value, 'x', [(x, (x + by) % 4) for x in range(4)])]
  transfers between devices with their start and end apart: 7 -> 7, of which waited for: 2 -> 4; matrix products, arithmetic and copies ran while one was open for 0% -> 0% of each run, Pallas kernels for 7% -> 4%
where the time goes in v5:
time: 125 us
  blocking collectives  48.2 us (39%)
  Pallas kernels  36.4 us (29%)
  starting transfers between devices  19.1 us (15%)
  waiting for transfers between devices  18 us (14%)
  local copies, waits for them, and re-layouts  2.66 us (2%)
    pallas_call x4, Pallas kernels, call(): pl.pallas_call(kernel, out_shape=outputs, in_specs=[smem] * len(scalars)...  34.8 us
    all_to_all x1, blocking collectives, local(): lax.all_to_all(result, PLANE, split_axis=0, concat_axis=0, tiled=True)  32.7 us
    ppermute x4, waiting for transfers between devices, ring(): return lax.ppermute(value, ('zh', 'h'), pairs)  16.1 us
    all_to_all x1, blocking collectives, local(): own = lax.all_to_all(own, PLANE, split_axis=0, concat_axis=0, tiled=True)  15.5 us
    ppermute x4, starting transfers between devices, ring(): return lax.ppermute(value, ('zh', 'h'), pairs)  9.65 us
    ppermute x2, starting transfers between devices, across(): return lax.ppermute(value, 'x', [(x, (x + by) % 4) for x in range(4)])  5.23 us
    all_to_all x1, starting transfers between devices, local(): lax.all_to_all(query, PLANE, split_axis=0, concat_axis=0, tiled=True)  4.26 us
  transfers between devices with their start and end apart: 7, of which 4 were waited for; matrix products, arithmetic and copies ran while one was open for 0% of the time, Pallas kernels for 4%

profile of v5, /device:TPU:449, one launch (start us, length us, event | category | flops | bytes accessed | tf_op | source)
XLA Modules:
  0.0 124.6 jit_solution(9078566660663829565)
XLA Ops:
  0.0 1.6 %key_value_exchange.2 = bf16[32,2,2,4,128]{4,3,2,1,0:T(4,128)(2,1)} custom-call(bf16[8,4,1024]{2,1,0:T(4,128)(2,1)} %keys_ref.1, bf16[8,4,1024]{2,1,0:T(4,128)(2,1)} %values_ref.1), custom_call_target="tpu_custom_call" | custom-call | tf_op jit(solution)/shard_map/key_value_exchange/pallas_call | solution.py:236
  1.6 15.5 %all_to_all.15 = bf16[32,2,2,4,128]{4,3,2,1,0:T(4,128)(2,1)S(1)} all-to-all(bf16[32,2,2,4,128]{4,3,2,1,0:T(4,128)(2,1)} %key_value_exchange.2), channel_id=1, replica_groups=mesh['x'=4,'zh'=2,'y'=4,'c'=2,'h'=8] {'x','y','c'}, dimensions={0} | all-to-all | bytes 262144 | tf_op jit(solution)/shard_map/key_value_exchange/all_to_all | solution.py:299
  17.1 5.2 %collective-permute-start = (bf16[2,2,128,128]{3,2,1,0:T(8,128)(2,1)S(1)}, bf16[2,2,128,128]{3,2,1,0:T(8,128)(2,1)S(1)}, u32[]{:S(2)}, u32[]{:S(2)}) collective-permute-start(bf16[2,2,128,128]{3,2,1,0:T(8,128)(2,1)S(1)} %bitcast.10), channel_id=1, source_target_pairs={{0,64},{1,65},{2,66},{3,67},{4,68},{5,69},{6,70},{7,71},{64,0},{65... | collective-permute-start | bytes 393224 | tf_op jit(solution)/shard_map/key_value_exchange/ppermute | solution.py:280
  22.3 0.0 copy-start
  22.3 1.2 copy-done
  23.5 1.1 query_exchange.1
  24.6 4.3 %all-to-all-start = ((bf16[32,2,64,128]{3,2,1,0:T(8,128)(2,1)}), bf16[32,2,64,128]{3,2,1,0:T(8,128)(2,1)S(1)}, u32[]{:S(2)}, u32[]{:S(2)}) async-start(bf16[32,2,64,128]{3,2,1,0:T(8,128)(2,1)} %query_exchange.1), calls=%async_computation | async-start | bytes 2097152 | tf_op jit(solution)/shard_map/query_exchange/all_to_all | solution.py:304
  28.9 0.0 copy-start.1
  28.9 11.9 %collective-permute-done.other = bf16[2,2,128,128]{3,2,1,0:T(8,128)(2,1)S(1)} collective-permute-done((bf16[2,2,128,128]{3,2,1,0:T(8,128)(2,1)S(1)}, bf16[2,2,128,128]{3,2,1,0:T(8,128)(2,1)S(1)}, u32[]{:S(2)}, u32[]{:S(2)}) %collective-permute-start) | collective-permute-done | bytes 131104 | tf_op jit(solution)/shard_map/key_value_exchange/ppermute | solution.py:280
  40.8 1.9 %collective-permute-start.1 = (bf16[2,2,256,128]{3,2,1,0:T(8,128)(2,1)S(1)}, bf16[2,2,256,128]{3,2,1,0:T(8,128)(2,1)S(1)}, u32[]{:S(2)}, u32[]{:S(2)}) collective-permute-start(bf16[2,2,256,128]{3,2,1,0:T(8,128)(2,1)S(1)} %key_value_exchange.3.own.refs_0_), channel_id=1, source_target_pairs={{0,1},{1,2},{2,3},{3,4},{4,5},{5,6},{6,7},{64,65},{65,66},{66,67},... | collective-permute-start | bytes 786440 | tf_op jit(solution)/shard_map/key_value_spread/ppermute | solution.py:280
  42.8 0.1 pad_add_fusion.place_ref
  42.9 1.3 %collective-permute-start.5 = (bf16[2,2,256,128]{3,2,1,0:T(8,128)(2,1)S(1)}, bf16[2,2,256,128]{3,2,1,0:T(8,128)(2,1)S(1)}, u32[]{:S(2)}, u32[]{:S(2)}) collective-permute-start(bf16[2,2,256,128]{3,2,1,0:T(8,128)(2,1)S(1)} %key_value_exchange.3.own.refs_0_), channel_id=1, source_target_pairs={{0,68},{1,69},{2,70},{3,71},{64,4},{65,5},{66,6},{67,7},{8,76},{9,... | collective-permute-start | bytes 786440 | tf_op jit(solution)/shard_map/key_value_spread/ppermute | solution.py:280
  44.2 1.3 %collective-permute-start.4 = (bf16[2,2,256,128]{3,2,1,0:T(8,128)(2,1)S(1)}, bf16[2,2,256,128]{3,2,1,0:T(8,128)(2,1)S(1)}, u32[]{:S(2)}, u32[]{:S(2)}) collective-permute-start(bf16[2,2,256,128]{3,2,1,0:T(8,128)(2,1)S(1)} %key_value_exchange.3.own.refs_0_), channel_id=1, source_target_pairs={{0,2},{1,3},{2,4},{3,5},{4,6},{5,7},{64,66},{65,67},{66,68},{67,69... | collective-permute-start | bytes 786440 | tf_op jit(solution)/shard_map/key_value_spread/ppermute | solution.py:280
  45.5 3.7 %collective-permute-done.1.eight.refs_3_ = bf16[2,2,256,128]{3,2,1,0:T(8,128)(2,1)S(1)} collective-permute-done((bf16[2,2,256,128]{3,2,1,0:T(8,128)(2,1)S(1)}, bf16[2,2,256,128]{3,2,1,0:T(8,128)(2,1)S(1)}, u32[]{:S(2)}, u32[]{:S(2)}) %collective-permute-start.1) | collective-permute-done | bytes 262176 | tf_op jit(solution)/shard_map/key_value_spread/ppermute | solution.py:280
  49.1 2.9 %collective-permute-start.3 = (bf16[2,2,256,128]{3,2,1,0:T(8,128)(2,1)S(1)}, bf16[2,2,256,128]{3,2,1,0:T(8,128)(2,1)S(1)}, u32[]{:S(2)}, u32[]{:S(2)}) collective-permute-start(bf16[2,2,256,128]{3,2,1,0:T(8,128)(2,1)S(1)} %get-tuple-element.5), channel_id=1, source_target_pairs={{0,256},{128,384},{256,0},{384,128},{1,257},{129,385},{257,1},{385... | collective-permute-start | bytes 786440 | tf_op jit(solution)/shard_map/key_value_spread/ppermute | solution.py:288
  52.1 2.3 %collective-permute-start.2 = (bf16[2,2,256,128]{3,2,1,0:T(8,128)(2,1)S(1)}, bf16[2,2,256,128]{3,2,1,0:T(8,128)(2,1)S(1)}, u32[]{:S(2)}, u32[]{:S(2)}) collective-permute-start(bf16[2,2,256,128]{3,2,1,0:T(8,128)(2,1)S(1)} %get-tuple-element.6), channel_id=1, source_target_pairs={{0,128},{128,256},{256,384},{384,0},{1,129},{129,257},{257,385},{3... | collective-permute-start | bytes 786440 | tf_op jit(solution)/shard_map/key_value_spread/ppermute | solution.py:288
  54.4 0.0 all-to-all-done.q_ref
  54.4 3.7 %attend.2.early_ref = f32[32,2,64,256]{3,2,1,0:T(8,128)S(1)} custom-call(s32[6,64]{1,0:T(8,128)S(1)} %bitcast.12, s32[2]{0:T(128)S(1)} %pad_add_fusion.place_ref, bf16[32,2,64,128]{3,2,1,0:T(8,128)(2,1)S(1)} %all-to-all-done.q_ref, bf16[2,2,256,128]{3,2,1,0:T(8,128)(2,1)S(1)} %key_value_exchange.3.own.refs_0_, ...), custom_call_target="tpu_custom_call" | custom-call | flops 4000000000 | bytes 1048576 | tf_op jit(solution)/shard_map/attend/pallas_call | solution.py:221
  58.1 0.6 collective-permute-done.5.refs_5_
  58.7 1.9 %collective-permute-done.2.refs_1_ = bf16[2,2,256,128]{3,2,1,0:T(8,128)(2,1)S(1)} collective-permute-done((bf16[2,2,256,128]{3,2,1,0:T(8,128)(2,1)S(1)}, bf16[2,2,256,128]{3,2,1,0:T(8,128)(2,1)S(1)}, u32[]{:S(2)}, u32[]{:S(2)}) %collective-permute-start.2) | collective-permute-done | bytes 262176 | tf_op jit(solution)/shard_map/key_value_spread/ppermute | solution.py:288
  60.6 29.9 %attend.3 = bf16[32,2,64,128]{3,2,1,0:T(8,128)(2,1)S(1)} custom-call(s32[6,64]{1,0:T(8,128)S(1)} %bitcast.13, s32[2]{0:T(128)S(1)} %pad_add_fusion.place_ref, bf16[32,2,64,128]{3,2,1,0:T(8,128)(2,1)S(1)} %all-to-all-done.q_ref, f32[32,2,64,256]{3,2,1,0:T(8,128)S(1)} %attend.2.early_ref, bf16[2,2,256,128]{3,2,1,0:T(8,128)(2,1)S(1)} %key_value_exchange.3.own.refs_0_, ...), custom_call_target="tpu_custom_call" | custom-call | flops 6000000000 | bytes 1048576 | tf_op jit(solution)/shard_map/attend/pallas_call | solution.py:221
  90.5 32.7 %all_to_all.16 = bf16[32,2,64,128]{3,2,1,0:T(8,128)(2,1)S(1)} all-to-all(bf16[32,2,64,128]{3,2,1,0:T(8,128)(2,1)S(1)} %attend.3), channel_id=1, replica_groups=mesh['x'=4,'zh'=2,'y'=4,'c'=2,'h'=8] {'x','y','c'}, dimensions={0} | all-to-all | bytes 2097152 | tf_op jit(solution)/shard_map/return_exchange/all_to_all | solution.py:317
  123.2 0.2 copy.6
  123.5 1.1 reshape.11
  (6 shorter events, 0.1 us)
Async XLA Ops:
  17.1 23.7 %collective-permute-start = (bf16[2,2,128,128]{3,2,1,0:T(8,128)(2,1)S(1)}, bf16[2,2,128,128]{3,2,1,0:T(8,128)(2,1)S(1)}, u32[]{:S(2)}, u32[]{:S(2)}) collective-permute-start(bf16[2,2,128,128]{3,2,1,0:T(8,128)(2,1)S(1)} %bitcast.10), channel_id=1, source_target_pairs={{0,64},{1,65},{2,66},{3,67},{4,68},{5,69},{6,70},{7,71},{64,0},{65... | collective-permute-start | bytes 393224 | tf_op jit(solution)/shard_map/key_value_exchange/ppermute | solution.py:280
  22.3 1.2 copy-start
  24.6 29.8 %all-to-all-start = ((bf16[32,2,64,128]{3,2,1,0:T(8,128)(2,1)}), bf16[32,2,64,128]{3,2,1,0:T(8,128)(2,1)S(1)}, u32[]{:S(2)}, u32[]{:S(2)}) async-start(bf16[32,2,64,128]{3,2,1,0:T(8,128)(2,1)} %query_exchange.1), calls=%async_computation | async-start | bytes 2097152 | tf_op jit(solution)/shard_map/query_exchange/all_to_all | solution.py:304
  28.9 25.5 %copy-start.1 = (s32[64,6]{0,1:T(8,128)S(1)}, s32[64,6]{0,1:T(8,128)}, u32[]{:S(2)}) copy-start(s32[64,6]{0,1:T(8,128)} %param.7) | copy-start | bytes 4612
  40.8 8.3 %collective-permute-start.1 = (bf16[2,2,256,128]{3,2,1,0:T(8,128)(2,1)S(1)}, bf16[2,2,256,128]{3,2,1,0:T(8,128)(2,1)S(1)}, u32[]{:S(2)}, u32[]{:S(2)}) collective-permute-start(bf16[2,2,256,128]{3,2,1,0:T(8,128)(2,1)S(1)} %key_value_exchange.3.own.refs_0_), channel_id=1, source_target_pairs={{0,1},{1,2},{2,3},{3,4},{4,5},{5,6},{6,7},{64,65},{65,66},{66,67},... | collective-permute-start | bytes 786440 | tf_op jit(solution)/shard_map/key_value_spread/ppermute | solution.py:280
  42.9 15.9 %collective-permute-start.5 = (bf16[2,2,256,128]{3,2,1,0:T(8,128)(2,1)S(1)}, bf16[2,2,256,128]{3,2,1,0:T(8,128)(2,1)S(1)}, u32[]{:S(2)}, u32[]{:S(2)}) collective-permute-start(bf16[2,2,256,128]{3,2,1,0:T(8,128)(2,1)S(1)} %key_value_exchange.3.own.refs_0_), channel_id=1, source_target_pairs={{0,68},{1,69},{2,70},{3,71},{64,4},{65,5},{66,6},{67,7},{8,76},{9,... | collective-permute-start | bytes 786440 | tf_op jit(solution)/shard_map/key_value_spread/ppermute | solution.py:280
  44.2 14.6 %collective-permute-start.4 = (bf16[2,2,256,128]{3,2,1,0:T(8,128)(2,1)S(1)}, bf16[2,2,256,128]{3,2,1,0:T(8,128)(2,1)S(1)}, u32[]{:S(2)}, u32[]{:S(2)}) collective-permute-start(bf16[2,2,256,128]{3,2,1,0:T(8,128)(2,1)S(1)} %key_value_exchange.3.own.refs_0_), channel_id=1, source_target_pairs={{0,2},{1,3},{2,4},{3,5},{4,6},{5,7},{64,66},{65,67},{66,68},{67,69... | collective-permute-start | bytes 786440 | tf_op jit(solution)/shard_map/key_value_spread/ppermute | solution.py:280
  49.1 9.6 %collective-permute-start.3 = (bf16[2,2,256,128]{3,2,1,0:T(8,128)(2,1)S(1)}, bf16[2,2,256,128]{3,2,1,0:T(8,128)(2,1)S(1)}, u32[]{:S(2)}, u32[]{:S(2)}) collective-permute-start(bf16[2,2,256,128]{3,2,1,0:T(8,128)(2,1)S(1)} %get-tuple-element.5), channel_id=1, source_target_pairs={{0,256},{128,384},{256,0},{384,128},{1,257},{129,385},{257,1},{385... | collective-permute-start | bytes 786440 | tf_op jit(solution)/shard_map/key_value_spread/ppermute | solution.py:288
  52.1 8.5 %collective-permute-start.2 = (bf16[2,2,256,128]{3,2,1,0:T(8,128)(2,1)S(1)}, bf16[2,2,256,128]{3,2,1,0:T(8,128)(2,1)S(1)}, u32[]{:S(2)}, u32[]{:S(2)}) collective-permute-start(bf16[2,2,256,128]{3,2,1,0:T(8,128)(2,1)S(1)} %get-tuple-element.6), channel_id=1, source_target_pairs={{0,128},{128,256},{256,384},{384,0},{1,129},{129,257},{257,385},{3... | collective-permute-start | bytes 786440 | tf_op jit(solution)/shard_map/key_value_spread/ppermute | solution.py:288

commit v6 on v5

--- a/solution.py
+++ b/solution.py
@@ -65,15 +65,7 @@
     return jnp.where(live_of(links_ref, place_ref, m, slot), 0.0, -1e30)
 
 
-def pack_pairs_kernel(keys_ref, values_ref, o_ref, keys, values, sems):
-    copies = [
-        pltpu.make_async_copy(keys_ref, keys, sems.at[0]),
-        pltpu.make_async_copy(values_ref, values, sems.at[1]),
-    ]
-    for copy in copies:
-        copy.start()
-    for copy in copies:
-        copy.wait()
+def pack_pairs_kernel(keys, values, o_ref):
     groups = keys.shape[2] // HD
     for x in range(4):
         for group in range(groups):
@@ -232,13 +224,11 @@
 def pack_pairs(keys, values):
     resp, near, width = keys.shape
     output = jax.ShapeDtypeStruct((resp // 2 * width // HD, 2, 2, near, HD), jnp.bfloat16)
-    block = pltpu.VMEM(keys.shape, keys.dtype)
     return pl.pallas_call(
         pack_pairs_kernel,
         out_shape=output,
-        in_specs=[pl.BlockSpec(memory_space=pl.ANY)] * 2,
+        in_specs=[pl.BlockSpec(memory_space=pltpu.VMEM)] * 2,
         out_specs=pl.BlockSpec(memory_space=pltpu.VMEM),
-        scratch_shapes=[block, block, pltpu.SemaphoreType.DMA((2,))],
         compiler_params=pltpu.CompilerParams(vmem_limit_bytes=60 * 1024 * 1024),
     )(keys, values)
 

time: 125 us -> 127 us (1.016)
  Pallas kernels: 36.4 us -> 38.1 us
    pallas_call x4, Pallas kernels: 34.8 us -> 36.5 us  [call(): pl.pallas_call(kernel, out_shape=outputs, in_specs=[smem] * len(scalars)...]
where the time goes in v6:
time: 127 us; the launch traced here: 126 us
  blocking collectives  48.2 us (38%)
  Pallas kernels  38.1 us (30%)
  starting transfers between devices  19.1 us (15%)
  waiting for transfers between devices  18 us (14%)
  local copies, waits for them, and re-layouts  2.66 us (2%)
    pallas_call x4, Pallas kernels, call(): pl.pallas_call(kernel, out_shape=outputs, in_specs=[smem] * len(scalars)...  36.5 us
    all_to_all x1, blocking collectives, local(): lax.all_to_all(result, PLANE, split_axis=0, concat_axis=0, tiled=True)  32.7 us
    ppermute x4, waiting for transfers between devices, ring(): return lax.ppermute(value, ('zh', 'h'), pairs)  16.2 us
    all_to_all x1, blocking collectives, local(): own = lax.all_to_all(own, PLANE, split_axis=0, concat_axis=0, tiled=True)  15.5 us
    ppermute x4, starting transfers between devices, ring(): return lax.ppermute(value, ('zh', 'h'), pairs)  9.65 us
    ppermute x2, starting transfers between devices, across(): return lax.ppermute(value, 'x', [(x, (x + by) % 4) for x in range(4)])  5.23 us
    all_to_all x1, starting transfers between devices, local(): lax.all_to_all(query, PLANE, split_axis=0, concat_axis=0, tiled=True)  4.26 us
  transfers between devices with their start and end apart: 7, of which 4 were waited for; matrix products, arithmetic and copies ran while one was open for 0% of the time, Pallas kernels for 4%

profile of v6, /device:TPU:449, one launch (start us, length us, event | category | flops | bytes accessed | tf_op | source)
XLA Modules:
  0.0 126.4 jit_solution(13970482846274011843)
XLA Ops:
  0.0 1.6 %key_value_exchange.2 = bf16[32,2,2,4,128]{4,3,2,1,0:T(4,128)(2,1)} custom-call(bf16[8,4,1024]{2,1,0:T(4,128)(2,1)} %keys.1, bf16[8,4,1024]{2,1,0:T(4,128)(2,1)} %values.1), custom_call_target="tpu_custom_call" | custom-call | tf_op jit(solution)/shard_map/key_value_exchange/pallas_call | solution.py:227
  1.6 15.5 %all_to_all.15 = bf16[32,2,2,4,128]{4,3,2,1,0:T(4,128)(2,1)S(1)} all-to-all(bf16[32,2,2,4,128]{4,3,2,1,0:T(4,128)(2,1)} %key_value_exchange.2), channel_id=1, replica_groups=mesh['x'=4,'zh'=2,'y'=4,'c'=2,'h'=8] {'x','y','c'}, dimensions={0} | all-to-all | bytes 262144 | tf_op jit(solution)/shard_map/key_value_exchange/all_to_all | solution.py:289
  17.1 5.2 %collective-permute-start = (bf16[2,2,128,128]{3,2,1,0:T(8,128)(2,1)S(1)}, bf16[2,2,128,128]{3,2,1,0:T(8,128)(2,1)S(1)}, u32[]{:S(2)}, u32[]{:S(2)}) collective-permute-start(bf16[2,2,128,128]{3,2,1,0:T(8,128)(2,1)S(1)} %bitcast.10), channel_id=1, source_target_pairs={{0,64},{1,65},{2,66},{3,67},{4,68},{5,69},{6,70},{7,71},{64,0},{65... | collective-permute-start | bytes 393224 | tf_op jit(solution)/shard_map/key_value_exchange/ppermute | solution.py:270
  22.2 0.0 copy-start
  22.3 1.2 copy-done
  23.5 1.1 query_exchange.1
  24.6 4.3 %all-to-all-start = ((bf16[32,2,64,128]{3,2,1,0:T(8,128)(2,1)}), bf16[32,2,64,128]{3,2,1,0:T(8,128)(2,1)S(1)}, u32[]{:S(2)}, u32[]{:S(2)}) async-start(bf16[32,2,64,128]{3,2,1,0:T(8,128)(2,1)} %query_exchange.1), calls=%async_computation | async-start | bytes 2097152 | tf_op jit(solution)/shard_map/query_exchange/all_to_all | solution.py:294
  28.9 0.0 copy-start.1
  28.9 11.9 %collective-permute-done.other = bf16[2,2,128,128]{3,2,1,0:T(8,128)(2,1)S(1)} collective-permute-done((bf16[2,2,128,128]{3,2,1,0:T(8,128)(2,1)S(1)}, bf16[2,2,128,128]{3,2,1,0:T(8,128)(2,1)S(1)}, u32[]{:S(2)}, u32[]{:S(2)}) %collective-permute-start) | collective-permute-done | bytes 131104 | tf_op jit(solution)/shard_map/key_value_exchange/ppermute | solution.py:270
  40.8 1.9 %collective-permute-start.1 = (bf16[2,2,256,128]{3,2,1,0:T(8,128)(2,1)S(1)}, bf16[2,2,256,128]{3,2,1,0:T(8,128)(2,1)S(1)}, u32[]{:S(2)}, u32[]{:S(2)}) collective-permute-start(bf16[2,2,256,128]{3,2,1,0:T(8,128)(2,1)S(1)} %key_value_exchange.3.own.refs_0_), channel_id=1, source_target_pairs={{0,1},{1,2},{2,3},{3,4},{4,5},{5,6},{6,7},{64,65},{65,66},{66,67},... | collective-permute-start | bytes 786440 | tf_op jit(solution)/shard_map/key_value_spread/ppermute | solution.py:270
  42.8 0.1 pad_add_fusion.place_ref
  42.8 1.3 %collective-permute-start.5 = (bf16[2,2,256,128]{3,2,1,0:T(8,128)(2,1)S(1)}, bf16[2,2,256,128]{3,2,1,0:T(8,128)(2,1)S(1)}, u32[]{:S(2)}, u32[]{:S(2)}) collective-permute-start(bf16[2,2,256,128]{3,2,1,0:T(8,128)(2,1)S(1)} %key_value_exchange.3.own.refs_0_), channel_id=1, source_target_pairs={{0,68},{1,69},{2,70},{3,71},{64,4},{65,5},{66,6},{67,7},{8,76},{9,... | collective-permute-start | bytes 786440 | tf_op jit(solution)/shard_map/key_value_spread/ppermute | solution.py:270
  44.1 1.3 %collective-permute-start.4 = (bf16[2,2,256,128]{3,2,1,0:T(8,128)(2,1)S(1)}, bf16[2,2,256,128]{3,2,1,0:T(8,128)(2,1)S(1)}, u32[]{:S(2)}, u32[]{:S(2)}) collective-permute-start(bf16[2,2,256,128]{3,2,1,0:T(8,128)(2,1)S(1)} %key_value_exchange.3.own.refs_0_), channel_id=1, source_target_pairs={{0,2},{1,3},{2,4},{3,5},{4,6},{5,7},{64,66},{65,67},{66,68},{67,69... | collective-permute-start | bytes 786440 | tf_op jit(solution)/shard_map/key_value_spread/ppermute | solution.py:270
  45.4 3.7 %collective-permute-done.1.eight.refs_3_ = bf16[2,2,256,128]{3,2,1,0:T(8,128)(2,1)S(1)} collective-permute-done((bf16[2,2,256,128]{3,2,1,0:T(8,128)(2,1)S(1)}, bf16[2,2,256,128]{3,2,1,0:T(8,128)(2,1)S(1)}, u32[]{:S(2)}, u32[]{:S(2)}) %collective-permute-start.1) | collective-permute-done | bytes 262176 | tf_op jit(solution)/shard_map/key_value_spread/ppermute | solution.py:270
  49.1 2.9 %collective-permute-start.3 = (bf16[2,2,256,128]{3,2,1,0:T(8,128)(2,1)S(1)}, bf16[2,2,256,128]{3,2,1,0:T(8,128)(2,1)S(1)}, u32[]{:S(2)}, u32[]{:S(2)}) collective-permute-start(bf16[2,2,256,128]{3,2,1,0:T(8,128)(2,1)S(1)} %get-tuple-element.5), channel_id=1, source_target_pairs={{0,256},{128,384},{256,0},{384,128},{1,257},{129,385},{257,1},{385... | collective-permute-start | bytes 786440 | tf_op jit(solution)/shard_map/key_value_spread/ppermute | solution.py:278
  52.0 2.3 %collective-permute-start.2 = (bf16[2,2,256,128]{3,2,1,0:T(8,128)(2,1)S(1)}, bf16[2,2,256,128]{3,2,1,0:T(8,128)(2,1)S(1)}, u32[]{:S(2)}, u32[]{:S(2)}) collective-permute-start(bf16[2,2,256,128]{3,2,1,0:T(8,128)(2,1)S(1)} %get-tuple-element.6), channel_id=1, source_target_pairs={{0,128},{128,256},{256,384},{384,0},{1,129},{129,257},{257,385},{3... | collective-permute-start | bytes 786440 | tf_op jit(solution)/shard_map/key_value_spread/ppermute | solution.py:278
  54.4 0.0 all-to-all-done.q_ref
  54.4 3.7 %attend.2.early_ref = f32[32,2,64,256]{3,2,1,0:T(8,128)S(1)} custom-call(s32[6,64]{1,0:T(8,128)S(1)} %bitcast.12, s32[2]{0:T(128)S(1)} %pad_add_fusion.place_ref, bf16[32,2,64,128]{3,2,1,0:T(8,128)(2,1)S(1)} %all-to-all-done.q_ref, bf16[2,2,256,128]{3,2,1,0:T(8,128)(2,1)S(1)} %key_value_exchange.3.own.refs_0_, ...), custom_call_target="tpu_custom_call" | custom-call | flops 4000000000 | bytes 1048576 | tf_op jit(solution)/shard_map/attend/pallas_call | solution.py:213
  58.1 0.6 collective-permute-done.5.refs_5_
  58.7 1.9 %collective-permute-done.2.refs_1_ = bf16[2,2,256,128]{3,2,1,0:T(8,128)(2,1)S(1)} collective-permute-done((bf16[2,2,256,128]{3,2,1,0:T(8,128)(2,1)S(1)}, bf16[2,2,256,128]{3,2,1,0:T(8,128)(2,1)S(1)}, u32[]{:S(2)}, u32[]{:S(2)}) %collective-permute-start.2) | collective-permute-done | bytes 262176 | tf_op jit(solution)/shard_map/key_value_spread/ppermute | solution.py:278
  60.5 31.7 %attend.3 = bf16[32,2,64,128]{3,2,1,0:T(8,128)(2,1)S(1)} custom-call(s32[6,64]{1,0:T(8,128)S(1)} %bitcast.13, s32[2]{0:T(128)S(1)} %pad_add_fusion.place_ref, bf16[32,2,64,128]{3,2,1,0:T(8,128)(2,1)S(1)} %all-to-all-done.q_ref, f32[32,2,64,256]{3,2,1,0:T(8,128)S(1)} %attend.2.early_ref, bf16[2,2,256,128]{3,2,1,0:T(8,128)(2,1)S(1)} %key_value_exchange.3.own.refs_0_, ...), custom_call_target="tpu_custom_call" | custom-call | flops 6000000000 | bytes 1048576 | tf_op jit(solution)/shard_map/attend/pallas_call | solution.py:213
  92.2 32.7 %all_to_all.16 = bf16[32,2,64,128]{3,2,1,0:T(8,128)(2,1)S(1)} all-to-all(bf16[32,2,64,128]{3,2,1,0:T(8,128)(2,1)S(1)} %attend.3), channel_id=1, replica_groups=mesh['x'=4,'zh'=2,'y'=4,'c'=2,'h'=8] {'x','y','c'}, dimensions={0} | all-to-all | bytes 2097152 | tf_op jit(solution)/shard_map/return_exchange/all_to_all | solution.py:307
  125.0 0.2 copy.6
  125.2 1.1 reshape.11
  (6 shorter events, 0.1 us)
Async XLA Ops:
  17.1 23.7 %collective-permute-start = (bf16[2,2,128,128]{3,2,1,0:T(8,128)(2,1)S(1)}, bf16[2,2,128,128]{3,2,1,0:T(8,128)(2,1)S(1)}, u32[]{:S(2)}, u32[]{:S(2)}) collective-permute-start(bf16[2,2,128,128]{3,2,1,0:T(8,128)(2,1)S(1)} %bitcast.10), channel_id=1, source_target_pairs={{0,64},{1,65},{2,66},{3,67},{4,68},{5,69},{6,70},{7,71},{64,0},{65... | collective-permute-start | bytes 393224 | tf_op jit(solution)/shard_map/key_value_exchange/ppermute | solution.py:270
  22.2 1.2 copy-start
  24.6 29.8 %all-to-all-start = ((bf16[32,2,64,128]{3,2,1,0:T(8,128)(2,1)}), bf16[32,2,64,128]{3,2,1,0:T(8,128)(2,1)S(1)}, u32[]{:S(2)}, u32[]{:S(2)}) async-start(bf16[32,2,64,128]{3,2,1,0:T(8,128)(2,1)} %query_exchange.1), calls=%async_computation | async-start | bytes 2097152 | tf_op jit(solution)/shard_map/query_exchange/all_to_all | solution.py:294
  28.9 25.5 %copy-start.1 = (s32[64,6]{0,1:T(8,128)S(1)}, s32[64,6]{0,1:T(8,128)}, u32[]{:S(2)}) copy-start(s32[64,6]{0,1:T(8,128)} %param.7) | copy-start | bytes 4612
  40.8 8.3 %collective-permute-start.1 = (bf16[2,2,256,128]{3,2,1,0:T(8,128)(2,1)S(1)}, bf16[2,2,256,128]{3,2,1,0:T(8,128)(2,1)S(1)}, u32[]{:S(2)}, u32[]{:S(2)}) collective-permute-start(bf16[2,2,256,128]{3,2,1,0:T(8,128)(2,1)S(1)} %key_value_exchange.3.own.refs_0_), channel_id=1, source_target_pairs={{0,1},{1,2},{2,3},{3,4},{4,5},{5,6},{6,7},{64,65},{65,66},{66,67},... | collective-permute-start | bytes 786440 | tf_op jit(solution)/shard_map/key_value_spread/ppermute | solution.py:270
  42.8 15.9 %collective-permute-start.5 = (bf16[2,2,256,128]{3,2,1,0:T(8,128)(2,1)S(1)}, bf16[2,2,256,128]{3,2,1,0:T(8,128)(2,1)S(1)}, u32[]{:S(2)}, u32[]{:S(2)}) collective-permute-start(bf16[2,2,256,128]{3,2,1,0:T(8,128)(2,1)S(1)} %key_value_exchange.3.own.refs_0_), channel_id=1, source_target_pairs={{0,68},{1,69},{2,70},{3,71},{64,4},{65,5},{66,6},{67,7},{8,76},{9,... | collective-permute-start | bytes 786440 | tf_op jit(solution)/shard_map/key_value_spread/ppermute | solution.py:270
  44.1 14.6 %collective-permute-start.4 = (bf16[2,2,256,128]{3,2,1,0:T(8,128)(2,1)S(1)}, bf16[2,2,256,128]{3,2,1,0:T(8,128)(2,1)S(1)}, u32[]{:S(2)}, u32[]{:S(2)}) collective-permute-start(bf16[2,2,256,128]{3,2,1,0:T(8,128)(2,1)S(1)} %key_value_exchange.3.own.refs_0_), channel_id=1, source_target_pairs={{0,2},{1,3},{2,4},{3,5},{4,6},{5,7},{64,66},{65,67},{66,68},{67,69... | collective-permute-start | bytes 786440 | tf_op jit(solution)/shard_map/key_value_spread/ppermute | solution.py:270
  49.1 9.6 %collective-permute-start.3 = (bf16[2,2,256,128]{3,2,1,0:T(8,128)(2,1)S(1)}, bf16[2,2,256,128]{3,2,1,0:T(8,128)(2,1)S(1)}, u32[]{:S(2)}, u32[]{:S(2)}) collective-permute-start(bf16[2,2,256,128]{3,2,1,0:T(8,128)(2,1)S(1)} %get-tuple-element.5), channel_id=1, source_target_pairs={{0,256},{128,384},{256,0},{384,128},{1,257},{129,385},{257,1},{385... | collective-permute-start | bytes 786440 | tf_op jit(solution)/shard_map/key_value_spread/ppermute | solution.py:278
  52.0 8.5 %collective-permute-start.2 = (bf16[2,2,256,128]{3,2,1,0:T(8,128)(2,1)S(1)}, bf16[2,2,256,128]{3,2,1,0:T(8,128)(2,1)S(1)}, u32[]{:S(2)}, u32[]{:S(2)}) collective-permute-start(bf16[2,2,256,128]{3,2,1,0:T(8,128)(2,1)S(1)} %get-tuple-element.6), channel_id=1, source_target_pairs={{0,128},{128,256},{256,384},{384,0},{1,129},{129,257},{257,385},{3... | collective-permute-start | bytes 786440 | tf_op jit(solution)/shard_map/key_value_spread/ppermute | solution.py:278

commit v7 on v6

--- a/solution.py
+++ b/solution.py
@@ -98,7 +98,7 @@
     lax.fori_loop(0, 4, one, 0)
 
 
-def early_kernel(links_ref, place_ref, q_ref, own, eight, o_ref):
+def early_kernel(links_ref, place_ref, q_ref, own, eight, sixteen, o_ref):
     per = q_ref.shape[2]
     step_sources = CHUNK // per
     for m in range(2):
@@ -106,6 +106,7 @@
         if m == 1:
             parts.append((own, 0, offset_of(links_ref, place_ref, 1, 0)))
         parts.append((eight, m, offset_of(links_ref, place_ref, m, 3)))
+        parts.append((sixteen, m, offset_of(links_ref, place_ref, m, 4)))
 
         def chunk(step, carry, m=m, parts=parts):
             start = step * step_sources
@@ -129,7 +130,7 @@
 
     for m in range(2):
         step_sources = CHUNK // per
-        sets = [(sixteen, m, 4), (thirtytwo, m, 5), (two, m, 2), (one, 1, m)]
+        sets = [(thirtytwo, m, 5), (two, m, 2), (one, 1, m)]
         if m == 0:
             sets.append((one, 0, 1))
         parts = [
@@ -301,7 +302,7 @@
         one = across(jnp.where(x >= 3, eight, own), 1)
     with jax.named_scope("attend"):
         links = links.T
-        early = attend_early(links, place, query, own, eight)
+        early = attend_early(links, place, query, own, eight, sixteen)
         result = attend_late(links, place, query, early, own, one, two, eight, sixteen, thirtytwo)
     with jax.named_scope("return_exchange"):
         result = lax.all_to_all(result, PLANE, split_axis=0, concat_axis=0, tiled=True)

time: 127 us -> 127 us (level)
  the two profiles are of different devices: /device:TPU:449 before, /device:TPU:385 now
where the time goes in v7:
time: 127 us; the launch traced here: 126 us
  Pallas kernels  38.1 us (30%)
  blocking collectives  35.8 us (28%)
  starting transfers between devices  27.6 us (22%)
  waiting for transfers between devices  22.1 us (17%)
  local copies, waits for them, and re-layouts  2.66 us (2%)
    pallas_call x4, Pallas kernels, call(): pl.pallas_call(kernel, out_shape=outputs, in_specs=[smem] * len(scalars)...  36.5 us
    ppermute x4, waiting for transfers between devices, ring(): return lax.ppermute(value, ('zh', 'h'), pairs)  22.1 us
    all_to_all x1, blocking collectives, local(): lax.all_to_all(result, PLANE, split_axis=0, concat_axis=0, tiled=True)  20.3 us
    ppermute x4, starting transfers between devices, ring(): return lax.ppermute(value, ('zh', 'h'), pairs)  18.1 us
    all_to_all x1, blocking collectives, local(): own = lax.all_to_all(own, PLANE, split_axis=0, concat_axis=0, tiled=True)  15.5 us
    ppermute x2, starting transfers between devices, across(): return lax.ppermute(value, 'x', [(x, (x + by) % 4) for x in range(4)])  5.23 us
    all_to_all x1, starting transfers between devices, local(): lax.all_to_all(query, PLANE, split_axis=0, concat_axis=0, tiled=True)  4.26 us
  transfers between devices with their start and end apart: 7, of which 2 were waited for; matrix products, arithmetic and copies ran while one was open for 0% of the time, Pallas kernels for 5%

profile of v7, /device:TPU:385, one launch (start us, length us, event | category | flops | bytes accessed | tf_op | source)
XLA Modules:
  0.0 126.4 jit_solution(17480628910587634829)
XLA Ops:
  0.0 1.6 %key_value_exchange.2 = bf16[32,2,2,4,128]{4,3,2,1,0:T(4,128)(2,1)} custom-call(bf16[8,4,1024]{2,1,0:T(4,128)(2,1)} %keys.1, bf16[8,4,1024]{2,1,0:T(4,128)(2,1)} %values.1), custom_call_target="tpu_custom_call" | custom-call | tf_op jit(solution)/shard_map/key_value_exchange/pallas_call | solution.py:228
  1.6 15.5 %all_to_all.15 = bf16[32,2,2,4,128]{4,3,2,1,0:T(4,128)(2,1)S(1)} all-to-all(bf16[32,2,2,4,128]{4,3,2,1,0:T(4,128)(2,1)} %key_value_exchange.2), channel_id=1, replica_groups=mesh['x'=4,'zh'=2,'y'=4,'c'=2,'h'=8] {'x','y','c'}, dimensions={0} | all-to-all | bytes 262144 | tf_op jit(solution)/shard_map/key_value_exchange/all_to_all | solution.py:290
  17.1 3.4 %collective-permute-start = (bf16[2,2,128,128]{3,2,1,0:T(8,128)(2,1)S(1)}, bf16[2,2,128,128]{3,2,1,0:T(8,128)(2,1)S(1)}, u32[]{:S(2)}, u32[]{:S(2)}) collective-permute-start(bf16[2,2,128,128]{3,2,1,0:T(8,128)(2,1)S(1)} %bitcast.10), channel_id=1, source_target_pairs={{0,64},{1,65},{2,66},{3,67},{4,68},{5,69},{6,70},{7,71},{64,0},{65... | collective-permute-start | bytes 393224 | tf_op jit(solution)/shard_map/key_value_exchange/ppermute | solution.py:271
  20.5 0.0 copy-start
  20.5 1.2 copy-done
  21.7 1.1 query_exchange.1
  22.8 4.3 %all-to-all-start = ((bf16[32,2,64,128]{3,2,1,0:T(8,128)(2,1)}), bf16[32,2,64,128]{3,2,1,0:T(8,128)(2,1)S(1)}, u32[]{:S(2)}, u32[]{:S(2)}) async-start(bf16[32,2,64,128]{3,2,1,0:T(8,128)(2,1)} %query_exchange.1), calls=%async_computation | async-start | bytes 2097152 | tf_op jit(solution)/shard_map/query_exchange/all_to_all | solution.py:295
  27.1 0.0 copy-start.1
  27.1 5.3 %collective-permute-done.other = bf16[2,2,128,128]{3,2,1,0:T(8,128)(2,1)S(1)} collective-permute-done((bf16[2,2,128,128]{3,2,1,0:T(8,128)(2,1)S(1)}, bf16[2,2,128,128]{3,2,1,0:T(8,128)(2,1)S(1)}, u32[]{:S(2)}, u32[]{:S(2)}) %collective-permute-start) | collective-permute-done | bytes 131104 | tf_op jit(solution)/shard_map/key_value_exchange/ppermute | solution.py:271
  32.4 5.6 %collective-permute-start.1 = (bf16[2,2,256,128]{3,2,1,0:T(8,128)(2,1)S(1)}, bf16[2,2,256,128]{3,2,1,0:T(8,128)(2,1)S(1)}, u32[]{:S(2)}, u32[]{:S(2)}) collective-permute-start(bf16[2,2,256,128]{3,2,1,0:T(8,128)(2,1)S(1)} %key_value_exchange.3.own.refs_0_), channel_id=1, source_target_pairs={{0,1},{1,2},{2,3},{3,4},{4,5},{5,6},{6,7},{64,65},{65,66},{66,67},... | collective-permute-start | bytes 786440 | tf_op jit(solution)/shard_map/key_value_spread/ppermute | solution.py:271
  38.0 7.9 %collective-permute-start.2 = (bf16[2,2,256,128]{3,2,1,0:T(8,128)(2,1)S(1)}, bf16[2,2,256,128]{3,2,1,0:T(8,128)(2,1)S(1)}, u32[]{:S(2)}, u32[]{:S(2)}) collective-permute-start(bf16[2,2,256,128]{3,2,1,0:T(8,128)(2,1)S(1)} %key_value_exchange.3.own.refs_0_), channel_id=1, source_target_pairs={{0,2},{1,3},{2,4},{3,5},{4,6},{5,7},{64,66},{65,67},{66,68},{67,69... | collective-permute-start | bytes 786440 | tf_op jit(solution)/shard_map/key_value_spread/ppermute | solution.py:271
  45.9 0.1 pad_add_fusion.place_ref
  45.9 1.3 %collective-permute-start.5 = (bf16[2,2,256,128]{3,2,1,0:T(8,128)(2,1)S(1)}, bf16[2,2,256,128]{3,2,1,0:T(8,128)(2,1)S(1)}, u32[]{:S(2)}, u32[]{:S(2)}) collective-permute-start(bf16[2,2,256,128]{3,2,1,0:T(8,128)(2,1)S(1)} %key_value_exchange.3.own.refs_0_), channel_id=1, source_target_pairs={{0,68},{1,69},{2,70},{3,71},{64,4},{65,5},{66,6},{67,7},{8,76},{9,... | collective-permute-start | bytes 786440 | tf_op jit(solution)/shard_map/key_value_spread/ppermute | solution.py:271
  47.2 0.0 collective-permute-done.1.eight.refs_3_
  47.3 2.9 %collective-permute-start.4 = (bf16[2,2,256,128]{3,2,1,0:T(8,128)(2,1)S(1)}, bf16[2,2,256,128]{3,2,1,0:T(8,128)(2,1)S(1)}, u32[]{:S(2)}, u32[]{:S(2)}) collective-permute-start(bf16[2,2,256,128]{3,2,1,0:T(8,128)(2,1)S(1)} %get-tuple-element.5), channel_id=1, source_target_pairs={{0,256},{128,384},{256,0},{384,128},{1,257},{129,385},{257,1},{385... | collective-permute-start | bytes 786440 | tf_op jit(solution)/shard_map/key_value_spread/ppermute | solution.py:279
  50.2 2.3 %collective-permute-start.3 = (bf16[2,2,256,128]{3,2,1,0:T(8,128)(2,1)S(1)}, bf16[2,2,256,128]{3,2,1,0:T(8,128)(2,1)S(1)}, u32[]{:S(2)}, u32[]{:S(2)}) collective-permute-start(bf16[2,2,256,128]{3,2,1,0:T(8,128)(2,1)S(1)} %get-tuple-element.6), channel_id=1, source_target_pairs={{0,128},{128,256},{256,384},{384,0},{1,129},{129,257},{257,385},{3... | collective-permute-start | bytes 786440 | tf_op jit(solution)/shard_map/key_value_spread/ppermute | solution.py:279
  52.5 0.0 collective-permute-done.2.sixteen.refs_4_
  52.5 0.0 all-to-all-done.q_ref
  52.6 4.8 %attend.2.early_ref = f32[32,2,64,256]{3,2,1,0:T(8,128)S(1)} custom-call(s32[6,64]{1,0:T(8,128)S(1)} %bitcast.12, s32[2]{0:T(128)S(1)} %pad_add_fusion.place_ref, bf16[32,2,64,128]{3,2,1,0:T(8,128)(2,1)S(1)} %all-to-all-done.q_ref, bf16[2,2,256,128]{3,2,1,0:T(8,128)(2,1)S(1)} %key_value_exchange.3.own.refs_0_, ...), custom_call_target="tpu_custom_call" | custom-call | flops 4000000000 | bytes 1048576 | tf_op jit(solution)/shard_map/attend/pallas_call | solution.py:214
  57.4 16.8 %collective-permute-done.5.refs_5_ = bf16[2,2,256,128]{3,2,1,0:T(8,128)(2,1)S(1)} collective-permute-done((bf16[2,2,256,128]{3,2,1,0:T(8,128)(2,1)S(1)}, bf16[2,2,256,128]{3,2,1,0:T(8,128)(2,1)S(1)}, u32[]{:S(2)}, u32[]{:S(2)}) %collective-permute-start.5) | collective-permute-done | bytes 262176 | tf_op jit(solution)/shard_map/key_value_spread/ppermute | solution.py:271
  74.2 30.5 %attend.3 = bf16[32,2,64,128]{3,2,1,0:T(8,128)(2,1)S(1)} custom-call(s32[6,64]{1,0:T(8,128)S(1)} %bitcast.13, s32[2]{0:T(128)S(1)} %pad_add_fusion.place_ref, bf16[32,2,64,128]{3,2,1,0:T(8,128)(2,1)S(1)} %all-to-all-done.q_ref, f32[32,2,64,256]{3,2,1,0:T(8,128)S(1)} %attend.2.early_ref, bf16[2,2,256,128]{3,2,1,0:T(8,128)(2,1)S(1)} %key_value_exchange.3.own.refs_0_, ...), custom_call_target="tpu_custom_call" | custom-call | flops 6000000000 | bytes 1048576 | tf_op jit(solution)/shard_map/attend/pallas_call | solution.py:214
  104.7 20.3 %all_to_all.16 = bf16[32,2,64,128]{3,2,1,0:T(8,128)(2,1)S(1)} all-to-all(bf16[32,2,64,128]{3,2,1,0:T(8,128)(2,1)S(1)} %attend.3), channel_id=1, replica_groups=mesh['x'=4,'zh'=2,'y'=4,'c'=2,'h'=8] {'x','y','c'}, dimensions={0} | all-to-all | bytes 2097152 | tf_op jit(solution)/shard_map/return_exchange/all_to_all | solution.py:308
  125.0 0.2 copy.6
  125.3 1.1 reshape.11
  (6 shorter events, 0.1 us)
Async XLA Ops:
  17.1 15.3 %collective-permute-start = (bf16[2,2,128,128]{3,2,1,0:T(8,128)(2,1)S(1)}, bf16[2,2,128,128]{3,2,1,0:T(8,128)(2,1)S(1)}, u32[]{:S(2)}, u32[]{:S(2)}) collective-permute-start(bf16[2,2,128,128]{3,2,1,0:T(8,128)(2,1)S(1)} %bitcast.10), channel_id=1, source_target_pairs={{0,64},{1,65},{2,66},{3,67},{4,68},{5,69},{6,70},{7,71},{64,0},{65... | collective-permute-start | bytes 393224 | tf_op jit(solution)/shard_map/key_value_exchange/ppermute | solution.py:271
  20.5 1.2 copy-start
  22.8 29.7 %all-to-all-start = ((bf16[32,2,64,128]{3,2,1,0:T(8,128)(2,1)}), bf16[32,2,64,128]{3,2,1,0:T(8,128)(2,1)S(1)}, u32[]{:S(2)}, u32[]{:S(2)}) async-start(bf16[32,2,64,128]{3,2,1,0:T(8,128)(2,1)} %query_exchange.1), calls=%async_computation | async-start | bytes 2097152 | tf_op jit(solution)/shard_map/query_exchange/all_to_all | solution.py:295
  27.1 25.5 %copy-start.1 = (s32[64,6]{0,1:T(8,128)S(1)}, s32[64,6]{0,1:T(8,128)}, u32[]{:S(2)}) copy-start(s32[64,6]{0,1:T(8,128)} %param.7) | copy-start | bytes 4612
  32.4 14.8 %collective-permute-start.1 = (bf16[2,2,256,128]{3,2,1,0:T(8,128)(2,1)S(1)}, bf16[2,2,256,128]{3,2,1,0:T(8,128)(2,1)S(1)}, u32[]{:S(2)}, u32[]{:S(2)}) collective-permute-start(bf16[2,2,256,128]{3,2,1,0:T(8,128)(2,1)S(1)} %key_value_exchange.3.own.refs_0_), channel_id=1, source_target_pairs={{0,1},{1,2},{2,3},{3,4},{4,5},{5,6},{6,7},{64,65},{65,66},{66,67},... | collective-permute-start | bytes 786440 | tf_op jit(solution)/shard_map/key_value_spread/ppermute | solution.py:271
  38.0 14.5 %collective-permute-start.2 = (bf16[2,2,256,128]{3,2,1,0:T(8,128)(2,1)S(1)}, bf16[2,2,256,128]{3,2,1,0:T(8,128)(2,1)S(1)}, u32[]{:S(2)}, u32[]{:S(2)}) collective-permute-start(bf16[2,2,256,128]{3,2,1,0:T(8,128)(2,1)S(1)} %key_value_exchange.3.own.refs_0_), channel_id=1, source_target_pairs={{0,2},{1,3},{2,4},{3,5},{4,6},{5,7},{64,66},{65,67},{66,68},{67,69... | collective-permute-start | bytes 786440 | tf_op jit(solution)/shard_map/key_value_spread/ppermute | solution.py:271
  45.9 28.3 %collective-permute-start.5 = (bf16[2,2,256,128]{3,2,1,0:T(8,128)(2,1)S(1)}, bf16[2,2,256,128]{3,2,1,0:T(8,128)(2,1)S(1)}, u32[]{:S(2)}, u32[]{:S(2)}) collective-permute-start(bf16[2,2,256,128]{3,2,1,0:T(8,128)(2,1)S(1)} %key_value_exchange.3.own.refs_0_), channel_id=1, source_target_pairs={{0,68},{1,69},{2,70},{3,71},{64,4},{65,5},{66,6},{67,7},{8,76},{9,... | collective-permute-start | bytes 786440 | tf_op jit(solution)/shard_map/key_value_spread/ppermute | solution.py:271
  47.3 26.9 %collective-permute-start.4 = (bf16[2,2,256,128]{3,2,1,0:T(8,128)(2,1)S(1)}, bf16[2,2,256,128]{3,2,1,0:T(8,128)(2,1)S(1)}, u32[]{:S(2)}, u32[]{:S(2)}) collective-permute-start(bf16[2,2,256,128]{3,2,1,0:T(8,128)(2,1)S(1)} %get-tuple-element.5), channel_id=1, source_target_pairs={{0,256},{128,384},{256,0},{384,128},{1,257},{129,385},{257,1},{385... | collective-permute-start | bytes 786440 | tf_op jit(solution)/shard_map/key_value_spread/ppermute | solution.py:279
  50.2 24.0 %collective-permute-start.3 = (bf16[2,2,256,128]{3,2,1,0:T(8,128)(2,1)S(1)}, bf16[2,2,256,128]{3,2,1,0:T(8,128)(2,1)S(1)}, u32[]{:S(2)}, u32[]{:S(2)}) collective-permute-start(bf16[2,2,256,128]{3,2,1,0:T(8,128)(2,1)S(1)} %get-tuple-element.6), channel_id=1, source_target_pairs={{0,128},{128,256},{256,384},{384,0},{1,129},{129,257},{257,385},{3... | collective-permute-start | bytes 786440 | tf_op jit(solution)/shard_map/key_value_spread/ppermute | solution.py:279

commit v8 on v6

--- a/solution.py
+++ b/solution.py
@@ -12,6 +12,7 @@
 SLOTS = 6
 FACTOR = HD ** (-0.5) * math.log2(math.e)
 CHUNK = 2048
+EARLY_CHUNK = 1024
 SAFE_CHUNK = 512
 LEAST, MOST = 2.0**-60, 2.0**60
 PLANE = ("x", "y", "c")
@@ -100,7 +101,7 @@
 
 def early_kernel(links_ref, place_ref, q_ref, own, eight, o_ref):
     per = q_ref.shape[2]
-    step_sources = CHUNK // per
+    step_sources = EARLY_CHUNK // per
     for m in range(2):
         parts = [(own, m, None)]
         if m == 1:
@@ -109,8 +110,8 @@
 
         def chunk(step, carry, m=m, parts=parts):
             start = step * step_sources
-            query = q_ref[pl.ds(start, step_sources), m].reshape(CHUNK, HD)
-            allowed = causal(start, CHUNK, per, place_ref[0], own.shape[2])
+            query = q_ref[pl.ds(start, step_sources), m].reshape(EARLY_CHUNK, HD)
+            allowed = causal(start, EARLY_CHUNK, per, place_ref[0], own.shape[2])
             total = weighted(query, None, parts, allowed)
             o_ref[pl.ds(start, step_sources), m] = total.reshape(step_sources, per, 2 * HD)
             return carry

time: 127 us -> 126 us (level)
  waiting for transfers between devices: 18 us -> 16.1 us
    ppermute x2, waiting for transfers between devices: 1.86 us -> 0.52 us  [across(): return lax.ppermute(value, 'x', [(x, (x + by) % 4) for x in range(4)])]
  transfers between devices with their start and end apart: 7 -> 7, of which waited for: 4 -> 3; matrix products, arithmetic and copies ran while one was open for 0% -> 0% of each run, Pallas kernels for 4% -> 5%
where the time goes in v8:
time: 126 us; the launch traced here: 125 us
  blocking collectives  48.6 us (39%)
  Pallas kernels  38.2 us (30%)
  starting transfers between devices  19.1 us (15%)
  waiting for transfers between devices  16.1 us (13%)
  local copies, waits for them, and re-layouts  2.66 us (2%)
    pallas_call x4, Pallas kernels, call(): pl.pallas_call(kernel, out_shape=outputs, in_specs=[smem] * len(scalars)...  36.6 us
    all_to_all x1, blocking collectives, local(): lax.all_to_all(result, PLANE, split_axis=0, concat_axis=0, tiled=True)  33.2 us
    ppermute x4, waiting for transfers between devices, ring(): return lax.ppermute(value, ('zh', 'h'), pairs)  15.6 us
    all_to_all x1, blocking collectives, local(): own = lax.all_to_all(own, PLANE, split_axis=0, concat_axis=0, tiled=True)  15.5 us
    ppermute x4, starting transfers between devices, ring(): return lax.ppermute(value, ('zh', 'h'), pairs)  9.65 us
    ppermute x2, starting transfers between devices, across(): return lax.ppermute(value, 'x', [(x, (x + by) % 4) for x in range(4)])  5.23 us
    all_to_all x1, starting transfers between devices, local(): lax.all_to_all(query, PLANE, split_axis=0, concat_axis=0, tiled=True)  4.26 us
  transfers between devices with their start and end apart: 7, of which 3 were waited for; matrix products, arithmetic and copies ran while one was open for 0% of the time, Pallas kernels for 5%

profile of v8, /device:TPU:449, one launch (start us, length us, event | category | flops | bytes accessed | tf_op | source)
XLA Modules:
  0.0 125.0 jit_solution(1213541756692327399)
XLA Ops:
  0.0 1.6 %key_value_exchange.2 = bf16[32,2,2,4,128]{4,3,2,1,0:T(4,128)(2,1)} custom-call(bf16[8,4,1024]{2,1,0:T(4,128)(2,1)} %keys.1, bf16[8,4,1024]{2,1,0:T(4,128)(2,1)} %values.1), custom_call_target="tpu_custom_call" | custom-call | tf_op jit(solution)/shard_map/key_value_exchange/pallas_call | solution.py:228
  1.6 15.5 %all_to_all.15 = bf16[32,2,2,4,128]{4,3,2,1,0:T(4,128)(2,1)S(1)} all-to-all(bf16[32,2,2,4,128]{4,3,2,1,0:T(4,128)(2,1)} %key_value_exchange.2), channel_id=1, replica_groups=mesh['x'=4,'zh'=2,'y'=4,'c'=2,'h'=8] {'x','y','c'}, dimensions={0} | all-to-all | bytes 262144 | tf_op jit(solution)/shard_map/key_value_exchange/all_to_all | solution.py:290
  17.1 5.2 %collective-permute-start = (bf16[2,2,128,128]{3,2,1,0:T(8,128)(2,1)S(1)}, bf16[2,2,128,128]{3,2,1,0:T(8,128)(2,1)S(1)}, u32[]{:S(2)}, u32[]{:S(2)}) collective-permute-start(bf16[2,2,128,128]{3,2,1,0:T(8,128)(2,1)S(1)} %bitcast.10), channel_id=1, source_target_pairs={{0,64},{1,65},{2,66},{3,67},{4,68},{5,69},{6,70},{7,71},{64,0},{65... | collective-permute-start | bytes 393224 | tf_op jit(solution)/shard_map/key_value_exchange/ppermute | solution.py:271
  22.2 0.0 copy-start
  22.3 1.2 copy-done
  23.5 1.1 query_exchange.1
  24.6 4.3 %all-to-all-start = ((bf16[32,2,64,128]{3,2,1,0:T(8,128)(2,1)}), bf16[32,2,64,128]{3,2,1,0:T(8,128)(2,1)S(1)}, u32[]{:S(2)}, u32[]{:S(2)}) async-start(bf16[32,2,64,128]{3,2,1,0:T(8,128)(2,1)} %query_exchange.1), calls=%async_computation | async-start | bytes 2097152 | tf_op jit(solution)/shard_map/query_exchange/all_to_all | solution.py:295
  28.9 0.0 copy-start.1
  28.9 11.9 %collective-permute-done.other = bf16[2,2,128,128]{3,2,1,0:T(8,128)(2,1)S(1)} collective-permute-done((bf16[2,2,128,128]{3,2,1,0:T(8,128)(2,1)S(1)}, bf16[2,2,128,128]{3,2,1,0:T(8,128)(2,1)S(1)}, u32[]{:S(2)}, u32[]{:S(2)}) %collective-permute-start) | collective-permute-done | bytes 131104 | tf_op jit(solution)/shard_map/key_value_exchange/ppermute | solution.py:271
  40.8 1.9 %collective-permute-start.1 = (bf16[2,2,256,128]{3,2,1,0:T(8,128)(2,1)S(1)}, bf16[2,2,256,128]{3,2,1,0:T(8,128)(2,1)S(1)}, u32[]{:S(2)}, u32[]{:S(2)}) collective-permute-start(bf16[2,2,256,128]{3,2,1,0:T(8,128)(2,1)S(1)} %key_value_exchange.3.own.refs_0_), channel_id=1, source_target_pairs={{0,1},{1,2},{2,3},{3,4},{4,5},{5,6},{6,7},{64,65},{65,66},{66,67},... | collective-permute-start | bytes 786440 | tf_op jit(solution)/shard_map/key_value_spread/ppermute | solution.py:271
  42.8 0.1 pad_add_fusion.place_ref
  42.8 1.3 %collective-permute-start.5 = (bf16[2,2,256,128]{3,2,1,0:T(8,128)(2,1)S(1)}, bf16[2,2,256,128]{3,2,1,0:T(8,128)(2,1)S(1)}, u32[]{:S(2)}, u32[]{:S(2)}) collective-permute-start(bf16[2,2,256,128]{3,2,1,0:T(8,128)(2,1)S(1)} %key_value_exchange.3.own.refs_0_), channel_id=1, source_target_pairs={{0,68},{1,69},{2,70},{3,71},{64,4},{65,5},{66,6},{67,7},{8,76},{9,... | collective-permute-start | bytes 786440 | tf_op jit(solution)/shard_map/key_value_spread/ppermute | solution.py:271
  44.1 1.3 %collective-permute-start.4 = (bf16[2,2,256,128]{3,2,1,0:T(8,128)(2,1)S(1)}, bf16[2,2,256,128]{3,2,1,0:T(8,128)(2,1)S(1)}, u32[]{:S(2)}, u32[]{:S(2)}) collective-permute-start(bf16[2,2,256,128]{3,2,1,0:T(8,128)(2,1)S(1)} %key_value_exchange.3.own.refs_0_), channel_id=1, source_target_pairs={{0,2},{1,3},{2,4},{3,5},{4,6},{5,7},{64,66},{65,67},{66,68},{67,69... | collective-permute-start | bytes 786440 | tf_op jit(solution)/shard_map/key_value_spread/ppermute | solution.py:271
  45.4 3.7 %collective-permute-done.1.eight.refs_3_ = bf16[2,2,256,128]{3,2,1,0:T(8,128)(2,1)S(1)} collective-permute-done((bf16[2,2,256,128]{3,2,1,0:T(8,128)(2,1)S(1)}, bf16[2,2,256,128]{3,2,1,0:T(8,128)(2,1)S(1)}, u32[]{:S(2)}, u32[]{:S(2)}) %collective-permute-start.1) | collective-permute-done | bytes 262176 | tf_op jit(solution)/shard_map/key_value_spread/ppermute | solution.py:271
  49.1 2.9 %collective-permute-start.3 = (bf16[2,2,256,128]{3,2,1,0:T(8,128)(2,1)S(1)}, bf16[2,2,256,128]{3,2,1,0:T(8,128)(2,1)S(1)}, u32[]{:S(2)}, u32[]{:S(2)}) collective-permute-start(bf16[2,2,256,128]{3,2,1,0:T(8,128)(2,1)S(1)} %get-tuple-element.5), channel_id=1, source_target_pairs={{0,256},{128,384},{256,0},{384,128},{1,257},{129,385},{257,1},{385... | collective-permute-start | bytes 786440 | tf_op jit(solution)/shard_map/key_value_spread/ppermute | solution.py:279
  52.0 2.3 %collective-permute-start.2 = (bf16[2,2,256,128]{3,2,1,0:T(8,128)(2,1)S(1)}, bf16[2,2,256,128]{3,2,1,0:T(8,128)(2,1)S(1)}, u32[]{:S(2)}, u32[]{:S(2)}) collective-permute-start(bf16[2,2,256,128]{3,2,1,0:T(8,128)(2,1)S(1)} %get-tuple-element.6), channel_id=1, source_target_pairs={{0,128},{128,256},{256,384},{384,0},{1,129},{129,257},{257,385},{3... | collective-permute-start | bytes 786440 | tf_op jit(solution)/shard_map/key_value_spread/ppermute | solution.py:279
  54.4 5.6 %attend.2.early_ref = f32[32,2,64,256]{3,2,1,0:T(8,128)S(1)} custom-call(s32[6,64]{1,0:T(8,128)S(1)} %bitcast.12, s32[2]{0:T(128)S(1)} %pad_add_fusion.place_ref, bf16[32,2,64,128]{3,2,1,0:T(8,128)(2,1)S(1)} %all-to-all-done.q_ref, bf16[2,2,256,128]{3,2,1,0:T(8,128)(2,1)S(1)} %key_value_exchange.3.own.refs_0_, ...), custom_call_target="tpu_custom_call" | custom-call | flops 4000000000 | bytes 1048576 | tf_op jit(solution)/shard_map/attend/pallas_call | solution.py:214
  60.0 0.0 collective-permute-done.4.refs_4_
  60.0 0.0 collective-permute-done.3.refs_2_
  60.0 0.5 collective-permute-done.2.refs_1_
  60.5 29.9 %attend.3 = bf16[32,2,64,128]{3,2,1,0:T(8,128)(2,1)S(1)} custom-call(s32[6,64]{1,0:T(8,128)S(1)} %bitcast.13, s32[2]{0:T(128)S(1)} %pad_add_fusion.place_ref, bf16[32,2,64,128]{3,2,1,0:T(8,128)(2,1)S(1)} %all-to-all-done.q_ref, f32[32,2,64,256]{3,2,1,0:T(8,128)S(1)} %attend.2.early_ref, bf16[2,2,256,128]{3,2,1,0:T(8,128)(2,1)S(1)} %key_value_exchange.3.own.refs_0_, ...), custom_call_target="tpu_custom_call" | custom-call | flops 6000000000 | bytes 1048576 | tf_op jit(solution)/shard_map/attend/pallas_call | solution.py:214
  90.4 33.2 %all_to_all.16 = bf16[32,2,64,128]{3,2,1,0:T(8,128)(2,1)S(1)} all-to-all(bf16[32,2,64,128]{3,2,1,0:T(8,128)(2,1)S(1)} %attend.3), channel_id=1, replica_groups=mesh['x'=4,'zh'=2,'y'=4,'c'=2,'h'=8] {'x','y','c'}, dimensions={0} | all-to-all | bytes 2097152 | tf_op jit(solution)/shard_map/return_exchange/all_to_all | solution.py:308
  123.6 0.2 copy.6
  123.8 1.1 reshape.11
  (6 shorter events, 0.1 us)
Async XLA Ops:
  17.1 23.7 %collective-permute-start = (bf16[2,2,128,128]{3,2,1,0:T(8,128)(2,1)S(1)}, bf16[2,2,128,128]{3,2,1,0:T(8,128)(2,1)S(1)}, u32[]{:S(2)}, u32[]{:S(2)}) collective-permute-start(bf16[2,2,128,128]{3,2,1,0:T(8,128)(2,1)S(1)} %bitcast.10), channel_id=1, source_target_pairs={{0,64},{1,65},{2,66},{3,67},{4,68},{5,69},{6,70},{7,71},{64,0},{65... | collective-permute-start | bytes 393224 | tf_op jit(solution)/shard_map/key_value_exchange/ppermute | solution.py:271
  22.2 1.2 copy-start
  24.6 29.8 %all-to-all-start = ((bf16[32,2,64,128]{3,2,1,0:T(8,128)(2,1)}), bf16[32,2,64,128]{3,2,1,0:T(8,128)(2,1)S(1)}, u32[]{:S(2)}, u32[]{:S(2)}) async-start(bf16[32,2,64,128]{3,2,1,0:T(8,128)(2,1)} %query_exchange.1), calls=%async_computation | async-start | bytes 2097152 | tf_op jit(solution)/shard_map/query_exchange/all_to_all | solution.py:295
  28.9 25.5 %copy-start.1 = (s32[64,6]{0,1:T(8,128)S(1)}, s32[64,6]{0,1:T(8,128)}, u32[]{:S(2)}) copy-start(s32[64,6]{0,1:T(8,128)} %param.7) | copy-start | bytes 4612
  40.8 8.3 %collective-permute-start.1 = (bf16[2,2,256,128]{3,2,1,0:T(8,128)(2,1)S(1)}, bf16[2,2,256,128]{3,2,1,0:T(8,128)(2,1)S(1)}, u32[]{:S(2)}, u32[]{:S(2)}) collective-permute-start(bf16[2,2,256,128]{3,2,1,0:T(8,128)(2,1)S(1)} %key_value_exchange.3.own.refs_0_), channel_id=1, source_target_pairs={{0,1},{1,2},{2,3},{3,4},{4,5},{5,6},{6,7},{64,65},{65,66},{66,67},... | collective-permute-start | bytes 786440 | tf_op jit(solution)/shard_map/key_value_spread/ppermute | solution.py:271
  42.8 17.2 %collective-permute-start.5 = (bf16[2,2,256,128]{3,2,1,0:T(8,128)(2,1)S(1)}, bf16[2,2,256,128]{3,2,1,0:T(8,128)(2,1)S(1)}, u32[]{:S(2)}, u32[]{:S(2)}) collective-permute-start(bf16[2,2,256,128]{3,2,1,0:T(8,128)(2,1)S(1)} %key_value_exchange.3.own.refs_0_), channel_id=1, source_target_pairs={{0,68},{1,69},{2,70},{3,71},{64,4},{65,5},{66,6},{67,7},{8,76},{9,... | collective-permute-start | bytes 786440 | tf_op jit(solution)/shard_map/key_value_spread/ppermute | solution.py:271
  44.1 15.9 %collective-permute-start.4 = (bf16[2,2,256,128]{3,2,1,0:T(8,128)(2,1)S(1)}, bf16[2,2,256,128]{3,2,1,0:T(8,128)(2,1)S(1)}, u32[]{:S(2)}, u32[]{:S(2)}) collective-permute-start(bf16[2,2,256,128]{3,2,1,0:T(8,128)(2,1)S(1)} %key_value_exchange.3.own.refs_0_), channel_id=1, source_target_pairs={{0,2},{1,3},{2,4},{3,5},{4,6},{5,7},{64,66},{65,67},{66,68},{67,69... | collective-permute-start | bytes 786440 | tf_op jit(solution)/shard_map/key_value_spread/ppermute | solution.py:271
  49.1 10.9 %collective-permute-start.3 = (bf16[2,2,256,128]{3,2,1,0:T(8,128)(2,1)S(1)}, bf16[2,2,256,128]{3,2,1,0:T(8,128)(2,1)S(1)}, u32[]{:S(2)}, u32[]{:S(2)}) collective-permute-start(bf16[2,2,256,128]{3,2,1,0:T(8,128)(2,1)S(1)} %get-tuple-element.5), channel_id=1, source_target_pairs={{0,256},{128,384},{256,0},{384,128},{1,257},{129,385},{257,1},{385... | collective-permute-start | bytes 786440 | tf_op jit(solution)/shard_map/key_value_spread/ppermute | solution.py:279
  52.0 8.5 %collective-permute-start.2 = (bf16[2,2,256,128]{3,2,1,0:T(8,128)(2,1)S(1)}, bf16[2,2,256,128]{3,2,1,0:T(8,128)(2,1)S(1)}, u32[]{:S(2)}, u32[]{:S(2)}) collective-permute-start(bf16[2,2,256,128]{3,2,1,0:T(8,128)(2,1)S(1)} %get-tuple-element.6), channel_id=1, source_target_pairs={{0,128},{128,256},{256,384},{384,0},{1,129},{129,257},{257,385},{3... | collective-permute-start | bytes 786440 | tf_op jit(solution)/shard_map/key_value_spread/ppermute | solution.py:279
